TPU v7x, 32 devices: a whole 2x2x4 slice. The times are simulated.
32 devices in a mesh: groups: 2 (over x), seq: 16 (over z, y, core).
Axes of the slice: x: 2, y: 2, z: 4, core: 2. Of those that a mesh axis runs over, the one named last changes fastest.
Arguments:
- x_stream: bfloat16 [4096, 8192], P(('groups', 'seq')), parts along dimension 0, may hold values from -6 to 6
- bc_stream: bfloat16 [4096, 2048], P(('groups', 'seq')), parts along dimension 0, may hold values from -6 to 6
- z_stream: bfloat16 [4096, 8192], P(('groups', 'seq')), parts along dimension 0, may hold values from -6 to 6
- dt_raw: bfloat16 [4096, 128], P(('groups', 'seq')), parts along dimension 0, may hold values from -3 to 5
- doc_ids: int32 [4096], P('groups'), parts along dimension 0, may hold values from 0 to 15, never falling along the last dimension, each value on 1 to 512 neighbouring positions
- conv_weight: float32 [4, 10240], replicated, may hold values from -3 to 3
- conv_bias: float32 [10240], replicated, may hold values from -1.8 to 1.8
- dt_bias: float32 [128], replicated, may hold values from -1 to 0.5
- a_log: float32 [128], replicated, may hold values from -8 to -2.5
- skip_d: float32 [128], replicated, may hold values from 0.5 to 1.5
- norm_gain: float32 [8192], replicated, may hold values from 0.5 to 1.5
Outputs:
- mixed: bfloat16 [4096, 8192], P(('groups', 'seq')), parts along dimension 0
- doc_cosine: float32 [32], P('groups'), parts along dimension 0
There are 2 independent parts, one for each index of `groups`. A program takes and returns all parts, laid end to end along the dimension named above; an argument that names none is the same for every part. Nothing has to cross between parts.
Inputs may be any that keep to these rules, and one draw needn't show every extreme that they name: `doc_ids`: document ids never fall along the stream; every id is used, each document has at most 512 tokens and one has exactly that many.
All inputs are finite; a program needn't handle non-finite values.
Results may differ from a plain program's by a relative error of at most 0.0054.
Values may be sent and summed in bfloat16 or wider, within the bound.
No kernel may reach another device: no remote copies, remote signals or barrier semaphores. Data moves between devices by JAX's collectives and lax.ppermute only.
A program may use at most 128 MiB of HBM per device.

v0:
```python
import jax
import jax.numpy as jnp
from jax import lax
from jax.sharding import PartitionSpec as P

STATE = 256
SPAN = 512
DOCS = 16


def shifted_2(array, axis, by):
    devices = lax.axis_size(axis)
    pairs = [(i, i + by) for i in range(devices) if 0 <= i + by < devices]
    return lax.ppermute(array, axis, pairs)


def causal_conv(extended, ext_docs, weight, bias, row_count):
    kernel_taps = weight.shape[0]
    own_docs = ext_docs[kernel_taps - 1 :]
    summed = jnp.zeros((row_count, extended.shape[1]), jnp.float32)
    for offset in range(kernel_taps):
        shifted = lax.slice_in_dim(extended, offset, offset + row_count, axis=0).astype(jnp.float32)
        same_doc = (
            lax.slice_in_dim(ext_docs, offset, offset + row_count, axis=0) == own_docs
        ).astype(jnp.float32)
        summed = summed + weight[offset][None, :] * shifted * same_doc[:, None]
    return jax.nn.silu(summed + bias[None, :]).astype(jnp.bfloat16)


def gated_norm(y_rows, z_rows, gain, group_count):
    row_count = y_rows.shape[0]
    gated = y_rows.astype(jnp.float32) * jax.nn.silu(z_rows.astype(jnp.float32))
    gated = gated.reshape(row_count, group_count, -1)
    scale = lax.rsqrt(jnp.mean(gated * gated, axis=-1, keepdims=True) + 1e-05)
    return (
        (gated * scale * gain.reshape(group_count, -1)[None])
        .reshape(row_count, -1)
        .astype(jnp.bfloat16)
    )


def scan_spans(x_heads, b_group, c_group, dt_heads, cum_log, seg_ids, skip_mine):

    def span_step(carry, block_data):
        carry_state, prev_doc = carry
        x_span, b_span, c_span, dt_span, cum_span, seg_span = block_data
        span_len = x_span.shape[0]
        row_index = lax.broadcasted_iota(jnp.int32, (span_len, span_len), 0)
        col_index = lax.broadcasted_iota(jnp.int32, (span_len, span_len), 1)
        same_mask = (seg_span[:, None] == seg_span[None, :]) & (row_index >= col_index)
        scores = jnp.einsum("is,js->ij", c_span, b_span, preferred_element_type=jnp.float32)
        cum_heads = jnp.transpose(cum_span)
        gaps_log = cum_heads[:, :, None] - cum_heads[:, None, :]
        decays = jnp.where(same_mask[None], jnp.exp(jnp.where(same_mask[None], gaps_log, 0.0)), 0.0)
        weights = (decays * scores[None] * jnp.transpose(dt_span)[:, None, :]).astype(jnp.bfloat16)
        intra_sum = jnp.einsum("hij,jhp->ihp", weights, x_span, preferred_element_type=jnp.float32)
        keep_mask = (seg_span == prev_doc).astype(jnp.float32)
        carried = jnp.einsum(
            "is,hps->ihp", c_span.astype(jnp.float32), carry_state, precision=lax.Precision.HIGHEST
        )
        carried = carried * (jnp.exp(cum_span) * keep_mask[:, None])[:, :, None]
        span_out = (
            intra_sum + carried + skip_mine[None, :, None] * x_span.astype(jnp.float32)
        ).astype(jnp.bfloat16)
        last_doc = seg_span[span_len - 1]
        tail_weight = (
            jnp.exp(cum_span[span_len - 1][None, :] - cum_span)
            * dt_span
            * (seg_span == last_doc).astype(jnp.float32)[:, None]
        )
        fresh_state = jnp.einsum(
            "jhp,js->hps",
            x_span.astype(jnp.float32) * tail_weight[:, :, None],
            b_span.astype(jnp.float32),
            precision=lax.Precision.HIGHEST,
        )
        kept = jnp.exp(cum_span[span_len - 1]) * (last_doc == prev_doc).astype(jnp.float32)
        carry_state = carry_state * kept[:, None, None] + fresh_state
        return ((carry_state, last_doc), span_out)

    head_count = x_heads.shape[2]
    initial = (
        jnp.zeros((head_count, x_heads.shape[3], b_group.shape[2]), jnp.float32),
        jnp.array(-1, jnp.int32),
    )
    final_carry, outputs = lax.scan(
        span_step, initial, (x_heads, b_group, c_group, dt_heads, cum_log, seg_ids)
    )
    return outputs


def on_device(
    x_stream,
    bc_stream,
    z_stream,
    dt_raw,
    doc_ids,
    conv_weight,
    conv_bias,
    dt_bias,
    a_log,
    skip_d,
    norm_gain,
):
    tok_rows, inner_width = x_stream.shape
    head_count = dt_raw.shape[1]
    head_dim = inner_width // head_count
    members = lax.axis_size("seq")
    where_me = lax.axis_index("seq")
    per_device = head_count // members
    own_width = per_device * head_dim
    group_count = bc_stream.shape[1] // (2 * STATE)
    group_owners = members // group_count
    all_rows = tok_rows * members
    kernel_taps = conv_weight.shape[0]
    pad_docs = jnp.concatenate([jnp.full((kernel_taps - 1,), -1, jnp.int32), doc_ids])
    edge_rows = jnp.concatenate(
        [x_stream[tok_rows - kernel_taps + 1 :], bc_stream[tok_rows - kernel_taps + 1 :]], axis=1
    )
    rim_rows = shifted_2(edge_rows, "seq", 1)
    ext_docs = lax.dynamic_slice_in_dim(pad_docs, where_me * tok_rows, tok_rows + kernel_taps - 1)
    x_values = causal_conv(
        jnp.concatenate([rim_rows[:, :inner_width], x_stream]),
        ext_docs,
        conv_weight[:, :inner_width],
        conv_bias[:inner_width],
        tok_rows,
    )
    bc_values = causal_conv(
        jnp.concatenate([rim_rows[:, inner_width:], bc_stream]),
        ext_docs,
        conv_weight[:, inner_width:],
        conv_bias[inner_width:],
        tok_rows,
    )
    x_send = x_values.reshape(tok_rows, 1, members, own_width)
    dt_send = dt_raw.reshape(tok_rows, 1, members, per_device)
    bc_send = jnp.repeat(bc_values.reshape(tok_rows, 2, group_count, STATE), group_owners, axis=2)
    got_x, got_bc, got_dt = (
        lax.all_to_all(x_send, "seq", split_axis=2, concat_axis=0, tiled=True),
        lax.all_to_all(bc_send, "seq", split_axis=2, concat_axis=0, tiled=True),
        lax.all_to_all(dt_send, "seq", split_axis=2, concat_axis=0, tiled=True),
    )
    bc_full = got_bc.reshape(all_rows, 2 * STATE)
    x_full = got_x.reshape(all_rows, own_width)
    dt_full = got_dt.reshape(all_rows, per_device)
    bias_mine = lax.dynamic_slice_in_dim(dt_bias, where_me * per_device, per_device)
    decay_mine = -jnp.exp(lax.dynamic_slice_in_dim(a_log, where_me * per_device, per_device))
    skip_mine = lax.dynamic_slice_in_dim(skip_d, where_me * per_device, per_device)
    step_size = jax.nn.softplus(dt_full.astype(jnp.float32) + bias_mine[None, :])
    span_count = all_rows // SPAN
    cum_log = jnp.cumsum(
        (decay_mine[None, :] * step_size).reshape(span_count, SPAN, per_device), axis=1
    )
    outputs = scan_spans(
        x_full.reshape(span_count, SPAN, per_device, head_dim),
        bc_full[:, :STATE].reshape(span_count, SPAN, STATE),
        bc_full[:, STATE:].reshape(span_count, SPAN, STATE),
        step_size.reshape(span_count, SPAN, per_device),
        cum_log,
        doc_ids.reshape(span_count, SPAN),
        skip_mine,
    )
    y_heads = outputs.reshape(all_rows, own_width)
    y_float = y_heads.astype(jnp.float32)
    x_float = x_full.astype(jnp.float32)
    row_sums = jnp.stack(
        [
            jnp.sum(y_float * x_float, axis=1),
            jnp.sum(y_float * y_float, axis=1),
            jnp.sum(x_float * x_float, axis=1),
        ],
        axis=1,
    )
    doc_table = (doc_ids[None, :] == jnp.arange(DOCS, dtype=jnp.int32)[:, None]).astype(jnp.float32)
    partial_sums = jnp.dot(doc_table, row_sums, precision=lax.Precision.HIGHEST)
    returned = lax.all_to_all(
        y_heads.reshape(members, tok_rows, own_width),
        "seq",
        split_axis=0,
        concat_axis=2,
        tiled=True,
    )
    doc_totals = lax.psum(partial_sums, "seq")
    y_rows = returned.reshape(tok_rows, inner_width)
    mixed = gated_norm(y_rows, z_stream, norm_gain, group_count)
    doc_cosine = doc_totals[:, 0] / jnp.sqrt(doc_totals[:, 1] * doc_totals[:, 2] + 1e-06)
    return (mixed, doc_cosine)


def solution(mesh):
    return jax.shard_map(
        on_device,
        mesh=mesh,
        in_specs=(
            P(("groups", "seq"), None),
            P(("groups", "seq"), None),
            P(("groups", "seq"), None),
            P(("groups", "seq"), None),
            P("groups"),
            P(),
            P(),
            P(),
            P(),
            P(),
            P(),
        ),
        out_specs=(P(("groups", "seq"), None), P("groups")),
        check_vma=False,
    )
```

profile of v0, /device:TPU:0, one launch (start us, length us, event | category | flops | bytes accessed | tf_op | source)
XLA Modules:
  0.0 284.8 jit_solution(15083256508914044041)
XLA Ops:
  0.6 0.9 slice.121
  2.4 2.4 collective-permute-start
  4.8 1.5 copy.34
  6.3 7.2 %all-to-all-start = ((bf16[128,1,16,8]{0,3,1,2:T(8,128)(2,1)}), bf16[128,1,16,8]{0,3,1,2:T(8,128)(2,1)S(1)}, u32[]{:S(2)}, u32[]{:S(2)}) async-start(bf16[128,1,16,8]{0,3,1,2:T(8,128)(2,1)} %bitcast.1), calls=%async_computation | async-start | bytes 65536 | tf_op jit(solution)/shard_map/all_to_all | solution.py:142
  13.5 1.4 fusion.59
  15.7 3.2 %copy.38 = bf16[128,8192]{0,1:T(8,128)(2,1)S(1)} copy(bf16[128,8192]{1,0:T(8,128)(2,1)} %param.13) | data formatting | bytes 4194304 | tf_op args[0]
  19.0 1.8 copy.37
  20.8 12.6 %multiply_convert_fusion.4 = bf16[128,8192]{0,1:T(8,128)(2,1)} fusion(bf16[128,8192]{0,1:T(8,128)(2,1)S(1)} %copy.38, bf16[3,8192]{0,1:T(8,128)(2,1)} %copy.37, f32[8192]{0:T(1024)S(1)} %slice-done, f32[8192]{0:T(1024)S(1)} %bitcast.161, f32[128]{0:T(128)S(1)} %get-tuple-element.177, f32[8192]{0:T(1024)S(1)} %bitcast.162, f32[128]{0:T(128)S(1)} %get-tuple-element.176, ...), kind=kLoop, calls=%fused_computation.70 | loop fusion | flops 30408704 | bytes 4408832 | tf_op jit(solution)/shard_map/convert_element_type | solution.py:27
  33.4 6.0 %all-to-all-start.1 = ((bf16[128,1,16,512]{0,3,1,2:T(8,128)(2,1)}), bf16[128,1,16,512]{0,3,1,2:T(8,128)(2,1)S(1)}, u32[]{:S(2)}, u32[]{:S(2)}) async-start(bf16[128,1,16,512]{0,3,1,2:T(8,128)(2,1)} %bitcast.155), calls=%async_computation.1 | async-start | bytes 4194304 | tf_op jit(solution)/shard_map/all_to_all | solution.py:140
  39.4 0.9 fusion.58
  42.1 38.4 %all-to-all-done.1 = bf16[128,1,16,512]{0,3,1,2:T(8,128)(2,1)S(1)} async-done(((bf16[128,1,16,512]{0,3,1,2:T(8,128)(2,1)}), bf16[128,1,16,512]{0,3,1,2:T(8,128)(2,1)S(1)}, u32[]{:S(2)}, u32[]{:S(2)}) %all-to-all-start.1) | async-done | bytes 2097184 | tf_op jit(solution)/shard_map/all_to_all | solution.py:140
  80.5 3.0 %broadcast_in_dim.23 = bf16[128,2,4,4,256]{4,1,0,3,2:T(2,128)(2,1)} broadcast(bf16[128,2,4,256]{3,1,0,2:T(2,128)(2,1)S(1)} %copy.42), dimensions={0,1,2,4} | broadcast | bytes 2621440 | tf_op jit(solution)/shard_map/broadcast_in_dim | solution.py:138
  83.5 11.3 %all-to-all-start.2 = ((bf16[128,2,16,256]{3,1,0,2:T(2,128)(2,1)}), bf16[128,2,16,256]{3,1,0,2:T(2,128)(2,1)}, u32[]{:S(2)}, u32[]{:S(2)}) async-start(bf16[128,2,16,256]{3,1,0,2:T(2,128)(2,1)} %bitcast.154), calls=%async_computation.2 | async-start | bytes 4194304 | tf_op jit(solution)/shard_map/all_to_all | solution.py:141
  95.2 4.5 %reduce-window.6 = f32[4,8,4,128]{3,1,2,0:T(8,128)S(1)} reduce-window(f32[4,8,4,128]{3,1,2,0:T(8,128)S(1)} %get-tuple-element.157, f32[]{:T(128)} %constant.28.clone.1), window={size=1x1x1x128 pad=0_0x0_0x0_0x127_0}, to_apply=%region_0.1 | reduce-window | flops 2080768 | bytes 131076 | tf_op jit(solution)/shard_map/reduce-window
  100.0 2.7 copy.41
  102.7 4.1 %reshape_reshape.6 = bf16[4,512,8,64]{1,0,3,2:T(4,128)(2,1)} reshape(bf16[16,128,1,1,512]{1,0,4,3,2:T(8,128)(2,1)} %copy.41) | data formatting | bytes 4194304 | tf_op jit(solution)/shard_map/reshape;reshape | solution.py:156
  106.8 3.4 %copy.43 = bf16[4,512,8,64]{1,3,2,0:T(8,128)(2,1)} copy(bf16[4,512,8,64]{1,0,3,2:T(4,128)(2,1)} %reshape_reshape.6) | data formatting | bytes 4194304
  110.2 25.7 %all-to-all-done.2 = bf16[128,2,16,256]{3,1,0,2:T(2,128)(2,1)} async-done(((bf16[128,2,16,256]{3,1,0,2:T(2,128)(2,1)}), bf16[128,2,16,256]{3,1,0,2:T(2,128)(2,1)}, u32[]{:S(2)}, u32[]{:S(2)}) %all-to-all-start.2) | async-done | bytes 2097184 | tf_op jit(solution)/shard_map/all_to_all | solution.py:141
  135.9 2.0 copy.49
  138.0 1.1 fusion.57
  139.1 51.9 %while.15 = (s32[]{:T(128)}, f32[8,64,256]{2,1,0:T(8,128)S(1)}, s32[]{:T(128)}, bf16[4,512,8,64]{1,3,2,0:T(8,128)(2,1)}, f32[4,512,8]{1,2,0:T(8,128)S(1)}, /*ind...) while((s32[]{:T(128)}, f32[8,64,256]{2,1,0:T(8,128)S(1)}, ...), condition=%wide.region_3.4_spmd.clone, body=%wide.region_2.3_spmd.clone.sunk | while | flops 2029275136 | bytes 9671070 | solution.py:86
  139.1 1.3 fusion.80
  140.6 4.3 %fusion.82 = f32[512,8,64]{0,2,1:T(8,128)S(1)} fusion(f32[8,512]{1,0:T(8,128)S(1)} %get-tuple-element.254, f32[512,512]{1,0:T(8,128)S(1)} %fusion.80, f32[8,512]{1,0:T(8,128)S(1)} %get-tuple-element.255, pred[512,512]{1,0:T(8,128)(4,1)S(1)} %fusion.81, bf16[4,512,8,64]{1,3,2,0:T(8,128)(2,1)} %get-tuple-element.291, s32[]{:T(128)} %get-tuple-element.271), kind=kOutput, calls=%fused_computation.3.clone.1 | convolution fusion | flops 281018368 | bytes 2933248 | tf_op jit(solution)/shard_map/while/body/eval_jaxpr/hij,jhp->ihp/dot_general | solution.py:56
  146.3 2.5 fusion.83
  149.4 2.0 convolution_add_fusion.2
  152.1 1.3 fusion.80
  153.6 4.3 %fusion.82 = f32[512,8,64]{0,2,1:T(8,128)S(1)} fusion(f32[8,512]{1,0:T(8,128)S(1)} %get-tuple-element.254, f32[512,512]{1,0:T(8,128)S(1)} %fusion.80, f32[8,512]{1,0:T(8,128)S(1)} %get-tuple-element.255, pred[512,512]{1,0:T(8,128)(4,1)S(1)} %fusion.81, bf16[4,512,8,64]{1,3,2,0:T(8,128)(2,1)} %get-tuple-element.291, s32[]{:T(128)} %get-tuple-element.271), kind=kOutput, calls=%fused_computation.3.clone.1 | convolution fusion | flops 281018368 | bytes 2933248 | tf_op jit(solution)/shard_map/while/body/eval_jaxpr/hij,jhp->ihp/dot_general | solution.py:56
  159.3 2.5 fusion.83
  162.4 2.0 convolution_add_fusion.2
  165.1 1.3 fusion.80
  166.6 4.3 %fusion.82 = f32[512,8,64]{0,2,1:T(8,128)S(1)} fusion(f32[8,512]{1,0:T(8,128)S(1)} %get-tuple-element.254, f32[512,512]{1,0:T(8,128)S(1)} %fusion.80, f32[8,512]{1,0:T(8,128)S(1)} %get-tuple-element.255, pred[512,512]{1,0:T(8,128)(4,1)S(1)} %fusion.81, bf16[4,512,8,64]{1,3,2,0:T(8,128)(2,1)} %get-tuple-element.291, s32[]{:T(128)} %get-tuple-element.271), kind=kOutput, calls=%fused_computation.3.clone.1 | convolution fusion | flops 281018368 | bytes 2933248 | tf_op jit(solution)/shard_map/while/body/eval_jaxpr/hij,jhp->ihp/dot_general | solution.py:56
  172.3 2.5 fusion.83
  175.4 2.0 convolution_add_fusion.2
  178.0 1.3 fusion.80
  179.5 4.3 %fusion.82 = f32[512,8,64]{0,2,1:T(8,128)S(1)} fusion(f32[8,512]{1,0:T(8,128)S(1)} %get-tuple-element.254, f32[512,512]{1,0:T(8,128)S(1)} %fusion.80, f32[8,512]{1,0:T(8,128)S(1)} %get-tuple-element.255, pred[512,512]{1,0:T(8,128)(4,1)S(1)} %fusion.81, bf16[4,512,8,64]{1,3,2,0:T(8,128)(2,1)} %get-tuple-element.291, s32[]{:T(128)} %get-tuple-element.271), kind=kOutput, calls=%fused_computation.3.clone.1 | convolution fusion | flops 281018368 | bytes 2933248 | tf_op jit(solution)/shard_map/while/body/eval_jaxpr/hij,jhp->ihp/dot_general | solution.py:56
  185.3 2.5 fusion.83
  188.4 2.0 convolution_add_fusion.2
  191.0 4.5 %copy.44 = bf16[4,512,8,64]{1,0,3,2:T(4,128)(2,1)} copy(bf16[4,512,8,64]{1,3,2,0:T(8,128)(2,1)} %get-tuple-element.59) | data formatting | bytes 4194304 | tf_op jit(solution)/shard_map/while | solution.py:86
  195.5 2.7 reshape_reshape.7
  198.3 1.9 copy.45
  200.2 11.3 %all-to-all-start.3 = ((bf16[16,128,512]{1,2,0:T(8,128)(2,1)}), bf16[16,128,512]{1,2,0:T(8,128)(2,1)}, u32[]{:S(2)}, u32[]{:S(2)}) async-start(bf16[16,128,512]{1,2,0:T(8,128)(2,1)} %copy.45), calls=%async_computation.3 | async-start | bytes 4194304 | tf_op jit(solution)/shard_map/all_to_all | solution.py:177
  211.4 3.2 %copy.46 = bf16[128,8192]{0,1:T(8,128)(2,1)S(1)} copy(bf16[128,8192]{1,0:T(8,128)(2,1)} %param.15) | data formatting | bytes 4194304 | tf_op args[2]
  214.7 4.3 %fusion.41 = (f32[4,512]{1,0:T(4,128)S(1)}, f32[4,512]{1,0:T(4,128)S(1)}) fusion(bf16[4,512,8,64]{1,0,3,2:T(4,128)(2,1)} %reshape_reshape.6, bf16[4,512,8,64]{1,3,2,0:T(8,128)(2,1)} %get-tuple-element.59), kind=kLoop, calls=%fused_computation.63 | loop fusion | flops 6287360 | bytes 4210688 | tf_op jit(solution)/shard_map/reduce_sum | solution.py:169
  219.6 54.2 %psum.7 = f32[16,3]{0,1:T(4,128)S(1)} all-reduce(f32[16,3]{0,1:T(4,128)S(1)} %fusion.49), channel_id=1, replica_groups=mesh['groups'=2,'seq'=16] {'seq'}, use_global_device_ids=true, to_apply=%region_8.9 | all-reduce | flops 48 | bytes 384 | tf_op jit(solution)/shard_map/psum | solution.py:184
  274.4 2.0 bitcast_convert_fusion
  276.4 1.4 bitcast_reduce_fusion
  277.8 3.0 %fusion.44 = bf16[128,8192]{0,1:T(8,128)(2,1)} fusion(f32[8192]{0:T(1024)S(1)} %copy-done.3, f32[128,4]{0,1:T(4,128)S(1)} %add_rsqrt_fusion, bf16[128,8192]{0,1:T(8,128)(2,1)S(1)} %copy.46, f32[16,1,128,512]{2,3,0,1:T(8,128)S(1)} %bitcast_convert_fusion), kind=kLoop, calls=%fused_computation.67 | loop fusion | flops 9437184 | bytes 8423424 | tf_op jit(solution)/shard_map/convert_element_type | solution.py:38
  280.8 4.1 %copy.48 = bf16[128,8192]{1,0:T(8,128)(2,1)} copy(bf16[128,8192]{0,1:T(8,128)(2,1)} %fusion.44) | data formatting | bytes 4194304
  (82 shorter events, 11.8 us)
Async XLA Ops:
  0.6 20.2 %slice-start = ((f32[10240]{0:T(1024)}), f32[8192]{0:T(1024)S(1)}, s32[]{:S(2)}) async-start(f32[10240]{0:T(1024)} %param.19), calls=%async_computation.4 | async-start | bytes 65536 | tf_op jit(solution)/shard_map/slice | solution.py:126
  2.4 16.5 %collective-permute-start = (bf16[3,10240]{1,0:T(4,128)(2,1)S(1)}, bf16[3,10240]{1,0:T(4,128)(2,1)S(1)}, u32[]{:S(2)}, u32[]{:S(2)}) collective-permute-start(bf16[3,10240]{1,0:T(4,128)(2,1)S(1)} %pad_maximum_fusion.2), channel_id=1, source_target_pairs={{0,1},{1,2},{2,3},{3,4},{4,5},{5,6},{6,7},{7,8},{8,9},{9,10},{10,1... | collective-permute-start | bytes 184328 | tf_op jit(solution)/shard_map/ppermute | solution.py:14
  6.3 27.1 %all-to-all-start = ((bf16[128,1,16,8]{0,3,1,2:T(8,128)(2,1)}), bf16[128,1,16,8]{0,3,1,2:T(8,128)(2,1)S(1)}, u32[]{:S(2)}, u32[]{:S(2)}) async-start(bf16[128,1,16,8]{0,3,1,2:T(8,128)(2,1)} %bitcast.1), calls=%async_computation | async-start | bytes 65536 | tf_op jit(solution)/shard_map/all_to_all | solution.py:142
  20.8 19.6 %copy-start.2 = (bf16[128,2048]{1,0:T(8,128)(2,1)S(1)}, bf16[128,2048]{1,0:T(8,128)(2,1)}, u32[]{:S(2)}) copy-start(bf16[128,2048]{1,0:T(8,128)(2,1)} %param.14) | copy-start | bytes 1572868
  20.8 19.6 %slice-start.1 = ((f32[10240]{0:T(1024)}), f32[2048]{0:T(1024)S(1)}, s32[]{:S(2)}) async-start(f32[10240]{0:T(1024)} %param.19), calls=%async_computation.5 | async-start | bytes 16384 | tf_op jit(solution)/shard_map/slice | solution.py:133
  33.4 47.1 %all-to-all-start.1 = ((bf16[128,1,16,512]{0,3,1,2:T(8,128)(2,1)}), bf16[128,1,16,512]{0,3,1,2:T(8,128)(2,1)S(1)}, u32[]{:S(2)}, u32[]{:S(2)}) async-start(bf16[128,1,16,512]{0,3,1,2:T(8,128)(2,1)} %bitcast.155), calls=%async_computation.1 | async-start | bytes 4194304 | tf_op jit(solution)/shard_map/all_to_all | solution.py:140
  41.7 53.2 %copy-start.4 = (s32[2048]{0:T(1024)S(1)}, s32[2048]{0:T(1024)}, u32[]{:S(2)}) copy-start(s32[2048]{0:T(1024)} %param.17) | copy-start | bytes 24580
  41.7 53.2 %copy-start.5 = (f32[128]{0:T(128)S(1)}, f32[128]{0:T(128)}, u32[]{:S(2)}) copy-start(f32[128]{0:T(128)} %param.20) | copy-start | bytes 1540
  41.7 53.2 %copy-start.6 = (f32[128]{0:T(128)S(1)}, f32[128]{0:T(128)}, u32[]{:S(2)}) copy-start(f32[128]{0:T(128)} %param.22) | copy-start | bytes 1540
  41.7 53.3 %copy-start.7 = (f32[128]{0:T(128)S(1)}, f32[128]{0:T(128)}, u32[]{:S(2)}) copy-start(f32[128]{0:T(128)} %param.21) | copy-start | bytes 1540
  80.5 22.2 %copy-start = (bf16[128,1,16,512]{0,3,1,2:T(8,128)(2,1)}, bf16[128,1,16,512]{0,3,1,2:T(8,128)(2,1)S(1)}, u32[]{:S(2)}) copy-start(bf16[128,1,16,512]{0,3,1,2:T(8,128)(2,1)S(1)} %all-to-all-done.1) | copy-start | bytes 6291460
  83.5 52.4 %all-to-all-start.2 = ((bf16[128,2,16,256]{3,1,0,2:T(2,128)(2,1)}), bf16[128,2,16,256]{3,1,0,2:T(2,128)(2,1)}, u32[]{:S(2)}, u32[]{:S(2)}) async-start(bf16[128,2,16,256]{3,1,0,2:T(2,128)(2,1)} %bitcast.154), calls=%async_computation.2 | async-start | bytes 4194304 | tf_op jit(solution)/shard_map/all_to_all | solution.py:141
  200.2 74.2 %all-to-all-start.3 = ((bf16[16,128,512]{1,2,0:T(8,128)(2,1)}), bf16[16,128,512]{1,2,0:T(8,128)(2,1)}, u32[]{:S(2)}, u32[]{:S(2)}) async-start(bf16[16,128,512]{1,2,0:T(8,128)(2,1)} %copy.45), calls=%async_computation.3 | async-start | bytes 4194304 | tf_op jit(solution)/shard_map/all_to_all | solution.py:177
  214.7 4.3 %copy-start.1 = (bf16[128,1,16,512]{0,3,1,2:T(8,128)(2,1)S(1)}, bf16[128,1,16,512]{0,3,1,2:T(8,128)(2,1)}, u32[]{:S(2)}) copy-start(bf16[128,1,16,512]{0,3,1,2:T(8,128)(2,1)} %copy-done) | copy-start | bytes 6291460
  276.4 1.4 copy-start.3
where the time goes:
time: 289 us; the launch traced here: 285 us
  waiting for transfers between devices  64.1 us (22%)
  blocking collectives  54.2 us (19%)
  local copies, waits for them, and re-layouts  48.5 us (17%)
  matrix products  40.7 us (14%)
  starting transfers between devices  38.1 us (13%)
  other arithmetic  33.4 us (12%)
  loops' own time  4.77 us (2%)
    psum x1, blocking collectives, on_device(): doc_totals = lax.psum(partial_sums, 'seq')  54.2 us
    all_to_all x1, waiting for transfers between devices, on_device(): lax.all_to_all(x_send, 'seq', split_axis=2, concat_axis=0, tiled=True)  38.4 us
    all_to_all x1, waiting for transfers between devices, on_device(): lax.all_to_all(bc_send, 'seq', split_axis=2, concat_axis=0, tiled=True)  25.7 us
    unnamed x24, local copies, waits for them, and re-layouts  17.5 us
    dot_general x4, matrix products, span_step(): jnp.einsum('hij,jhp->ihp', weights, x_span, preferred_element_type=jnp.fl...  17.2 us
    convert_element_type x2, other arithmetic, causal_conv(): return jax.nn.silu(summed + bias[None, :]).astype(jnp.bfloat16)  13.4 us
    all_to_all x1, starting transfers between devices, on_device(): lax.all_to_all(bc_send, 'seq', split_axis=2, concat_axis=0, tiled=True)  11.3 us
    all_to_all x1, starting transfers between devices, on_device(): lax.all_to_all(y_heads.reshape(members, tok_rows, own_width), 'seq', spli...  11.3 us
  transfers between devices with their start and end apart: 5, of which 2 were waited for; matrix products, arithmetic and copies ran while one was open for 17% of the time, Pallas kernels for 0%

commit v1 on v0

v1 whole, which is shorter than its diff:
```python
import functools

import jax
import jax.numpy as jnp
from jax import lax
from jax.experimental import pallas as pl
from jax.experimental.pallas import tpu as pltpu
from jax.sharding import PartitionSpec as P

STATE = 256
SPAN = 512
DOCS = 16
CHUNKS = 4
HALO = 16
LANES = 128
VMEM_LIMIT = 20 * 1024 * 1024

F32 = jnp.float32
BF16 = jnp.bfloat16
ANY = pl.BlockSpec(memory_space=pl.ANY)


def iota(shape, dim):
    return lax.broadcasted_iota(jnp.int32, shape, dim)


def whole(shape):
    return pl.BlockSpec(shape, lambda i, pref: (0,) * len(shape))


def call(kernel, rank, inputs, in_specs, out_shapes, out_specs, scratch, name, grid=(1,), cost=None, aliases={}):
    return pl.pallas_call(
        kernel,
        grid_spec=pltpu.PrefetchScalarGridSpec(
            num_scalar_prefetch=1,
            grid=grid,
            in_specs=in_specs,
            out_specs=out_specs,
            scratch_shapes=scratch,
        ),
        out_shape=out_shapes,
        compiler_params=pltpu.CompilerParams(vmem_limit_bytes=VMEM_LIMIT),
        cost_estimate=cost,
        input_output_aliases=aliases,
        name=name,
    )(rank, *inputs)


def cost(us):
    return pl.CostEstimate(flops=int(us * 1e7), bytes_accessed=int(us * 3e4), transcendentals=0)


def pack_kernel(team, chunks, gw, rank_ref, x_ref, bc_ref, dt_ref, *refs):
    xv_ref, tail_ref, bcv_ref, dtv_ref, in_sems, out_sems = refs[-6:]
    outs = list(refs[:-6])
    rank = rank_ref[0]
    rows = x_ref.shape[0]
    cw = gw // chunks
    half = bc_ref.shape[1] // 2

    def fetch(src, dst, sem):
        made = pltpu.make_async_copy(src, dst, in_sems.at[sem])
        made.start()
        return made

    fetches = [fetch(bc_ref, bcv_ref, 0), fetch(dt_ref, dtv_ref, 1)]
    x_fetches = {}
    for k in (2, 3, 1):
        at = pl.multiple_of((rank ^ k) * gw, LANES)
        x_fetches[k] = fetch(x_ref.at[:, pl.ds(at, gw)], xv_ref.at[k - 1], 1 + k)
    tail_fetch = fetch(x_ref.at[pl.ds(rows - HALO, HALO)], tail_ref, 1 + team)

    copies = []

    def copy(src, dst):
        made = pltpu.make_async_copy(src, dst, out_sems.at[len(copies)])
        made.start()
        copies.append(made)

    def copy_bcd(dest, out, first):
        at = pl.multiple_of(dest * STATE, STATE)
        copy(bcv_ref.at[:, pl.ds(at, STATE)], out.at[:, first : first + STATE])
        at = pl.multiple_of(half + dest * STATE, STATE)
        copy(bcv_ref.at[:, pl.ds(at, STATE)], out.at[:, first + STATE : first + 2 * STATE])
        copy(dtv_ref, out.at[:, first + 2 * STATE : first + 2 * STATE + LANES])

    for made in fetches:
        made.wait()
    copy_bcd(rank, outs.pop(0), 0)
    for k in (2, 3):
        copy_bcd(rank ^ k, outs.pop(0), 0)
    near = outs.pop(0)
    copy_bcd(rank ^ 1, near, gw)
    for k in (2, 3):
        x_fetches[k].wait()
        for q in range(chunks):
            copy(xv_ref.at[k - 1, :, pl.ds(q * cw, cw)], outs.pop(0))
    x_fetches[1].wait()
    copy(xv_ref.at[0], near.at[:, 0:gw])
    tail_fetch.wait()
    tail = pl.ds(rows - HALO, HALO)
    for g in range(team):
        out = outs.pop(0)
        copy(tail_ref.at[:, pl.ds(g * gw, gw)], out.at[:, 0:gw])
        copy(bcv_ref.at[tail, pl.ds(g * STATE, STATE)], out.at[:, gw : gw + STATE])
        copy(bcv_ref.at[tail, pl.ds(half + g * STATE, STATE)], out.at[:, gw + STATE : gw + 2 * STATE])
    for made in copies:
        made.wait()


def column_of(row):
    return jnp.transpose(jnp.broadcast_to(row, (LANES, row.shape[1])))


def shift_kernel(taps, rank_ref, docs_ref, shift_ref):
    tiles = shift_ref.shape[0]
    for a in range(tiles):
        near = docs_ref[0:1, a * LANES : (a + 2) * LANES]
        own = column_of(docs_ref[0:1, (a + 1) * LANES : (a + 2) * LANES])
        same = jnp.concatenate([own, own], axis=1) == near
        row, col = iota((LANES, 2 * LANES), 0), iota((LANES, 2 * LANES), 1)
        for back in range(1, taps):
            hit = same & (col == row + (LANES - back))
            shift_ref[a, (back - 1) * LANES : back * LANES, :] = jnp.where(hit, 1.0, 0.0).astype(BF16)


def gather_rows(rank, sources, raw_ref, halo_refs, sems):
    copies = []
    for k, source in enumerate(sources):
        at = pl.multiple_of(LANES + (rank ^ k) * LANES, LANES)
        made = pltpu.make_async_copy(source, raw_ref.at[pl.ds(at, LANES)], sems.at[k])
        made.start()
        copies.append(made)
    halo = halo_refs[0][...].astype(F32)
    for ref in halo_refs[1:]:
        halo = halo + ref[...].astype(F32)
    width = halo.shape[1]
    raw_ref[0 : LANES - HALO, 0:width] = jnp.zeros((LANES - HALO, width), BF16)
    raw_ref[LANES - HALO : LANES, 0:width] = halo.astype(BF16)
    for made in copies:
        made.wait()


def silu(value):
    half = 0.5 * value
    return half + half * jnp.tanh(half)


def conv_tile(raw, shift, taps, bias):
    count = len(taps)
    moved = jnp.dot(shift, raw, preferred_element_type=F32)
    total = raw[LANES:].astype(F32) * taps[count - 1] + bias
    for back in range(1, count):
        total = total + moved[(back - 1) * LANES : back * LANES] * taps[count - 1 - back]
    return silu(total).astype(BF16)


def split_hi(value):
    hi = value.astype(BF16).astype(F32)
    return hi, value - hi


def bc_kernel(team, taps, near_at, rank_ref, *refs):
    bcd = list(refs[:team])
    bcd[1] = bcd[1].at[:, pl.ds(near_at, 2 * STATE + LANES)]
    halo_b = refs[team : 2 * team]
    halo_c = refs[2 * team : 3 * team]
    shift_ref, docs_ref, wb_b_ref, wb_c_ref, heads_ref = refs[3 * team : 3 * team + 5]
    s_ref, bt_ref, cm_ref, uv_ref, row_ref, raw_ref, b_ref, c_ref, sems = refs[3 * team + 5 :]
    rank = rank_ref[0]
    tiles = SPAN // LANES
    own_heads = LANES // team

    copies = []
    for k in range(team):
        at = pl.multiple_of(LANES + (rank ^ k) * LANES, LANES)
        made = pltpu.make_async_copy(bcd[k], raw_ref.at[pl.ds(at, LANES)], sems.at[k])
        made.start()
        copies.append(made)
    raw_ref[0 : LANES - HALO, :] = jnp.zeros((LANES - HALO, raw_ref.shape[1]), BF16)
    for place, parts in ((0, halo_b), (STATE, halo_c)):
        halo = parts[0][...].astype(F32)
        for ref in parts[1:]:
            halo = halo + ref[...].astype(F32)
        raw_ref[LANES - HALO : LANES, place : place + STATE] = halo.astype(BF16)
    for made in copies:
        made.wait()

    lane = iota((LANES, LANES), 1)
    part = lane // own_heads

    def mine(value):
        near = part[: value.shape[0]]
        moved = pltpu.roll(value, (LANES - rank * own_heads) % LANES, 1)
        kept = jnp.where(near == 0, moved, 0.0)
        total = kept
        for step in range(1, team):
            total = total + pltpu.roll(kept, step * own_heads, 1)
        return total

    heads = mine(heads_ref[...])
    bias_row, skip_row = heads[0:1], heads[2:3]
    decay_row = -jnp.exp(heads[1:2])
    ones = jnp.where(iota((LANES, LANES), 0) >= lane, 1.0, 0.0)

    last_doc = docs_ref[0:1, LANES + SPAN - 1 : LANES + SPAN]
    prev_doc = docs_ref[0:1, LANES - 1 : LANES]
    start = jnp.zeros((1, LANES), F32)
    rows_g, rows_e = [], []
    for a in range(tiles):
        here = slice(a * LANES, (a + 1) * LANES)
        raw = raw_ref[a * LANES : (a + 2) * LANES, :]
        shift = shift_ref[a]
        b_tile = conv_tile(raw[:, 0:STATE], shift, [wb_b_ref[i : i + 1, :] for i in range(taps)], wb_b_ref[taps : taps + 1, :])
        c_tile = conv_tile(raw[:, STATE : 2 * STATE], shift, [wb_c_ref[i : i + 1, :] for i in range(taps)], wb_c_ref[taps : taps + 1, :])
        b_ref[here, :] = b_tile
        own = column_of(docs_ref[0:1, (a + 1) * LANES : (a + 2) * LANES])
        own_two = jnp.concatenate([own, own], axis=1)
        cm_ref[here, :] = jnp.where(own_two == prev_doc, c_tile.astype(F32), 0.0).astype(BF16)
        masked = jnp.where(own_two == last_doc, b_tile.astype(F32), 0.0)
        bt_ref[:, here] = jnp.transpose(masked).astype(BF16)
        for b in range(a + 1):
            there = slice(b * LANES, (b + 1) * LANES)
            scores = lax.dot_general(
                c_tile, b_ref[there, :], (((1,), (1,)), ((), ())), preferred_element_type=F32
            )
            keep = own == docs_ref[0:1, (b + 1) * LANES : (b + 2) * LANES]
            if a == b:
                keep = keep & (iota((LANES, LANES), 0) >= lane)
            s_ref[here, there] = jnp.where(keep, scores, 0.0).astype(BF16)
        raised = mine(raw[LANES:, 2 * STATE : 2 * STATE + LANES].astype(F32)) + bias_row
        step = jnp.maximum(raised, 0.0) + jnp.log1p(jnp.exp(-jnp.abs(raised)))
        cum = jnp.dot(ones, decay_row * step, precision=lax.Precision.HIGHEST, preferred_element_type=F32)
        u_hi, u_lo = split_hi(jnp.exp(cum))
        v_hi, v_lo = split_hi(jnp.exp(-cum) * step)
        packed = jnp.where(part == 0, v_hi, jnp.where(part == 1, v_lo, jnp.where(part == 2, u_hi, u_lo)))
        uv_ref[here, :] = packed.astype(BF16)
        tile_total = cum[LANES - 1 : LANES]
        rows_g.append(jnp.exp(tile_total))
        rows_e.append(jnp.exp(start))
        start = start + tile_total
    passes = jnp.exp(start) * jnp.where(last_doc == prev_doc, 1.0, 0.0)
    every = rows_g + rows_e + [skip_row, passes] + [jnp.zeros((1, LANES), F32)] * 6
    hi, lo = split_hi(jnp.concatenate(every, axis=0))
    near = part[: 16]
    row_ref[...] = jnp.where(near == 0, hi, jnp.where(near == 1, lo, 0.0)).astype(BF16)


def spreader(first, width, hdim, own_heads, upper):
    row, col = iota((LANES, width), 0), iota((LANES, width), 1)
    hit = (row % own_heads) == (first + col // hdim)
    half = (row >= 2 * own_heads) if upper else (row < 2 * own_heads)
    return jnp.where(hit & half, 1.0, 0.0).astype(BF16)


def mix_kernel(team, taps, first, hdim, start_col, own_cols, rank_ref, *refs):
    x_ref = refs[0]
    got = refs[1:team]
    halos = refs[team : 2 * team]
    shift_ref, wb_ref, s_ref, bt_ref, uv_ref, row_ref = refs[2 * team : 2 * team + 6]
    xc_ref, yl_ref, st_ref, raw_ref, xf_ref, xb_ref, sems = refs[2 * team + 6 :]
    rank = rank_ref[0]
    tiles = SPAN // LANES
    width = xc_ref.shape[1]
    own_heads = LANES // team
    at = pl.multiple_of(rank * own_cols + start_col, LANES)
    sources = [x_ref.at[:, pl.ds(at, width)], got[0].at[:, pl.ds(start_col, width)], got[1], got[2]]
    gather_rows(rank, sources, raw_ref, halos, sems)
    spread_v = spreader(first, width, hdim, own_heads, False)
    spread_u = spreader(first, width, hdim, own_heads, True)
    rows = jnp.dot(row_ref[...], spread_v, preferred_element_type=F32)
    skip = rows[2 * tiles : 2 * tiles + 1]
    weights = [wb_ref[i : i + 1, :] for i in range(taps)]
    bias = wb_ref[taps : taps + 1, :]
    for a in range(tiles):
        here = slice(a * LANES, (a + 1) * LANES)
        xc = conv_tile(raw_ref[a * LANES : (a + 2) * LANES, :], shift_ref[a], weights, bias)
        xc_ref[here, :] = xc
        xf = xc.astype(F32)
        uv = uv_ref[here, :]
        scaled = jnp.dot(uv, spread_v, preferred_element_type=F32) * xf
        xf_ref[here, :] = scaled
        xb_ref[here, :] = scaled.astype(BF16)
        total = jnp.dot(
            s_ref[here, 0 : (a + 1) * LANES], xb_ref[0 : (a + 1) * LANES, :], preferred_element_type=F32
        )
        yl_ref[here, :] = jnp.dot(uv, spread_u, preferred_element_type=F32) * total + skip * xf
        for b in range(a + 1):
            there = slice(b * LANES, (b + 1) * LANES)
            later = xf_ref[there, :] * rows[a : a + 1]
            if a < tiles - 1:
                xf_ref[there, :] = later
            xb_ref[there, :] = later.astype(BF16)
    st_ref[...] = jnp.dot(bt_ref[...], xb_ref[...], preferred_element_type=F32).astype(BF16)


def carry_kernel(team, first, hdim, rank_ref, st_ref, yl_ref, xc_ref, cm_ref, uv_ref, row_ref, docs_ref, *refs):
    outs = refs[-team - 2 : -2]
    stat_ref, rows_ref = refs[-2:]
    rank = rank_ref[0]
    tiles = SPAN // LANES
    width = xc_ref.shape[1]
    own_heads = LANES // team
    spread_v = spreader(first, width, hdim, own_heads, False)
    spread_u = spreader(first, width, hdim, own_heads, True)
    rows_ref[...] = jnp.dot(row_ref[...], spread_v, preferred_element_type=F32)
    sums = jnp.zeros((DOCS, 3 * LANES), F32)
    for k in range(team):
        tile = rank ^ k
        here = pl.ds(pl.multiple_of(tile * LANES, LANES), LANES)
        came = jnp.dot(cm_ref[here, :], st_ref[...], preferred_element_type=F32)
        decay = jnp.dot(uv_ref[here, :], spread_u, preferred_element_type=F32)
        y = yl_ref[here, :] + decay * (came * rows_ref[pl.ds(tiles + tile, 1), :])
        y = y.astype(BF16)
        outs[k][...] = y
        y = y.astype(F32)
        x = xc_ref[here, :].astype(F32)
        parts = []
        for product in (y * x, y * y, x * x):
            part = product[:, 0:LANES]
            for c in range(1, width // LANES):
                part = part + product[:, c * LANES : (c + 1) * LANES]
            parts.append(part)
        docs = docs_ref[0:1, pl.ds(pl.multiple_of((tile + 1) * LANES, LANES), LANES)]
        table = jnp.where(iota((DOCS, LANES), 0).astype(F32) == docs, 1.0, 0.0)
        sums = sums + jnp.dot(
            table, jnp.concatenate(parts, axis=1), precision=lax.Precision.HIGHEST, preferred_element_type=F32
        )
    lane = iota((DOCS, LANES), 1)
    out = jnp.zeros((DOCS, LANES), F32)
    for i in range(3):
        out = jnp.where(lane == i, jnp.sum(sums[:, i * LANES : (i + 1) * LANES], axis=1, keepdims=True), out)
    stat_ref[...] = out


def norm_kernel(team, chunks, rank_ref, *refs):
    y_refs = refs[:-4]
    z_ref, gain_ref, out_ref, gated_ref = refs[-4:]
    width = z_ref.shape[1]
    cw = width // chunks
    for k in range(team):

        @pl.when(pl.program_id(0) == k)
        def _():
            part = jnp.zeros((LANES, LANES), F32)
            for q in range(chunks):
                cols = slice(q * cw, (q + 1) * cw)
                y = y_refs[k][:, cols] if k < 2 else y_refs[2 + (k - 2) * chunks + q][...]
                gated = y.astype(F32) * silu(z_ref[:, cols].astype(F32))
                gated_ref[:, cols] = gated
                square = gated * gated
                for c in range(cw // LANES):
                    part = part + square[:, c * LANES : (c + 1) * LANES]
            scale = lax.rsqrt(jnp.sum(part, axis=1, keepdims=True) * (1.0 / width) + 1e-05)
            for q in range(chunks):
                cols = slice(q * cw, (q + 1) * cw)
                out_ref[:, cols] = (gated_ref[:, cols] * scale * gain_ref[0:1, cols]).astype(BF16)


def on_device(
    x_stream,
    bc_stream,
    z_stream,
    dt_raw,
    doc_ids,
    conv_weight,
    conv_bias,
    dt_bias,
    a_log,
    skip_d,
    norm_gain,
):
    rows, inner = x_stream.shape
    heads = dt_raw.shape[1]
    hdim = inner // heads
    taps = conv_weight.shape[0]
    members = lax.axis_size("seq")
    team = SPAN // rows
    tiles = SPAN // LANES
    gw = inner // team
    cw = gw // CHUNKS
    me = lax.axis_index("seq")
    rank = jnp.reshape(me % team, (1,)).astype(jnp.int32)
    doc_most = rows * members // 4
    hops = (doc_most - 2) // SPAN + 1

    swap = lambda array, k: lax.ppermute(array, "seq", [(i, i ^ k) for i in range(members)])
    onward = lambda array: lax.ppermute(array, "seq", [(i, i + team) for i in range(members - team)])

    shape = jax.ShapeDtypeStruct
    bcd_w = 2 * STATE + LANES
    halo_w = gw + 2 * STATE
    pack_shapes = (
        [shape((rows, bcd_w), BF16)] * 3
        + [shape((rows, gw + bcd_w), BF16)]
        + [shape((rows, cw), BF16)] * (2 * CHUNKS)
        + [shape((HALO, halo_w), BF16)] * team
    )
    packed = call(
        functools.partial(pack_kernel, team, CHUNKS, gw),
        rank,
        (x_stream, bc_stream, dt_raw),
        [ANY] * 3,
        pack_shapes,
        [ANY] * len(pack_shapes),
        [
            pltpu.VMEM((team - 1, rows, gw), BF16),
            pltpu.VMEM((HALO, inner), BF16),
            pltpu.VMEM(bc_stream.shape, BF16),
            pltpu.VMEM(dt_raw.shape, BF16),
            pltpu.SemaphoreType.DMA((2 + team,)),
            pltpu.SemaphoreType.DMA((3 * team + 2 * CHUNKS + 1 + 3 * team,)),
        ],
        "pack",
        cost=cost(2),
    )
    bcd = [packed[0], None, swap(packed[1], 2), swap(packed[2], 3)]
    bcd[1] = swap(packed[3], 1)
    halos = []
    for g in range(team):
        pairs = [(i, i - i % team + team + g) for i in range(team - 1, members - team, team)]
        halos.append(lax.ppermute(packed[4 + 2 * CHUNKS + g], "seq", pairs))
    got = [
        [bcd[1], swap(packed[4 + q], 2), swap(packed[4 + CHUNKS + q], 3)] for q in range(CHUNKS)
    ]

    ext_docs = jnp.concatenate([jnp.full((LANES,), -1, jnp.int32), doc_ids])
    docs = lax.dynamic_slice_in_dim(ext_docs, (me // team) * SPAN, SPAN + LANES).astype(F32)[None]
    wb = jnp.concatenate([conv_weight, conv_bias[None]], axis=0)
    head_rows = jnp.concatenate(
        [dt_bias[None], a_log[None], skip_d[None], jnp.zeros((5, heads), F32)], axis=0
    )
    shift_shape = (tiles, (taps - 1) * LANES, 2 * LANES)
    shift = call(
        functools.partial(shift_kernel, taps),
        rank,
        (docs,),
        [whole(docs.shape)],
        shape(shift_shape, BF16),
        whole(shift_shape),
        [],
        "shift",
        cost=cost(1.5),
    )

    b_block, c_block = inner // STATE, inner // STATE + team
    scores, b_turned, c_masked, uv, row_pack = call(
        functools.partial(bc_kernel, team, taps, gw),
        rank,
        (*bcd, *halos, *halos, shift, docs, wb, wb, head_rows),
        [ANY] * team
        + [pl.BlockSpec((HALO, STATE), lambda i, pref: (0, gw // STATE))] * team
        + [pl.BlockSpec((HALO, STATE), lambda i, pref: (0, gw // STATE + 1))] * team
        + [
            whole(shift_shape),
            whole(docs.shape),
            pl.BlockSpec((taps + 1, STATE), lambda i, pref: (0, b_block + pref[0])),
            pl.BlockSpec((taps + 1, STATE), lambda i, pref: (0, c_block + pref[0])),
            whole(head_rows.shape),
        ],
        [
            shape((SPAN, SPAN), BF16),
            shape((STATE, SPAN), BF16),
            shape((SPAN, STATE), BF16),
            shape((SPAN, LANES), BF16),
            shape((16, LANES), BF16),
        ],
        [
            whole((SPAN, SPAN)),
            whole((STATE, SPAN)),
            whole((SPAN, STATE)),
            whole((SPAN, LANES)),
            whole((16, LANES)),
        ],
        [
            pltpu.VMEM((LANES + SPAN, bcd_w), BF16),
            pltpu.VMEM((SPAN, STATE), BF16),
            pltpu.VMEM((SPAN, STATE), BF16),
            pltpu.SemaphoreType.DMA((team,)),
        ],
        "bc",
        cost=cost(4),
    )

    per_chunk = cw // hdim
    y_parts, stats = [], None
    for q in range(CHUNKS):
        xc, y_local, fresh = call(
            functools.partial(mix_kernel, team, taps, q * per_chunk, hdim, q * cw, gw),
            rank,
            (x_stream, *got[q], *halos, shift, wb, scores, b_turned, uv, row_pack),
            [ANY] * team
            + [pl.BlockSpec((HALO, cw), lambda i, pref, q=q: (0, q))] * team
            + [
                whole(shift_shape),
                pl.BlockSpec((taps + 1, cw), lambda i, pref, q=q: (0, pref[0] * CHUNKS + q)),
                whole((SPAN, SPAN)),
                whole((STATE, SPAN)),
                whole((SPAN, LANES)),
                whole((16, LANES)),
            ],
            [shape((SPAN, cw), BF16), shape((SPAN, cw), F32), shape((STATE, cw), BF16)],
            [whole((SPAN, cw)), whole((SPAN, cw)), whole((STATE, cw))],
            [
                pltpu.VMEM((LANES + SPAN, cw), BF16),
                pltpu.VMEM((SPAN, cw), F32),
                pltpu.VMEM((SPAN, cw), BF16),
                pltpu.SemaphoreType.DMA((team,)),
            ],
            "mix",
            cost=cost(4),
        )
        state = onward(fresh)
        if hops > 1:
            own_heads = heads // team
            first = q * per_chunk
            part = row_pack[2 * tiles + 1].astype(F32)
            kept = part[first : first + per_chunk] + part[own_heads + first : own_heads + first + per_chunk]
            kept = jnp.repeat(kept, hdim)[None]
            for _ in range(hops - 1):
                state = onward((fresh.astype(F32) + kept * state.astype(F32)).astype(BF16))
        outs = call(
            functools.partial(carry_kernel, team, q * per_chunk, hdim),
            rank,
            (state, y_local, xc, c_masked, uv, row_pack, docs) + ((y_own, y_near) if q else ()),
            [
                whole((STATE, cw)),
                whole((SPAN, cw)),
                whole((SPAN, cw)),
                whole((SPAN, STATE)),
                whole((SPAN, LANES)),
                whole((16, LANES)),
                whole(docs.shape),
            ]
            + [ANY] * (2 if q else 0),
            [shape((rows, gw), BF16)] * 2 + [shape((rows, cw), BF16)] * 2 + [shape((DOCS, LANES), F32)],
            [pl.BlockSpec((rows, cw), lambda i, pref, q=q: (0, q))] * 2
            + [whole((rows, cw))] * 2
            + [whole((DOCS, LANES))],
            [pltpu.VMEM((16, cw), F32)],
            "carry",
            cost=cost(3),
            aliases={8: 0, 9: 1} if q else {},
        )
        y_own, y_near = outs[:2]
        y_parts.append([swap(outs[k], k) for k in (2, 3)])
        stats = outs[team] if stats is None else stats + outs[team]
    y_near = swap(y_near, 1)

    step = 1
    while step < members:
        stats = stats + swap(stats, step)
        step *= 2

    mixed = call(
        functools.partial(norm_kernel, team, CHUNKS),
        rank,
        (y_own, y_near, *[y_parts[q][k] for k in range(2) for q in range(CHUNKS)], z_stream, norm_gain[None]),
        [whole((rows, gw))] * 2
        + [whole((rows, cw))] * (2 * CHUNKS)
        + [
            pl.BlockSpec((rows, gw), lambda i, pref: (0, pref[0] ^ i)),
            pl.BlockSpec((1, gw), lambda i, pref: (0, pref[0] ^ i)),
        ],
        shape((rows, inner), BF16),
        pl.BlockSpec((rows, gw), lambda i, pref: (0, pref[0] ^ i)),
        [pltpu.VMEM((rows, gw), F32)],
        "norm",
        grid=(team,),
        cost=cost(4),
    )
    doc_cosine = stats[:, 0] / jnp.sqrt(stats[:, 1] * stats[:, 2] + 1e-06)
    return (mixed, doc_cosine)


def solution(mesh):
    return jax.shard_map(
        on_device,
        mesh=mesh,
        in_specs=(
            P(("groups", "seq"), None),
            P(("groups", "seq"), None),
            P(("groups", "seq"), None),
            P(("groups", "seq"), None),
            P("groups"),
            P(),
            P(),
            P(),
            P(),
            P(),
            P(),
        ),
        out_specs=(P(("groups", "seq"), None), P("groups")),
        check_vma=False,
    )
```

time: 289 us -> 116 us (0.40)
  blocking collectives: 54.2 us -> 0 us
  matrix products: 40.7 us -> 0 us
  local copies, waits for them, and re-layouts: 48.5 us -> 9.03 us
  other arithmetic: 33.4 us -> 0.95 us
  waiting for transfers between devices: 64.1 us -> 36.3 us
  Pallas kernels: 0 us -> 24.9 us
  loops' own time: 4.77 us -> 0 us
  starting transfers between devices: 38.1 us -> 42.1 us
    all_to_all x4 -> x0, waiting for transfers between devices: 64.1 us -> none  [the longest x1 38.4 us: on_device(): lax.all_to_all(x_send, 'seq', split_axis=2, concat_axis=0, tiled=True)]
    psum x1 -> x0, blocking collectives: 54.2 us -> none  [on_device(): doc_totals = lax.psum(partial_sums, 'seq')]
    dot_general x17 -> x0, matrix products: 40.7 us -> none  [the longest x4 17.2 us: span_step(): jnp.einsum('hij,jhp->ihp', weights, x_span, preferred_element_type=jnp.fl...]
    ppermute x1 -> x32, starting transfers between devices: 2.36 us -> 42.1 us  [the longest x24 29.1 us: on_device(): lax.ppermute(array, 'seq', [(i, i ^ k) for i in range(members)])]
    ppermute x1 -> x32, waiting for transfers between devices: 0.01 us -> 36.3 us  [the longest x24 32.4 us: on_device(): lax.ppermute(array, 'seq', [(i, i ^ k) for i in range(members)])]
    all_to_all x4 -> x0, starting transfers between devices: 35.8 us -> none  [the longest x1 11.3 us: on_device(): lax.all_to_all(bc_send, 'seq', split_axis=2, concat_axis=0, tiled=True)]
    pallas_call x0 -> x12, Pallas kernels: none -> 24.9 us  [call(): pl.pallas_call(kernel, grid_spec=pltpu.PrefetchScalarGridSpec(num_scalar_...]
    convert_element_type x10 -> x1, other arithmetic: 20.7 us -> 0.08 us  [on_device(): lax.dynamic_slice_in_dim(ext_docs, me // team * SPAN, SPAN + LANES)]
  transfers between devices with their start and end apart: 5 -> 32, of which waited for: 2 -> 12; matrix products, arithmetic and copies ran while one was open for 17% -> 1% of each run, Pallas kernels for 0% -> 16%
where the time goes in v1:
time: 116 us; the launch traced here: 114 us
  starting transfers between devices  42.1 us (36%)
  waiting for transfers between devices  36.3 us (31%)
  Pallas kernels  24.9 us (21%)
  local copies, waits for them, and re-layouts  9.03 us (8%)
    ppermute x24, waiting for transfers between devices, on_device(): lax.ppermute(array, 'seq', [(i, i ^ k) for i in range(members)])  32.4 us
    ppermute x24, starting transfers between devices, on_device(): lax.ppermute(array, 'seq', [(i, i ^ k) for i in range(members)])  29.1 us
    pallas_call x12, Pallas kernels, call(): pl.pallas_call(kernel, grid_spec=pltpu.PrefetchScalarGridSpec(num_scalar_...  24.9 us
    ppermute x4, starting transfers between devices, on_device(): lax.ppermute(array, 'seq', [(i, i + team) for i in range(members - team)])  10.4 us
    unnamed x42, local copies, waits for them, and re-layouts  8.95 us
    ppermute x4, waiting for transfers between devices, on_device(): lax.ppermute(array, 'seq', [(i, i + team) for i in range(members - team)])  3.88 us
    ppermute x4, starting transfers between devices, on_device(): halos.append(lax.ppermute(packed[4 + 2 * CHUNKS + g], 'seq', pairs))  2.65 us
  transfers between devices with their start and end apart: 32, of which 12 were waited for; matrix products, arithmetic and copies ran while one was open for 1% of the time, Pallas kernels for 16%

profile of v1, /device:TPU:0, one launch (start us, length us, event | category | flops | bytes accessed | tf_op | source)
XLA Modules:
  0.0 114.3 jit_solution(10028322734208500627)
XLA Ops:
  0.7 1.6 %copy-done = bf16[128,8192]{1,0:T(8,128)(2,1)S(1)} copy-done((bf16[128,8192]{1,0:T(8,128)(2,1)S(1)}, bf16[128,8192]{1,0:T(8,128)(2,1)}, u32[]{:S(2)}) %copy-start) | copy-done | bytes 2097176
  2.3 1.0 copy-done.3
  3.3 0.8 copy-done.8
  4.1 1.7 %pack.1 = (bf16[128,640]{1,0:T(8,128)(2,1)S(1)}, bf16[128,640]{1,0:T(8,128)(2,1)}, bf16[128,640]{1,0:T(8,128)(2,1)}, bf16[128,2688]{1,0:T(8,128)(2,1)}, bf16[128...) custom-call(s32[1]{0:T(128)} %bitcast.rank_ref, ...), custom_call_target="tpu_custom_call" | custom-call | flops 20000000 | bytes 60000 | tf_op jit(solution)/shard_map/pack/pallas_call | solution.py:32
  5.8 0.7 copy-done.4
  7.1 0.7 copy-done.11
  7.8 0.7 copy-done.12
  9.7 3.0 %collective-permute-start.16 = (bf16[128,512]{1,0:T(8,128)(2,1)S(1)}, bf16[128,512]{1,0:T(8,128)(2,1)S(1)}, u32[]{:S(2)}, u32[]{:S(2)}) collective-permute-start(bf16[128,512]{1,0:T(8,128)(2,1)S(1)} %get-tuple-element.83), channel_id=1, source_target_pairs={{0,2},{1,3},{2,0},{3,1},{4,6},{5,7},{6,4},{7,5},{8,10},{9,11},{10,... | collective-permute-start | bytes 393224 | tf_op jit(solution)/shard_map/ppermute | solution.py:387
  14.0 0.7 collective-permute-start.5
  14.7 0.7 collective-permute-start.6
  15.5 8.2 %collective-permute-start.7 = (bf16[128,640]{1,0:T(8,128)(2,1)}, bf16[128,640]{1,0:T(8,128)(2,1)}, u32[]{:S(2)}, u32[]{:S(2)}) collective-permute-start(bf16[128,640]{1,0:T(8,128)(2,1)} %get-tuple-element.63), channel_id=1, source_target_pairs={{0,2},{1,3},{2,0},{3,1},{4,6},{5,7},{6,4},{7,5},{8,10},{9,11},{10,... | collective-permute-start | bytes 491528 | tf_op jit(solution)/shard_map/ppermute | solution.py:387
  23.7 1.7 %collective-permute-start.17 = (bf16[128,512]{1,0:T(8,128)(2,1)}, bf16[128,512]{1,0:T(8,128)(2,1)}, u32[]{:S(2)}, u32[]{:S(2)}) collective-permute-start(bf16[128,512]{1,0:T(8,128)(2,1)} %get-tuple-element.84), channel_id=1, source_target_pairs={{0,3},{1,2},{2,1},{3,0},{4,7},{5,6},{6,5},{7,4},{8,11},{9,10},{10,... | collective-permute-start | bytes 393224 | tf_op jit(solution)/shard_map/ppermute | solution.py:387
  26.6 8.3 %collective-permute-done.17.refs_3_ = bf16[128,512]{1,0:T(8,128)(2,1)} collective-permute-done((bf16[128,512]{1,0:T(8,128)(2,1)}, bf16[128,512]{1,0:T(8,128)(2,1)}, u32[]{:S(2)}, u32[]{:S(2)}) %collective-permute-start.17) | collective-permute-done | bytes 131104 | tf_op jit(solution)/shard_map/ppermute | solution.py:387
  34.9 1.9 %collective-permute-start.14 = (bf16[128,512]{1,0:T(8,128)(2,1)}, bf16[128,512]{1,0:T(8,128)(2,1)S(1)}, u32[]{:S(2)}, u32[]{:S(2)}) collective-permute-start(bf16[128,512]{1,0:T(8,128)(2,1)} %copy-done.14), channel_id=1, source_target_pairs={{0,3},{1,2},{2,1},{3,0},{4,7},{5,6},{6,5},{7,4},{8,11},{9,10},{10,... | collective-permute-start | bytes 393224 | tf_op jit(solution)/shard_map/ppermute | solution.py:387
  36.8 0.8 collective-permute-done.13.refs_2_
  37.5 2.0 %collective-permute-start.10 = (bf16[128,512]{1,0:T(8,128)(2,1)}, bf16[128,512]{1,0:T(8,128)(2,1)S(1)}, u32[]{:S(2)}, u32[]{:S(2)}) collective-permute-start(bf16[128,512]{1,0:T(8,128)(2,1)} %copy-done.13), channel_id=1, source_target_pairs={{0,2},{1,3},{2,0},{3,1},{4,6},{5,7},{6,4},{7,5},{8,10},{9,11},{10,... | collective-permute-start | bytes 393224 | tf_op jit(solution)/shard_map/ppermute | solution.py:387
  39.9 1.5 %collective-permute-start.2 = (bf16[128,512]{1,0:T(8,128)(2,1)}, bf16[128,512]{1,0:T(8,128)(2,1)S(1)}, u32[]{:S(2)}, u32[]{:S(2)}) collective-permute-start(bf16[128,512]{1,0:T(8,128)(2,1)} %copy-done.10), channel_id=1, source_target_pairs={{0,3},{1,2},{2,1},{3,0},{4,7},{5,6},{6,5},{7,4},{8,11},{9,10},{10,... | collective-permute-start | bytes 393224 | tf_op jit(solution)/shard_map/ppermute | solution.py:387
  41.5 0.9 copy-done.5
  42.4 3.3 %bc.1 = (bf16[512,512]{1,0:T(8,128)(2,1)S(1)}, bf16[256,512]{1,0:T(8,128)(2,1)S(1)}, bf16[512,256]{1,0:T(8,128)(2,1)S(1)}, bf16[512,128]{1,0:T(8,128)(2,1)S(1)}, bf16[16,128]{1,0:T(8,128)(2,1)S(1)}) custom-call(s32[1]{0:T(128)} %bitcast.rank_ref, bf16[128,640]{1,0:T(8,128)(2,1)S(1)} %copy-done.5, bf16[128,2688]{1,0:T(8,128)(2,1)S(1)} %collective-permute-done.refs_1_, ...), custom_call_target="tpu_custom_call" | custom-call | flops 40000000 | bytes 120000 | tf_op jit(solution)/shard_map/bc/pallas_call | solution.py:32
  45.7 3.1 %mix.7 = (bf16[512,512]{1,0:T(8,128)(2,1)S(1)}, f32[512,512]{1,0:T(8,128)S(1)}, bf16[256,512]{1,0:T(8,128)(2,1)S(1)}) custom-call(s32[1]{0:T(128)} %bitcast.rank_ref, bf16[128,8192]{1,0:T(8,128)(2,1)S(1)} %copy-done.1, bf16[128,2688]{1,0:T(8,128)(2,1)S(1)} %collective-permute-done.refs_1_, bf16[128,512]{1,0:T(8,128)(2,1)S(1)} %copy-done.7, ...), custom_call_target="tpu_custom_call" | custom-call | flops 40000000 | bytes 120000 | tf_op jit(solution)/shard_map/mix/pallas_call | solution.py:32
  48.9 3.5 %collective-permute-start.18 = (bf16[256,512]{1,0:T(8,128)(2,1)S(1)}, bf16[256,512]{1,0:T(8,128)(2,1)S(1)}, u32[]{:S(2)}, u32[]{:S(2)}) collective-permute-start(bf16[256,512]{1,0:T(8,128)(2,1)S(1)} %get-tuple-element.85), channel_id=1, source_target_pairs={{0,4},{1,5},{2,6},{3,7},{4,8},{5,9},{6,10},{7,11},{8,12},{9,13},{1... | collective-permute-start | bytes 786440 | tf_op jit(solution)/shard_map/ppermute | solution.py:388
  52.4 2.9 %mix.6 = (bf16[512,512]{1,0:T(8,128)(2,1)S(1)}, f32[512,512]{1,0:T(8,128)S(1)}, bf16[256,512]{1,0:T(8,128)(2,1)S(1)}) custom-call(s32[1]{0:T(128)} %bitcast.rank_ref, bf16[128,8192]{1,0:T(8,128)(2,1)S(1)} %copy-done.1, bf16[128,2688]{1,0:T(8,128)(2,1)S(1)} %collective-permute-done.refs_1_, bf16[128,512]{1,0:T(8,128)(2,1)} %collective-permute-done.13.refs_2_, ...), custom_call_target="tpu_custom_call" | custom-call | flops 40000000 | bytes 120000 | tf_op jit(solution)/shard_map/mix/pallas_call | solution.py:32
  55.4 2.2 %collective-permute-start.15 = (bf16[256,512]{1,0:T(8,128)(2,1)S(1)}, bf16[256,512]{1,0:T(8,128)(2,1)S(1)}, u32[]{:S(2)}, u32[]{:S(2)}) collective-permute-start(bf16[256,512]{1,0:T(8,128)(2,1)S(1)} %get-tuple-element.80), channel_id=1, source_target_pairs={{0,4},{1,5},{2,6},{3,7},{4,8},{5,9},{6,10},{7,11},{8,12},{9,13},{1... | collective-permute-start | bytes 786440 | tf_op jit(solution)/shard_map/ppermute | solution.py:388
  57.6 2.4 %mix.5 = (bf16[512,512]{1,0:T(8,128)(2,1)S(1)}, f32[512,512]{1,0:T(8,128)S(1)}, bf16[256,512]{1,0:T(8,128)(2,1)S(1)}) custom-call(s32[1]{0:T(128)} %bitcast.rank_ref, bf16[128,8192]{1,0:T(8,128)(2,1)S(1)} %copy-done.1, bf16[128,2688]{1,0:T(8,128)(2,1)S(1)} %collective-permute-done.refs_1_, bf16[128,512]{1,0:T(8,128)(2,1)S(1)} %collective-permute-done.10.refs_2_, ...), custom_call_target="tpu_custom_call" | custom-call | flops 40000000 | bytes 120000 | tf_op jit(solution)/shard_map/mix/pallas_call | solution.py:32
  60.0 2.6 %collective-permute-start.12 = (bf16[256,512]{1,0:T(8,128)(2,1)S(1)}, bf16[256,512]{1,0:T(8,128)(2,1)S(1)}, u32[]{:S(2)}, u32[]{:S(2)}) collective-permute-start(bf16[256,512]{1,0:T(8,128)(2,1)S(1)} %get-tuple-element.75), channel_id=1, source_target_pairs={{0,4},{1,5},{2,6},{3,7},{4,8},{5,9},{6,10},{7,11},{8,12},{9,13},{1... | collective-permute-start | bytes 786440 | tf_op jit(solution)/shard_map/ppermute | solution.py:388
  62.6 2.4 %mix.4 = (bf16[512,512]{1,0:T(8,128)(2,1)S(1)}, f32[512,512]{1,0:T(8,128)S(1)}, bf16[256,512]{1,0:T(8,128)(2,1)S(1)}) custom-call(s32[1]{0:T(128)} %bitcast.rank_ref, bf16[128,8192]{1,0:T(8,128)(2,1)S(1)} %copy-done.1, bf16[128,2688]{1,0:T(8,128)(2,1)S(1)} %collective-permute-done.refs_1_, bf16[128,512]{1,0:T(8,128)(2,1)S(1)} %collective-permute-done.1.refs_2_, ...), custom_call_target="tpu_custom_call" | custom-call | flops 40000000 | bytes 120000 | tf_op jit(solution)/shard_map/mix/pallas_call | solution.py:32
  65.0 2.1 %collective-permute-start.9 = (bf16[256,512]{1,0:T(8,128)(2,1)S(1)}, bf16[256,512]{1,0:T(8,128)(2,1)S(1)}, u32[]{:S(2)}, u32[]{:S(2)}) collective-permute-start(bf16[256,512]{1,0:T(8,128)(2,1)S(1)} %get-tuple-element.69), channel_id=1, source_target_pairs={{0,4},{1,5},{2,6},{3,7},{4,8},{5,9},{6,10},{7,11},{8,12},{9,13},{1... | collective-permute-start | bytes 786440 | tf_op jit(solution)/shard_map/ppermute | solution.py:388
  67.1 1.4 %carry.4 = (bf16[128,2048]{1,0:T(8,128)(2,1)S(1)}, bf16[128,2048]{1,0:T(8,128)(2,1)S(1)}, bf16[128,512]{1,0:T(8,128)(2,1)S(1)}, bf16[128,512]{1,0:T(8,128)(2,1)S(1)}, f32[16,128]{1,0:T(8,128)S(1)}) custom-call(s32[1]{0:T(128)} %bitcast.rank_ref, bf16[256,512]{1,0:T(8,128)(2,1)S(1)} %collective-permute-done.18.st_ref, ...), custom_call_target="tpu_custom_call" | custom-call | flops 30000000 | bytes 90000 | tf_op jit(solution)/shard_map/carry/pallas_call | solution.py:32
  68.6 1.4 %carry.5 = (bf16[128,2048]{1,0:T(8,128)(2,1)S(1)}, bf16[128,2048]{1,0:T(8,128)(2,1)S(1)}, bf16[128,512]{1,0:T(8,128)(2,1)S(1)}, bf16[128,512]{1,0:T(8,128)(2,1)S(1)}, f32[16,128]{1,0:T(8,128)S(1)}) custom-call(s32[1]{0:T(128)} %bitcast.rank_ref, bf16[256,512]{1,0:T(8,128)(2,1)S(1)} %collective-permute-done.15.st_ref, ...), custom_call_target="tpu_custom_call", output_to_operand_aliasing={{0}: (8, {}), {1}: (9, {})} | custom-call | flops 30000000 | bytes 90000 | tf_op jit(solution)/shard_map/carry/pallas_call | solution.py:32
  70.2 1.5 %carry.6 = (bf16[128,2048]{1,0:T(8,128)(2,1)S(1)}, bf16[128,2048]{1,0:T(8,128)(2,1)S(1)}, bf16[128,512]{1,0:T(8,128)(2,1)S(1)}, bf16[128,512]{1,0:T(8,128)(2,1)S(1)}, f32[16,128]{1,0:T(8,128)S(1)}) custom-call(s32[1]{0:T(128)} %bitcast.rank_ref, bf16[256,512]{1,0:T(8,128)(2,1)S(1)} %collective-permute-done.12.st_ref, ...), custom_call_target="tpu_custom_call", output_to_operand_aliasing={{0}: (8, {}), {1}: (9, {})} | custom-call | flops 30000000 | bytes 90000 | tf_op jit(solution)/shard_map/carry/pallas_call | solution.py:32
  71.7 3.7 %collective-permute-done.9.st_ref = bf16[256,512]{1,0:T(8,128)(2,1)S(1)} collective-permute-done((bf16[256,512]{1,0:T(8,128)(2,1)S(1)}, bf16[256,512]{1,0:T(8,128)(2,1)S(1)}, u32[]{:S(2)}, u32[]{:S(2)}) %collective-permute-start.9) | collective-permute-done | bytes 262176 | tf_op jit(solution)/shard_map/ppermute | solution.py:388
  75.4 1.4 %carry.7 = (bf16[128,2048]{1,0:T(8,128)(2,1)S(1)}, bf16[128,2048]{1,0:T(8,128)(2,1)S(1)}, bf16[128,512]{1,0:T(8,128)(2,1)S(1)}, bf16[128,512]{1,0:T(8,128)(2,1)S(1)}, f32[16,128]{1,0:T(8,128)S(1)}) custom-call(s32[1]{0:T(128)} %bitcast.rank_ref, bf16[256,512]{1,0:T(8,128)(2,1)S(1)} %collective-permute-done.9.st_ref, ...), custom_call_target="tpu_custom_call", output_to_operand_aliasing={{0}: (8, {}), {1}: (9, {})} | custom-call | flops 30000000 | bytes 90000 | tf_op jit(solution)/shard_map/carry/pallas_call | solution.py:32
  77.3 1.4 %collective-permute-done.28 = f32[16,128]{1,0:T(8,128)S(1)} collective-permute-done((f32[16,128]{1,0:T(8,128)S(1)}, f32[16,128]{1,0:T(8,128)S(1)}, u32[]{:S(2)}, u32[]{:S(2)}) %collective-permute-start.28) | collective-permute-done | bytes 8224 | tf_op jit(solution)/shard_map/ppermute | solution.py:387
  78.9 3.5 %collective-permute-done.29 = f32[16,128]{1,0:T(8,128)S(1)} collective-permute-done((f32[16,128]{1,0:T(8,128)S(1)}, f32[16,128]{1,0:T(8,128)S(1)}, u32[]{:S(2)}, u32[]{:S(2)}) %collective-permute-start.29) | collective-permute-done | bytes 8224 | tf_op jit(solution)/shard_map/ppermute | solution.py:387
  82.4 2.5 %collective-permute-start.30 = (f32[16,128]{1,0:T(8,128)S(1)}, f32[16,128]{1,0:T(8,128)S(1)}, u32[]{:S(2)}, u32[]{:S(2)}) collective-permute-start(f32[16,128]{1,0:T(8,128)S(1)} %add.41), channel_id=1, source_target_pairs={{0,4},{1,5},{2,6},{3,7},{4,0},{5,1},{6,2},{7,3},{8,12},{9,13},{10,... | collective-permute-start | bytes 24584 | tf_op jit(solution)/shard_map/ppermute | solution.py:387
  84.9 1.6 %collective-permute-done.30 = f32[16,128]{1,0:T(8,128)S(1)} collective-permute-done((f32[16,128]{1,0:T(8,128)S(1)}, f32[16,128]{1,0:T(8,128)S(1)}, u32[]{:S(2)}, u32[]{:S(2)}) %collective-permute-start.30) | collective-permute-done | bytes 8224 | tf_op jit(solution)/shard_map/ppermute | solution.py:387
  86.5 1.7 %collective-permute-start.31 = (f32[16,128]{1,0:T(8,128)S(1)}, f32[16,128]{1,0:T(8,128)S(1)}, u32[]{:S(2)}, u32[]{:S(2)}) collective-permute-start(f32[16,128]{1,0:T(8,128)S(1)} %add.42), channel_id=1, source_target_pairs={{0,8},{1,9},{2,10},{3,11},{4,12},{5,13},{6,14},{7,15},{8,0},{9,1},... | collective-permute-start | bytes 24584 | tf_op jit(solution)/shard_map/ppermute | solution.py:387
  88.5 1.9 %collective-permute-start.22 = (bf16[128,512]{1,0:T(8,128)(2,1)S(1)}, bf16[128,512]{1,0:T(8,128)(2,1)S(1)}, u32[]{:S(2)}, u32[]{:S(2)}) collective-permute-start(bf16[128,512]{1,0:T(8,128)(2,1)S(1)} %get-tuple-element.98), channel_id=1, source_target_pairs={{0,2},{1,3},{2,0},{3,1},{4,6},{5,7},{6,4},{7,5},{8,10},{9,11},{10,... | collective-permute-start | bytes 393224 | tf_op jit(solution)/shard_map/ppermute | solution.py:387
  90.3 0.7 collective-permute-done.31
  91.1 0.7 collective-permute-start.26
  91.8 2.8 %collective-permute-done.23.refs_5_ = bf16[128,512]{1,0:T(8,128)(2,1)S(1)} collective-permute-done((bf16[128,512]{1,0:T(8,128)(2,1)S(1)}, bf16[128,512]{1,0:T(8,128)(2,1)S(1)}, u32[]{:S(2)}, u32[]{:S(2)}) %collective-permute-start.23) | collective-permute-done | bytes 131104 | tf_op jit(solution)/shard_map/ppermute | solution.py:387
  94.6 1.3 %collective-permute-start.25 = (bf16[128,512]{1,0:T(8,128)(2,1)S(1)}, bf16[128,512]{1,0:T(8,128)(2,1)S(1)}, u32[]{:S(2)}, u32[]{:S(2)}) collective-permute-start(bf16[128,512]{1,0:T(8,128)(2,1)S(1)} %get-tuple-element.101), channel_id=1, source_target_pairs={{0,3},{1,2},{2,1},{3,0},{4,7},{5,6},{6,5},{7,4},{8,11},{9,10},{10,... | collective-permute-start | bytes 393224 | tf_op jit(solution)/shard_map/ppermute | solution.py:387
  95.9 4.3 %collective-permute-done.22.refs_4_ = bf16[128,512]{1,0:T(8,128)(2,1)S(1)} collective-permute-done((bf16[128,512]{1,0:T(8,128)(2,1)S(1)}, bf16[128,512]{1,0:T(8,128)(2,1)S(1)}, u32[]{:S(2)}, u32[]{:S(2)}) %collective-permute-start.22) | collective-permute-done | bytes 131104 | tf_op jit(solution)/shard_map/ppermute | solution.py:387
  100.2 1.3 %collective-permute-start.24 = (bf16[128,512]{1,0:T(8,128)(2,1)S(1)}, bf16[128,512]{1,0:T(8,128)(2,1)S(1)}, u32[]{:S(2)}, u32[]{:S(2)}) collective-permute-start(bf16[128,512]{1,0:T(8,128)(2,1)S(1)} %get-tuple-element.100), channel_id=1, source_target_pairs={{0,3},{1,2},{2,1},{3,0},{4,7},{5,6},{6,5},{7,4},{8,11},{9,10},{10,... | collective-permute-start | bytes 393224 | tf_op jit(solution)/shard_map/ppermute | solution.py:387
  101.5 0.7 fusion.3
  102.2 3.6 %collective-permute-done.21.refs_3_ = bf16[128,512]{1,0:T(8,128)(2,1)S(1)} collective-permute-done((bf16[128,512]{1,0:T(8,128)(2,1)S(1)}, bf16[128,512]{1,0:T(8,128)(2,1)S(1)}, u32[]{:S(2)}, u32[]{:S(2)}) %collective-permute-start.21) | collective-permute-done | bytes 131104 | tf_op jit(solution)/shard_map/ppermute | solution.py:387
  105.8 5.3 %collective-permute-done.20.refs_2_ = bf16[128,512]{1,0:T(8,128)(2,1)S(1)} collective-permute-done((bf16[128,512]{1,0:T(8,128)(2,1)S(1)}, bf16[128,512]{1,0:T(8,128)(2,1)S(1)}, u32[]{:S(2)}, u32[]{:S(2)}) %collective-permute-start.20) | collective-permute-done | bytes 131104 | tf_op jit(solution)/shard_map/ppermute | solution.py:387
  111.1 3.1 %norm.1 = bf16[128,8192]{1,0:T(8,128)(2,1)} custom-call(s32[1]{0:T(128)} %bitcast.rank_ref, bf16[128,2048]{1,0:T(8,128)(2,1)S(1)} %get-tuple-element.94.refs_0_, bf16[128,2048]{1,0:T(8,128)(2,1)S(1)} %collective-permute-done.19.refs_1_, bf16[128,512]{1,0:T(8,128)(2,1)S(1)} %collective-permute-done.20.refs_2_, ...), custom_call_target="tpu_custom_call" | custom-call | flops 40000000 | bytes 120000 | tf_op jit(solution)/shard_map/norm/pallas_call | solution.py:32
  (82 shorter events, 6.0 us)
Async XLA Ops:
  0.6 25.6 %copy-start.17 = (s32[2048]{0:T(1024)S(1)}, s32[2048]{0:T(1024)}, u32[]{:S(2)}) copy-start(s32[2048]{0:T(1024)} %param.15) | copy-start | bytes 24580
  0.6 40.8 %copy-start.20 = (f32[128]{0:T(128)S(1)}, f32[128]{0:T(128)}, u32[]{:S(2)}) copy-start(f32[128]{0:T(128)} %param.18) | copy-start | bytes 1540
  0.7 40.8 %copy-start.19 = (f32[128]{0:T(128)S(1)}, f32[128]{0:T(128)}, u32[]{:S(2)}) copy-start(f32[128]{0:T(128)} %param.19) | copy-start | bytes 1540
  0.7 40.8 %copy-start.18 = (f32[128]{0:T(128)S(1)}, f32[128]{0:T(128)}, u32[]{:S(2)}) copy-start(f32[128]{0:T(128)} %param.20) | copy-start | bytes 1540
  0.7 1.6 %copy-start = (bf16[128,8192]{1,0:T(8,128)(2,1)S(1)}, bf16[128,8192]{1,0:T(8,128)(2,1)}, u32[]{:S(2)}) copy-start(bf16[128,8192]{1,0:T(8,128)(2,1)} %refs_0_.7) | copy-start | bytes 6291460
  2.3 1.0 copy-start.3
  3.3 0.8 copy-start.8
  4.1 22.0 %copy-start.15 = (f32[4,10240]{1,0:T(4,128)S(1)}, f32[4,10240]{1,0:T(4,128)}, u32[]{:S(2)}) copy-start(f32[4,10240]{1,0:T(4,128)} %param.16) | copy-start | bytes 491524
  4.1 22.0 %copy-start.16 = (f32[10240]{0:T(1024)S(1)}, f32[10240]{0:T(1024)}, u32[]{:S(2)}) copy-start(f32[10240]{0:T(1024)} %param.17) | copy-start | bytes 122884
  5.8 0.7 copy-start.4
  7.1 0.7 copy-start.11
  9.7 15.7 %collective-permute-start.16 = (bf16[128,512]{1,0:T(8,128)(2,1)S(1)}, bf16[128,512]{1,0:T(8,128)(2,1)S(1)}, u32[]{:S(2)}, u32[]{:S(2)}) collective-permute-start(bf16[128,512]{1,0:T(8,128)(2,1)S(1)} %get-tuple-element.83), channel_id=1, source_target_pairs={{0,2},{1,3},{2,0},{3,1},{4,6},{5,7},{6,4},{7,5},{8,10},{9,11},{10,... | collective-permute-start | bytes 393224 | tf_op jit(solution)/shard_map/ppermute | solution.py:387
  12.7 2.7 %collective-permute-start.3 = (bf16[16,2560]{1,0:T(8,128)(2,1)S(1)}, bf16[16,2560]{1,0:T(8,128)(2,1)S(1)}, u32[]{:S(2)}, u32[]{:S(2)}) collective-permute-start(bf16[16,2560]{1,0:T(8,128)(2,1)S(1)} %get-tuple-element.58), channel_id=1, source_target_pairs={{3,4},{7,8},{11,12},{19,20},{23,24},{27,28}} | collective-permute-start | bytes 245768 | tf_op jit(solution)/shard_map/ppermute | solution.py:422
  13.4 2.1 %collective-permute-start.4 = (bf16[16,2560]{1,0:T(8,128)(2,1)S(1)}, bf16[16,2560]{1,0:T(8,128)(2,1)S(1)}, u32[]{:S(2)}, u32[]{:S(2)}) collective-permute-start(bf16[16,2560]{1,0:T(8,128)(2,1)S(1)} %get-tuple-element.59), channel_id=1, source_target_pairs={{3,5},{7,9},{11,13},{19,21},{23,25},{27,29}} | collective-permute-start | bytes 245768 | tf_op jit(solution)/shard_map/ppermute | solution.py:422
  14.0 9.6 %collective-permute-start.5 = (bf16[16,2560]{1,0:T(8,128)(2,1)S(1)}, bf16[16,2560]{1,0:T(8,128)(2,1)S(1)}, u32[]{:S(2)}, u32[]{:S(2)}) collective-permute-start(bf16[16,2560]{1,0:T(8,128)(2,1)S(1)} %get-tuple-element.60), channel_id=1, source_target_pairs={{3,6},{7,10},{11,14},{19,22},{23,26},{27,30}} | collective-permute-start | bytes 245768 | tf_op jit(solution)/shard_map/ppermute | solution.py:422
  14.7 9.0 %collective-permute-start.6 = (bf16[16,2560]{1,0:T(8,128)(2,1)S(1)}, bf16[16,2560]{1,0:T(8,128)(2,1)S(1)}, u32[]{:S(2)}, u32[]{:S(2)}) collective-permute-start(bf16[16,2560]{1,0:T(8,128)(2,1)S(1)} %get-tuple-element.61), channel_id=1, source_target_pairs={{3,7},{7,11},{11,15},{19,23},{23,27},{27,31}} | collective-permute-start | bytes 245768 | tf_op jit(solution)/shard_map/ppermute | solution.py:422
  15.4 24.5 %collective-permute-start = (bf16[128,2688]{1,0:T(8,128)(2,1)}, bf16[128,2688]{1,0:T(8,128)(2,1)S(1)}, u32[]{:S(2)}, u32[]{:S(2)}) collective-permute-start(bf16[128,2688]{1,0:T(8,128)(2,1)} %get-tuple-element.55), channel_id=1, source_target_pairs={{0,1},{1,0},{2,3},{3,2},{4,5},{5,4},{6,7},{7,6},{8,9},{9,8},{10,11... | collective-permute-start | bytes 2064392 | tf_op jit(solution)/shard_map/ppermute | solution.py:387
  15.5 24.1 %collective-permute-start.7 = (bf16[128,640]{1,0:T(8,128)(2,1)}, bf16[128,640]{1,0:T(8,128)(2,1)}, u32[]{:S(2)}, u32[]{:S(2)}) collective-permute-start(bf16[128,640]{1,0:T(8,128)(2,1)} %get-tuple-element.63), channel_id=1, source_target_pairs={{0,2},{1,3},{2,0},{3,1},{4,6},{5,7},{6,4},{7,5},{8,10},{9,11},{10,... | collective-permute-start | bytes 491528 | tf_op jit(solution)/shard_map/ppermute | solution.py:387
  23.7 15.9 %collective-permute-start.8 = (bf16[128,640]{1,0:T(8,128)(2,1)}, bf16[128,640]{1,0:T(8,128)(2,1)}, u32[]{:S(2)}, u32[]{:S(2)}) collective-permute-start(bf16[128,640]{1,0:T(8,128)(2,1)} %get-tuple-element.64), channel_id=1, source_target_pairs={{0,3},{1,2},{2,1},{3,0},{4,7},{5,6},{6,5},{7,4},{8,11},{9,10},{10,... | collective-permute-start | bytes 491528 | tf_op jit(solution)/shard_map/ppermute | solution.py:387
  23.7 11.2 %collective-permute-start.17 = (bf16[128,512]{1,0:T(8,128)(2,1)}, bf16[128,512]{1,0:T(8,128)(2,1)}, u32[]{:S(2)}, u32[]{:S(2)}) collective-permute-start(bf16[128,512]{1,0:T(8,128)(2,1)} %get-tuple-element.84), channel_id=1, source_target_pairs={{0,3},{1,2},{2,1},{3,0},{4,7},{5,6},{6,5},{7,4},{8,11},{9,10},{10,... | collective-permute-start | bytes 393224 | tf_op jit(solution)/shard_map/ppermute | solution.py:387
  26.1 11.5 %collective-permute-start.13 = (bf16[128,512]{1,0:T(8,128)(2,1)}, bf16[128,512]{1,0:T(8,128)(2,1)}, u32[]{:S(2)}, u32[]{:S(2)}) collective-permute-start(bf16[128,512]{1,0:T(8,128)(2,1)} %get-tuple-element.78), channel_id=1, source_target_pairs={{0,2},{1,3},{2,0},{3,1},{4,6},{5,7},{6,4},{7,5},{8,10},{9,11},{10,... | collective-permute-start | bytes 393224 | tf_op jit(solution)/shard_map/ppermute | solution.py:387
  26.2 19.5 %copy-start.1 = (bf16[128,8192]{1,0:T(8,128)(2,1)S(1)}, bf16[128,8192]{1,0:T(8,128)(2,1)}, u32[]{:S(2)}) copy-start(bf16[128,8192]{1,0:T(8,128)(2,1)} %refs_0_.7) | copy-start | bytes 6291460
  34.9 14.0 %collective-permute-start.14 = (bf16[128,512]{1,0:T(8,128)(2,1)}, bf16[128,512]{1,0:T(8,128)(2,1)S(1)}, u32[]{:S(2)}, u32[]{:S(2)}) collective-permute-start(bf16[128,512]{1,0:T(8,128)(2,1)} %copy-done.14), channel_id=1, source_target_pairs={{0,3},{1,2},{2,1},{3,0},{4,7},{5,6},{6,5},{7,4},{8,11},{9,10},{10,... | collective-permute-start | bytes 393224 | tf_op jit(solution)/shard_map/ppermute | solution.py:387
  37.5 17.8 %collective-permute-start.10 = (bf16[128,512]{1,0:T(8,128)(2,1)}, bf16[128,512]{1,0:T(8,128)(2,1)S(1)}, u32[]{:S(2)}, u32[]{:S(2)}) collective-permute-start(bf16[128,512]{1,0:T(8,128)(2,1)} %copy-done.13), channel_id=1, source_target_pairs={{0,2},{1,3},{2,0},{3,1},{4,6},{5,7},{6,4},{7,5},{8,10},{9,11},{10,... | collective-permute-start | bytes 393224 | tf_op jit(solution)/shard_map/ppermute | solution.py:387
  39.6 18.0 %collective-permute-start.11 = (bf16[128,512]{1,0:T(8,128)(2,1)}, bf16[128,512]{1,0:T(8,128)(2,1)S(1)}, u32[]{:S(2)}, u32[]{:S(2)}) collective-permute-start(bf16[128,512]{1,0:T(8,128)(2,1)} %copy-done.12), channel_id=1, source_target_pairs={{0,3},{1,2},{2,1},{3,0},{4,7},{5,6},{6,5},{7,4},{8,11},{9,10},{10,... | collective-permute-start | bytes 393224 | tf_op jit(solution)/shard_map/ppermute | solution.py:387
  39.6 23.0 %collective-permute-start.1 = (bf16[128,512]{1,0:T(8,128)(2,1)}, bf16[128,512]{1,0:T(8,128)(2,1)S(1)}, u32[]{:S(2)}, u32[]{:S(2)}) collective-permute-start(bf16[128,512]{1,0:T(8,128)(2,1)} %copy-done.11), channel_id=1, source_target_pairs={{0,2},{1,3},{2,0},{3,1},{4,6},{5,7},{6,4},{7,5},{8,10},{9,11},{10,... | collective-permute-start | bytes 393224 | tf_op jit(solution)/shard_map/ppermute | solution.py:387
  39.9 22.7 %collective-permute-start.2 = (bf16[128,512]{1,0:T(8,128)(2,1)}, bf16[128,512]{1,0:T(8,128)(2,1)S(1)}, u32[]{:S(2)}, u32[]{:S(2)}) collective-permute-start(bf16[128,512]{1,0:T(8,128)(2,1)} %copy-done.10), channel_id=1, source_target_pairs={{0,3},{1,2},{2,1},{3,0},{4,7},{5,6},{6,5},{7,4},{8,11},{9,10},{10,... | collective-permute-start | bytes 393224 | tf_op jit(solution)/shard_map/ppermute | solution.py:387
  41.5 0.9 copy-start.5
  42.4 3.3 %copy-start.7 = (bf16[128,512]{1,0:T(8,128)(2,1)S(1)}, bf16[128,512]{1,0:T(8,128)(2,1)}, u32[]{:S(2)}) copy-start(bf16[128,512]{1,0:T(8,128)(2,1)} %copy-done.6) | copy-start | bytes 393220
  48.9 18.3 %collective-permute-start.18 = (bf16[256,512]{1,0:T(8,128)(2,1)S(1)}, bf16[256,512]{1,0:T(8,128)(2,1)S(1)}, u32[]{:S(2)}, u32[]{:S(2)}) collective-permute-start(bf16[256,512]{1,0:T(8,128)(2,1)S(1)} %get-tuple-element.85), channel_id=1, source_target_pairs={{0,4},{1,5},{2,6},{3,7},{4,8},{5,9},{6,10},{7,11},{8,12},{9,13},{1... | collective-permute-start | bytes 786440 | tf_op jit(solution)/shard_map/ppermute | solution.py:388
  55.4 13.2 %collective-permute-start.15 = (bf16[256,512]{1,0:T(8,128)(2,1)S(1)}, bf16[256,512]{1,0:T(8,128)(2,1)S(1)}, u32[]{:S(2)}, u32[]{:S(2)}) collective-permute-start(bf16[256,512]{1,0:T(8,128)(2,1)S(1)} %get-tuple-element.80), channel_id=1, source_target_pairs={{0,4},{1,5},{2,6},{3,7},{4,8},{5,9},{6,10},{7,11},{8,12},{9,13},{1... | collective-permute-start | bytes 786440 | tf_op jit(solution)/shard_map/ppermute | solution.py:388
  60.0 10.2 %collective-permute-start.12 = (bf16[256,512]{1,0:T(8,128)(2,1)S(1)}, bf16[256,512]{1,0:T(8,128)(2,1)S(1)}, u32[]{:S(2)}, u32[]{:S(2)}) collective-permute-start(bf16[256,512]{1,0:T(8,128)(2,1)S(1)} %get-tuple-element.75), channel_id=1, source_target_pairs={{0,4},{1,5},{2,6},{3,7},{4,8},{5,9},{6,10},{7,11},{8,12},{9,13},{1... | collective-permute-start | bytes 786440 | tf_op jit(solution)/shard_map/ppermute | solution.py:388
  65.0 10.3 %collective-permute-start.9 = (bf16[256,512]{1,0:T(8,128)(2,1)S(1)}, bf16[256,512]{1,0:T(8,128)(2,1)S(1)}, u32[]{:S(2)}, u32[]{:S(2)}) collective-permute-start(bf16[256,512]{1,0:T(8,128)(2,1)S(1)} %get-tuple-element.69), channel_id=1, source_target_pairs={{0,4},{1,5},{2,6},{3,7},{4,8},{5,9},{6,10},{7,11},{8,12},{9,13},{1... | collective-permute-start | bytes 786440 | tf_op jit(solution)/shard_map/ppermute | solution.py:388
  71.7 39.4 %copy-start.2 = (bf16[128,8192]{1,0:T(8,128)(2,1)S(1)}, bf16[128,8192]{1,0:T(8,128)(2,1)}, u32[]{:S(2)}) copy-start(bf16[128,8192]{1,0:T(8,128)(2,1)} %refs_10_.1) | copy-start | bytes 6291460
  71.7 39.5 %copy-start.9 = (f32[8192]{0:T(1024)S(1)}, f32[8192]{0:T(1024)}, u32[]{:S(2)}) copy-start(f32[8192]{0:T(1024)} %param.21) | copy-start | bytes 98308
  76.8 34.3 %collective-permute-start.19 = (bf16[128,2048]{1,0:T(8,128)(2,1)S(1)}, bf16[128,2048]{1,0:T(8,128)(2,1)S(1)}, u32[]{:S(2)}, u32[]{:S(2)}) collective-permute-start(bf16[128,2048]{1,0:T(8,128)(2,1)S(1)} %get-tuple-element.95), channel_id=1, source_target_pairs={{0,1},{1,0},{2,3},{3,2},{4,5},{5,4},{6,7},{7,6},{8,9},{9,8},{10,11... | collective-permute-start | bytes 1572872 | tf_op jit(solution)/shard_map/ppermute | solution.py:387
  76.8 1.9 %collective-permute-start.28 = (f32[16,128]{1,0:T(8,128)S(1)}, f32[16,128]{1,0:T(8,128)S(1)}, u32[]{:S(2)}, u32[]{:S(2)}) collective-permute-start(f32[16,128]{1,0:T(8,128)S(1)} %add_add_fusion), channel_id=1, source_target_pairs={{0,1},{1,0},{2,3},{3,2},{4,5},{5,4},{6,7},{7,6},{8,9},{9,8},{10,11... | collective-permute-start | bytes 24584 | tf_op jit(solution)/shard_map/ppermute | solution.py:387
  78.8 3.7 %collective-permute-start.29 = (f32[16,128]{1,0:T(8,128)S(1)}, f32[16,128]{1,0:T(8,128)S(1)}, u32[]{:S(2)}, u32[]{:S(2)}) collective-permute-start(f32[16,128]{1,0:T(8,128)S(1)} %add.40), channel_id=1, source_target_pairs={{0,2},{1,3},{2,0},{3,1},{4,6},{5,7},{6,4},{7,5},{8,10},{9,11},{10,... | collective-permute-start | bytes 24584 | tf_op jit(solution)/shard_map/ppermute | solution.py:387
  82.4 4.1 %collective-permute-start.30 = (f32[16,128]{1,0:T(8,128)S(1)}, f32[16,128]{1,0:T(8,128)S(1)}, u32[]{:S(2)}, u32[]{:S(2)}) collective-permute-start(f32[16,128]{1,0:T(8,128)S(1)} %add.41), channel_id=1, source_target_pairs={{0,4},{1,5},{2,6},{3,7},{4,0},{5,1},{6,2},{7,3},{8,12},{9,13},{10,... | collective-permute-start | bytes 24584 | tf_op jit(solution)/shard_map/ppermute | solution.py:387
  86.5 4.5 %collective-permute-start.31 = (f32[16,128]{1,0:T(8,128)S(1)}, f32[16,128]{1,0:T(8,128)S(1)}, u32[]{:S(2)}, u32[]{:S(2)}) collective-permute-start(f32[16,128]{1,0:T(8,128)S(1)} %add.42), channel_id=1, source_target_pairs={{0,8},{1,9},{2,10},{3,11},{4,12},{5,13},{6,14},{7,15},{8,0},{9,1},... | collective-permute-start | bytes 24584 | tf_op jit(solution)/shard_map/ppermute | solution.py:387
  88.3 6.3 %collective-permute-start.23 = (bf16[128,512]{1,0:T(8,128)(2,1)S(1)}, bf16[128,512]{1,0:T(8,128)(2,1)S(1)}, u32[]{:S(2)}, u32[]{:S(2)}) collective-permute-start(bf16[128,512]{1,0:T(8,128)(2,1)S(1)} %get-tuple-element.99), channel_id=1, source_target_pairs={{0,2},{1,3},{2,0},{3,1},{4,6},{5,7},{6,4},{7,5},{8,10},{9,11},{10,... | collective-permute-start | bytes 393224 | tf_op jit(solution)/shard_map/ppermute | solution.py:387
  88.5 6.1 %collective-permute-start.27 = (bf16[128,512]{1,0:T(8,128)(2,1)S(1)}, bf16[128,512]{1,0:T(8,128)(2,1)S(1)}, u32[]{:S(2)}, u32[]{:S(2)}) collective-permute-start(bf16[128,512]{1,0:T(8,128)(2,1)S(1)} %get-tuple-element.103), channel_id=1, source_target_pairs={{0,3},{1,2},{2,1},{3,0},{4,7},{5,6},{6,5},{7,4},{8,11},{9,10},{10,... | collective-permute-start | bytes 393224 | tf_op jit(solution)/shard_map/ppermute | solution.py:387
  88.5 11.7 %collective-permute-start.22 = (bf16[128,512]{1,0:T(8,128)(2,1)S(1)}, bf16[128,512]{1,0:T(8,128)(2,1)S(1)}, u32[]{:S(2)}, u32[]{:S(2)}) collective-permute-start(bf16[128,512]{1,0:T(8,128)(2,1)S(1)} %get-tuple-element.98), channel_id=1, source_target_pairs={{0,2},{1,3},{2,0},{3,1},{4,6},{5,7},{6,4},{7,5},{8,10},{9,11},{10,... | collective-permute-start | bytes 393224 | tf_op jit(solution)/shard_map/ppermute | solution.py:387
  91.1 9.1 %collective-permute-start.26 = (bf16[128,512]{1,0:T(8,128)(2,1)S(1)}, bf16[128,512]{1,0:T(8,128)(2,1)S(1)}, u32[]{:S(2)}, u32[]{:S(2)}) collective-permute-start(bf16[128,512]{1,0:T(8,128)(2,1)S(1)} %get-tuple-element.102), channel_id=1, source_target_pairs={{0,3},{1,2},{2,1},{3,0},{4,7},{5,6},{6,5},{7,4},{8,11},{9,10},{10,... | collective-permute-start | bytes 393224 | tf_op jit(solution)/shard_map/ppermute | solution.py:387
  94.6 11.2 %collective-permute-start.21 = (bf16[128,512]{1,0:T(8,128)(2,1)S(1)}, bf16[128,512]{1,0:T(8,128)(2,1)S(1)}, u32[]{:S(2)}, u32[]{:S(2)}) collective-permute-start(bf16[128,512]{1,0:T(8,128)(2,1)S(1)} %get-tuple-element.97), channel_id=1, source_target_pairs={{0,2},{1,3},{2,0},{3,1},{4,6},{5,7},{6,4},{7,5},{8,10},{9,11},{10,... | collective-permute-start | bytes 393224 | tf_op jit(solution)/shard_map/ppermute | solution.py:387
  94.6 11.2 %collective-permute-start.25 = (bf16[128,512]{1,0:T(8,128)(2,1)S(1)}, bf16[128,512]{1,0:T(8,128)(2,1)S(1)}, u32[]{:S(2)}, u32[]{:S(2)}) collective-permute-start(bf16[128,512]{1,0:T(8,128)(2,1)S(1)} %get-tuple-element.101), channel_id=1, source_target_pairs={{0,3},{1,2},{2,1},{3,0},{4,7},{5,6},{6,5},{7,4},{8,11},{9,10},{10,... | collective-permute-start | bytes 393224 | tf_op jit(solution)/shard_map/ppermute | solution.py:387
  100.2 10.9 %collective-permute-start.20 = (bf16[128,512]{1,0:T(8,128)(2,1)S(1)}, bf16[128,512]{1,0:T(8,128)(2,1)S(1)}, u32[]{:S(2)}, u32[]{:S(2)}) collective-permute-start(bf16[128,512]{1,0:T(8,128)(2,1)S(1)} %get-tuple-element.96), channel_id=1, source_target_pairs={{0,2},{1,3},{2,0},{3,1},{4,6},{5,7},{6,4},{7,5},{8,10},{9,11},{10,... | collective-permute-start | bytes 393224 | tf_op jit(solution)/shard_map/ppermute | solution.py:387
  100.2 10.9 %collective-permute-start.24 = (bf16[128,512]{1,0:T(8,128)(2,1)S(1)}, bf16[128,512]{1,0:T(8,128)(2,1)S(1)}, u32[]{:S(2)}, u32[]{:S(2)}) collective-permute-start(bf16[128,512]{1,0:T(8,128)(2,1)S(1)} %get-tuple-element.100), channel_id=1, source_target_pairs={{0,3},{1,2},{2,1},{3,0},{4,7},{5,6},{6,5},{7,4},{8,11},{9,10},{10,... | collective-permute-start | bytes 393224 | tf_op jit(solution)/shard_map/ppermute | solution.py:387
  (5 other events, 3.3 us)

commit v2 on v1

v2 whole, which is shorter than its diff:
```python
import functools

import jax
import jax.numpy as jnp
from jax import lax
from jax.experimental import pallas as pl
from jax.experimental.pallas import tpu as pltpu
from jax.sharding import PartitionSpec as P

STATE = 256
SPAN = 512
DOCS = 16
HALO = 16
PARTS = (2, 3, 3)
LANES = 128
VMEM_LIMIT = 20 * 1024 * 1024
VMEM_MOST = 60 * 1024 * 1024

F32 = jnp.float32
BF16 = jnp.bfloat16
ANY = pl.BlockSpec(memory_space=pl.ANY)


def iota(shape, dim):
    return lax.broadcasted_iota(jnp.int32, shape, dim)


def whole(shape):
    return pl.BlockSpec(shape, lambda i, pref: (0,) * len(shape))


def call(kernel, rank, inputs, in_specs, out_shapes, out_specs, scratch, name, grid=(1,), cost=None, aliases={}, limit=VMEM_LIMIT):
    return pl.pallas_call(
        kernel,
        grid_spec=pltpu.PrefetchScalarGridSpec(
            num_scalar_prefetch=1,
            grid=grid,
            in_specs=in_specs,
            out_specs=out_specs,
            scratch_shapes=scratch,
        ),
        out_shape=out_shapes,
        compiler_params=pltpu.CompilerParams(vmem_limit_bytes=limit),
        cost_estimate=cost,
        input_output_aliases=aliases,
        name=name,
    )(rank, *inputs)


def cost(us):
    return pl.CostEstimate(flops=int(us * 1e9), bytes_accessed=int(us * 3e6), transcendentals=0)


def pack_kernel(team, chunks, gw, rank_ref, x_ref, bc_ref, dt_ref, *refs):
    xv_ref, tail_ref, bcv_ref, dtv_ref, in_sems, out_sems = refs[-6:]
    outs = list(refs[:-6])
    rank = rank_ref[0]
    rows = x_ref.shape[0]
    half = bc_ref.shape[1] // 2
    fold = gw * HALO // rows

    def fetch(src, dst, sem):
        made = pltpu.make_async_copy(src, dst, in_sems.at[sem])
        made.start()
        return made

    fetches = [fetch(bc_ref, bcv_ref, 0), fetch(dt_ref, dtv_ref, 1)]
    x_fetches = {}
    for k in (2, 3, 1):
        at = pl.multiple_of((rank ^ k) * gw, LANES)
        x_fetches[k] = fetch(x_ref.at[:, pl.ds(at, gw)], xv_ref.at[k - 1], 1 + k)
    at = pl.multiple_of(rank * gw, LANES)
    last = pl.ds(rows - HALO, HALO)
    tail_fetch = fetch(x_ref.at[last, pl.ds(at, gw)], tail_ref, 1 + team)

    copies = []

    def copy(src, dst):
        made = pltpu.make_async_copy(src, dst, out_sems.at[len(copies)])
        made.start()
        copies.append(made)

    for made in fetches:
        made.wait()
    for k in (2, 3, 1):
        out = outs.pop(0)
        at = pl.multiple_of((rank ^ k) * STATE, STATE)
        copy(bcv_ref.at[:, pl.ds(at, STATE)], out.at[:, 0:STATE])
        at = pl.multiple_of(half + (rank ^ k) * STATE, STATE)
        copy(bcv_ref.at[:, pl.ds(at, STATE)], out.at[:, STATE : 2 * STATE])
        copy(dtv_ref, out.at[:, 2 * STATE : 2 * STATE + LANES])
        x_fetches[k].wait()
        first = 2 * STATE + LANES
        for j in range(rows // HALO):
            tail = xv_ref.at[k - 1, pl.ds(rows - HALO, HALO), pl.ds(j * fold, fold)]
            copy(tail, out.at[pl.ds(j * HALO, HALO), first : first + fold])
        size = gw if k == 1 else chunks[0]
        copy(xv_ref.at[k - 1, :, pl.ds(0, size)], out.at[:, first + fold : first + fold + size])
    done = chunks[0]
    for size in chunks[1:]:
        for k in (2, 3):
            copy(xv_ref.at[k - 1, :, pl.ds(done, size)], outs.pop(0))
        done += size
    out = outs.pop(0)
    b_at = pl.multiple_of(rank * STATE, LANES)
    c_at = pl.multiple_of(half + rank * STATE, LANES)
    copy(bcv_ref.at[last, pl.ds(b_at, STATE)], out.at[:, gw : gw + STATE])
    copy(bcv_ref.at[last, pl.ds(c_at, STATE)], out.at[:, gw + STATE : gw + 2 * STATE])
    tail_fetch.wait()
    copy(tail_ref, out.at[:, 0:gw])
    for made in copies:
        made.wait()


def relay_kernel(team, gw, rank_ref, tail_ref, *refs):
    got = refs[: team - 1]
    out_ref, sems = refs[team - 1 :]
    rank = rank_ref[0]
    rows = got[0].shape[0]
    fold = gw * HALO // rows
    tail = pl.ds(rows - HALO, HALO)

    def copy_all(pairs):
        copies = []
        for i, (src, dst) in enumerate(pairs):
            made = pltpu.make_async_copy(src, dst, sems.at[i])
            made.start()
            copies.append(made)
        for made in copies:
            made.wait()

    @pl.when(rank == team - 1)
    def _():
        out_ref[...] = tail_ref[...]

    for k in range(1, team):

        @pl.when(rank ^ k == team - 1)
        def _():
            first = 2 * STATE + LANES
            pairs = [(got[k - 1].at[tail, 0 : 2 * STATE], out_ref.at[:, gw : gw + 2 * STATE])]
            for j in range(rows // HALO):
                src = got[k - 1].at[pl.ds(j * HALO, HALO), first : first + fold]
                pairs.append((src, out_ref.at[:, j * fold : (j + 1) * fold]))
            copy_all(pairs)


def column_of(row):
    return jnp.transpose(jnp.broadcast_to(row, (LANES, row.shape[1])))


def shift_kernel(taps, rank_ref, docs_ref, shift_ref):
    tiles = shift_ref.shape[0]
    for a in range(tiles):
        near = docs_ref[0:1, a * LANES : (a + 2) * LANES]
        own = column_of(docs_ref[0:1, (a + 1) * LANES : (a + 2) * LANES])
        same = jnp.concatenate([own, own], axis=1) == near
        row, col = iota((LANES, 2 * LANES), 0), iota((LANES, 2 * LANES), 1)
        for back in range(1, taps):
            hit = same & (col == row + (LANES - back))
            shift_ref[a, (back - 1) * LANES : back * LANES, :] = jnp.where(hit, 1.0, 0.0).astype(BF16)


def gather_rows(rank, sources, raw_ref, halo, sems):
    copies = []
    for k, parts in enumerate(sources):
        at = pl.multiple_of(LANES + (rank ^ k) * LANES, LANES)
        for source, first in parts:
            dst = raw_ref.at[pl.ds(at, LANES), first : first + source.shape[1]]
            made = pltpu.make_async_copy(source, dst, sems.at[len(copies)])
            made.start()
            copies.append(made)
    width = halo.shape[1]
    raw_ref[0 : LANES - HALO, 0:width] = jnp.zeros((LANES - HALO, width), BF16)
    raw_ref[LANES - HALO : LANES, 0:width] = halo
    for made in copies:
        made.wait()


def silu(value):
    half = 0.5 * value
    return half + half * jnp.tanh(half)


def conv_tile(raw, shift, taps, bias):
    count = len(taps)
    moved = jnp.dot(shift, raw, preferred_element_type=F32)
    total = raw[LANES:].astype(F32) * taps[count - 1] + bias
    for back in range(1, count):
        total = total + moved[(back - 1) * LANES : back * LANES] * taps[count - 1 - back]
    return silu(total).astype(BF16)


def split_hi(value):
    hi = value.astype(BF16).astype(F32)
    return hi, value - hi


def bc_kernel(team, taps, gw, rank_ref, bc_ref, dt_ref, *refs):
    got = refs[: team - 1]
    halo_ref, shift_ref, docs_ref, wb_b_ref, wb_c_ref, heads_ref = refs[team - 1 : team + 5]
    s_ref, bt_ref, cm_ref, uv_ref, row_ref, raw_ref, b_ref, sems = refs[team + 5 :]
    rank = rank_ref[0]
    tiles = SPAN // LANES
    own_heads = LANES // team
    half = bc_ref.shape[1] // 2
    b_at = pl.multiple_of(rank * STATE, LANES)
    c_at = pl.multiple_of(half + rank * STATE, LANES)
    own = [(bc_ref.at[:, pl.ds(b_at, STATE)], 0), (bc_ref.at[:, pl.ds(c_at, STATE)], STATE), (dt_ref, 2 * STATE)]
    others = [[(ref.at[:, 0 : 2 * STATE + LANES], 0)] for ref in got]
    gather_rows(rank, [own] + others, raw_ref, halo_ref[:, gw : gw + 2 * STATE], sems)

    lane = iota((LANES, LANES), 1)
    part = lane // own_heads

    def mine(value):
        near = part[: value.shape[0]]
        moved = pltpu.roll(value, (LANES - rank * own_heads) % LANES, 1)
        kept = jnp.where(near == 0, moved, 0.0)
        total = kept
        for step in range(1, team):
            total = total + pltpu.roll(kept, step * own_heads, 1)
        return total

    heads = mine(heads_ref[...])
    bias_row, skip_row = heads[0:1], heads[2:3]
    decay_row = -jnp.exp(heads[1:2])
    ones = jnp.where(iota((LANES, LANES), 0) >= lane, 1.0, 0.0)

    last_doc = docs_ref[0:1, LANES + SPAN - 1 : LANES + SPAN]
    prev_doc = docs_ref[0:1, LANES - 1 : LANES]
    start = jnp.zeros((1, LANES), F32)
    rows_g, rows_e = [], []
    for a in range(tiles):
        here = slice(a * LANES, (a + 1) * LANES)
        raw = raw_ref[a * LANES : (a + 2) * LANES, :]
        shift = shift_ref[a]
        b_tile = conv_tile(raw[:, 0:STATE], shift, [wb_b_ref[i : i + 1, :] for i in range(taps)], wb_b_ref[taps : taps + 1, :])
        c_tile = conv_tile(raw[:, STATE : 2 * STATE], shift, [wb_c_ref[i : i + 1, :] for i in range(taps)], wb_c_ref[taps : taps + 1, :])
        b_ref[here, :] = b_tile
        own = column_of(docs_ref[0:1, (a + 1) * LANES : (a + 2) * LANES])
        own_two = jnp.concatenate([own, own], axis=1)
        cm_ref[here, :] = jnp.where(own_two == prev_doc, c_tile.astype(F32), 0.0).astype(BF16)
        masked = jnp.where(own_two == last_doc, b_tile.astype(F32), 0.0)
        bt_ref[:, here] = jnp.transpose(masked).astype(BF16)
        for b in range(a + 1):
            there = slice(b * LANES, (b + 1) * LANES)
            scores = lax.dot_general(
                c_tile, b_ref[there, :], (((1,), (1,)), ((), ())), preferred_element_type=F32
            )
            keep = own == docs_ref[0:1, (b + 1) * LANES : (b + 2) * LANES]
            if a == b:
                keep = keep & (iota((LANES, LANES), 0) >= lane)
            s_ref[here, there] = jnp.where(keep, scores, 0.0).astype(BF16)
        raised = mine(raw[LANES:, 2 * STATE : 2 * STATE + LANES].astype(F32)) + bias_row
        step = jnp.maximum(raised, 0.0) + jnp.log1p(jnp.exp(-jnp.abs(raised)))
        cum = jnp.dot(ones, decay_row * step, precision=lax.Precision.HIGHEST, preferred_element_type=F32)
        u_hi, u_lo = split_hi(jnp.exp(cum))
        v_hi, v_lo = split_hi(jnp.exp(-cum) * step)
        packed = jnp.where(part == 0, v_hi, jnp.where(part == 1, v_lo, jnp.where(part == 2, u_hi, u_lo)))
        uv_ref[here, :] = packed.astype(BF16)
        tile_total = cum[LANES - 1 : LANES]
        rows_g.append(jnp.exp(tile_total))
        rows_e.append(jnp.exp(start))
        start = start + tile_total
    passes = jnp.exp(start) * jnp.where(last_doc == prev_doc, 1.0, 0.0)
    every = rows_g + rows_e + [skip_row, passes] + [jnp.zeros((1, LANES), F32)] * 6
    hi, lo = split_hi(jnp.concatenate(every, axis=0))
    near = part[: 16]
    row_ref[...] = jnp.where(near == 0, hi, jnp.where(near == 1, lo, 0.0)).astype(BF16)


def spreader(first, width, hdim, own_heads, upper):
    row, col = iota((LANES, width), 0), iota((LANES, width), 1)
    hit = (row % own_heads) == (first + col // hdim)
    half = (row >= 2 * own_heads) if upper else (row < 2 * own_heads)
    return jnp.where(hit & half, 1.0, 0.0).astype(BF16)


def mix_kernel(team, taps, hdim, gw, start, places, rank_ref, *refs):
    x_ref = refs[0]
    got = refs[1:team]
    halo_ref, shift_ref, wb_ref, s_ref, bt_ref, uv_ref, row_ref = refs[team : team + 7]
    xc_ref, yl_ref, st_ref, raw_ref, xf_ref, xb_ref, sems = refs[-7:]
    rank = rank_ref[0]
    tiles = SPAN // LANES
    width = xc_ref.shape[1]
    own_heads = LANES // team
    first = start // hdim
    cols = slice(start, start + width)
    at = pl.multiple_of(rank * gw + start, LANES)
    sources = [[(x_ref.at[:, pl.ds(at, width)], 0)]]
    for ref, place in zip(got, places):
        sources.append([(ref.at[:, place : place + width], 0)])
    gather_rows(rank, sources, raw_ref, halo_ref[:, cols], sems)
    spread_v = spreader(first, width, hdim, own_heads, False)
    spread_u = spreader(first, width, hdim, own_heads, True)
    rows = jnp.dot(row_ref[...], spread_v, preferred_element_type=F32)
    skip = rows[2 * tiles : 2 * tiles + 1]
    weights = [wb_ref[i : i + 1, cols] for i in range(taps)]
    bias = wb_ref[taps : taps + 1, cols]
    for a in range(tiles):
        here = slice(a * LANES, (a + 1) * LANES)
        xc = conv_tile(raw_ref[a * LANES : (a + 2) * LANES, :], shift_ref[a], weights, bias)
        xc_ref[here, :] = xc
        xf = xc.astype(F32)
        uv = uv_ref[here, :]
        scaled = jnp.dot(uv, spread_v, preferred_element_type=F32) * xf
        xf_ref[here, :] = scaled
        xb_ref[here, :] = scaled.astype(BF16)
        total = jnp.dot(
            s_ref[here, 0 : (a + 1) * LANES], xb_ref[0 : (a + 1) * LANES, :], preferred_element_type=F32
        )
        yl_ref[here, :] = jnp.dot(uv, spread_u, preferred_element_type=F32) * total + skip * xf
        for b in range(a + 1):
            there = slice(b * LANES, (b + 1) * LANES)
            later = xf_ref[there, :] * rows[a : a + 1]
            if a < tiles - 1:
                xf_ref[there, :] = later
            xb_ref[there, :] = later.astype(BF16)
    st_ref[...] = jnp.dot(bt_ref[...], xb_ref[...], preferred_element_type=F32).astype(BF16)


def carry_kernel(team, start, hdim, rank_ref, st_ref, yl_ref, xc_ref, cm_ref, uv_ref, row_ref, docs_ref, *refs):
    own_ref, near_ref, far_ref, across_ref, stat_ref, rows_ref, held_ref, sem = refs[-8:]
    first = start // hdim
    rank = rank_ref[0]
    tiles = SPAN // LANES
    width = xc_ref.shape[1]
    own_heads = LANES // team
    spread_v = spreader(first, width, hdim, own_heads, False)
    spread_u = spreader(first, width, hdim, own_heads, True)
    rows_ref[...] = jnp.dot(row_ref[...], spread_v, preferred_element_type=F32)
    sums = jnp.zeros((DOCS, 3 * LANES), F32)
    for k in (1, 2, 3, 0):
        tile = rank ^ k
        here = pl.ds(pl.multiple_of(tile * LANES, LANES), LANES)
        came = jnp.dot(cm_ref[here, :], st_ref[...], preferred_element_type=F32)
        decay = jnp.dot(uv_ref[here, :], spread_u, preferred_element_type=F32)
        y = yl_ref[here, :] + decay * (came * rows_ref[pl.ds(tiles + tile, 1), :])
        y = y.astype(BF16)
        if k == 1:
            held_ref[...] = y
            near = pltpu.make_async_copy(held_ref, near_ref.at[:, start : start + width], sem)
            near.start()
        else:
            (own_ref, None, far_ref, across_ref)[k][...] = y
        y = y.astype(F32)
        x = xc_ref[here, :].astype(F32)
        parts = []
        for product in (y * x, y * y, x * x):
            part = product[:, 0:LANES]
            for c in range(1, width // LANES):
                part = part + product[:, c * LANES : (c + 1) * LANES]
            parts.append(part)
        docs = docs_ref[0:1, pl.ds(pl.multiple_of((tile + 1) * LANES, LANES), LANES)]
        table = jnp.where(iota((DOCS, LANES), 0).astype(F32) == docs, 1.0, 0.0)
        sums = sums + jnp.dot(
            table, jnp.concatenate(parts, axis=1), precision=lax.Precision.HIGHEST, preferred_element_type=F32
        )
    lane = iota((DOCS, LANES), 1)
    out = jnp.zeros((DOCS, LANES), F32)
    for i in range(3):
        out = jnp.where(lane == i, jnp.sum(sums[:, i * LANES : (i + 1) * LANES], axis=1, keepdims=True), out)
    stat_ref[...] = out
    near.wait()


def sum_kernel(rank_ref, *refs):
    total = refs[0][...]
    for ref in refs[1:-1]:
        total = total + ref[...]
    refs[-1][...] = total


def norm_kernel(blocks, rank_ref, *refs):
    y_count = sum(len(block) for block in blocks)
    z_ref, gain_ref = refs[y_count : y_count + 2]
    out_ref, gated_ref = refs[-2:]
    width = z_ref.shape[1]
    for step, block in enumerate(blocks):

        @pl.when(pl.program_id(0) == step)
        def _():
            part = jnp.zeros((LANES, LANES), F32)
            done = 0
            for at in block:
                y_ref = refs[at]
                size = y_ref.shape[1]
                cols = slice(done, done + size)
                gated = y_ref[...].astype(F32) * silu(z_ref[:, cols].astype(F32))
                gated_ref[:, cols] = gated
                square = gated * gated
                for c in range(size // LANES):
                    part = part + square[:, c * LANES : (c + 1) * LANES]
                done += size
            scale = lax.rsqrt(jnp.sum(part, axis=1, keepdims=True) * (1.0 / width) + 1e-05)
            for c in range(width // (4 * LANES)):
                cols = slice(c * 4 * LANES, (c + 1) * 4 * LANES)
                out_ref[:, cols] = (gated_ref[:, cols] * scale * gain_ref[0:1, cols]).astype(BF16)


def on_device(
    x_stream,
    bc_stream,
    z_stream,
    dt_raw,
    doc_ids,
    conv_weight,
    conv_bias,
    dt_bias,
    a_log,
    skip_d,
    norm_gain,
):
    rows, inner = x_stream.shape
    heads = dt_raw.shape[1]
    hdim = inner // heads
    taps = conv_weight.shape[0]
    members = lax.axis_size("seq")
    team = SPAN // rows
    tiles = SPAN // LANES
    gw = inner // team
    chunks = [gw // 8 * part for part in PARTS]
    me = lax.axis_index("seq")
    rank = jnp.reshape(me % team, (1,)).astype(jnp.int32)
    doc_most = rows * members // 4
    hops = (doc_most - 2) // SPAN + 1

    def swap(array, k):
        return lax.ppermute(array, "seq", [(i, i ^ k) for i in range(members)])

    def onward(array):
        return lax.ppermute(array, "seq", [(i, i + team) for i in range(members - team)])

    shape = jax.ShapeDtypeStruct
    bcd_w = 2 * STATE + LANES
    lead_w = bcd_w + gw * HALO // rows
    widths = [lead_w + chunks[0]] * 2 + [lead_w + gw] + [size for size in chunks[1:] for _ in range(2)]
    halo_shape = (HALO, gw + 2 * STATE)
    packed = call(
        functools.partial(pack_kernel, team, chunks, gw),
        rank,
        (x_stream, bc_stream, dt_raw),
        [ANY] * 3,
        [shape((rows, width), BF16) for width in widths] + [shape(halo_shape, BF16)],
        [ANY] * (len(widths) + 1),
        [
            pltpu.VMEM((team - 1, rows, gw), BF16),
            pltpu.VMEM((HALO, gw), BF16),
            pltpu.VMEM(bc_stream.shape, BF16),
            pltpu.VMEM(dt_raw.shape, BF16),
            pltpu.SemaphoreType.DMA((2 + team,)),
            pltpu.SemaphoreType.DMA((3 * (4 + rows // HALO) + 2 * len(chunks) + 3,)),
        ],
        "pack",
        cost=cost(2),
        limit=VMEM_MOST,
    )
    near = swap(packed[2], 1)
    lead = [near, swap(packed[0], 2), swap(packed[1], 3)]
    got = [lead]
    for q in range(1, len(chunks)):
        got.append([near, swap(packed[1 + 2 * q], 2), swap(packed[2 + 2 * q], 3)])

    ext_docs = jnp.concatenate([jnp.full((LANES,), -1, jnp.int32), doc_ids])
    docs = lax.dynamic_slice_in_dim(ext_docs, (me // team) * SPAN, SPAN + LANES).astype(F32)[None]
    wb = jnp.concatenate([conv_weight, conv_bias[None]], axis=0)
    head_rows = jnp.concatenate(
        [dt_bias[None], a_log[None], skip_d[None], jnp.zeros((5, heads), F32)], axis=0
    )
    shift_shape = (tiles, (taps - 1) * LANES, 2 * LANES)
    shift = call(
        functools.partial(shift_kernel, taps),
        rank,
        (docs,),
        [whole(docs.shape)],
        shape(shift_shape, BF16),
        whole(shift_shape),
        [],
        "shift",
        cost=cost(1.5),
    )
    halo = onward(
        call(
            functools.partial(relay_kernel, team, gw),
            rank,
            (packed[-1], *lead),
            [whole(halo_shape)] + [ANY] * (team - 1),
            shape(halo_shape, BF16),
            whole(halo_shape),
            [pltpu.SemaphoreType.DMA((1 + rows // HALO,))],
            "relay",
            cost=cost(1),
        )
    )

    b_block, c_block = inner // STATE, inner // STATE + team
    scores, b_turned, c_masked, uv, row_pack = call(
        functools.partial(bc_kernel, team, taps, gw),
        rank,
        (bc_stream, dt_raw, *lead, halo, shift, docs, wb, wb, head_rows),
        [ANY] * 2
        + [ANY] * (team - 1)
        + [
            whole(halo_shape),
            whole(shift_shape),
            whole(docs.shape),
            pl.BlockSpec((taps + 1, STATE), lambda i, pref: (0, b_block + pref[0])),
            pl.BlockSpec((taps + 1, STATE), lambda i, pref: (0, c_block + pref[0])),
            whole(head_rows.shape),
        ],
        [
            shape((SPAN, SPAN), BF16),
            shape((STATE, SPAN), BF16),
            shape((SPAN, STATE), BF16),
            shape((SPAN, LANES), BF16),
            shape((16, LANES), BF16),
        ],
        [
            whole((SPAN, SPAN)),
            whole((STATE, SPAN)),
            whole((SPAN, STATE)),
            whole((SPAN, LANES)),
            whole((16, LANES)),
        ],
        [
            pltpu.VMEM((LANES + SPAN, bcd_w), BF16),
            pltpu.VMEM((SPAN, STATE), BF16),
            pltpu.SemaphoreType.DMA((team + 2,)),
        ],
        "bc",
        cost=cost(4),
    )

    def mix(q, after):
        start, size = sum(chunks[:q]), chunks[q]
        far = lead_w if q == 0 else 0
        xc, y_local, fresh = call(
            functools.partial(mix_kernel, team, taps, hdim, gw, start, (lead_w + start, far, far)),
            rank,
            (x_stream, *got[q], halo, shift, wb, scores, b_turned, uv, row_pack, *after),
            [ANY]
            + [ANY] * (team - 1)
            + [
                whole(halo_shape),
                whole(shift_shape),
                pl.BlockSpec((taps + 1, gw), lambda i, pref: (0, pref[0])),
                whole((SPAN, SPAN)),
                whole((STATE, SPAN)),
                whole((SPAN, LANES)),
                whole((16, LANES)),
            ]
            + [ANY] * len(after),
            [shape((SPAN, size), BF16), shape((SPAN, size), F32), shape((STATE, size), BF16)],
            [whole((SPAN, size)), whole((SPAN, size)), whole((STATE, size))],
            [
                pltpu.VMEM((LANES + SPAN, size), BF16),
                pltpu.VMEM((SPAN, size), F32),
                pltpu.VMEM((SPAN, size), BF16),
                pltpu.SemaphoreType.DMA((team,)),
            ],
            "mix",
            cost=cost(4),
        )
        state = onward(fresh)
        if hops > 1:
            first, count, own_heads = start // hdim, size // hdim, heads // team
            part = row_pack[2 * tiles + 1].astype(F32)
            kept = part[first : first + count] + part[own_heads + first : own_heads + first + count]
            kept = jnp.repeat(kept, hdim)[None]
            for _ in range(hops - 1):
                state = onward((fresh.astype(F32) + kept * state.astype(F32)).astype(BF16))
        return state, y_local, xc

    def carry(q, mixed, y_near, after):
        start, size = sum(chunks[:q]), chunks[q]
        before = [y_near] if q else []
        return call(
            functools.partial(carry_kernel, team, start, hdim),
            rank,
            (*mixed, c_masked, uv, row_pack, docs, *before, *after),
            [
                whole((STATE, size)),
                whole((SPAN, size)),
                whole((SPAN, size)),
                whole((SPAN, STATE)),
                whole((SPAN, LANES)),
                whole((16, LANES)),
                whole(docs.shape),
            ]
            + [ANY] * (len(before) + len(after)),
            [shape((rows, size), BF16), shape((rows, gw), BF16)]
            + [shape((rows, size), BF16)] * 2
            + [shape((DOCS, LANES), F32)],
            [whole((rows, size)), ANY, whole((rows, size)), whole((rows, size)), whole((DOCS, LANES))],
            [pltpu.VMEM((16, size), F32), pltpu.VMEM((rows, size), BF16), pltpu.SemaphoreType.DMA],
            "carry",
            cost=cost(3),
            aliases={8: 1} if q else {},
        )

    y_own, y_far, y_across, stats, y_near = [], [], [], [], None
    ready = [mix(0, []), mix(1, [])]
    for q in range(len(chunks)):
        after = [y_far[q - 1], y_across[q - 1]] if q else []
        own, y_near, far, across, sums = carry(q, ready[q], y_near, after)
        y_own.append(own)
        y_far.append(swap(far, 2))
        y_across.append(swap(across, 3))
        stats.append(sums)
        if q + 2 < len(chunks):
            ready.append(mix(q + 2, [sums]))
    y_near = swap(y_near, 1)

    stats = call(
        sum_kernel,
        rank,
        tuple(stats),
        [whole((DOCS, LANES))] * len(stats),
        shape((DOCS, LANES), F32),
        whole((DOCS, LANES)),
        [],
        "sums",
        cost=cost(0.1),
    )
    step = 1
    while step < members:
        stats = stats + swap(stats, step)
        step *= 2

    gain = norm_gain[None]

    def norm(blocks, first, before):
        parts = [array for block in blocks for array in block]
        places, done = [], 0
        for block in blocks:
            places.append(list(range(done, done + len(block))))
            done += len(block)
        place = pl.BlockSpec((rows, gw), lambda i, pref: (0, pref[0] ^ (first + i)))
        return call(
            functools.partial(norm_kernel, places),
            rank,
            (*parts, z_stream, gain, *before),
            [whole(array.shape) for array in parts]
            + [place, pl.BlockSpec((1, gw), lambda i, pref: (0, pref[0] ^ (first + i)))]
            + [ANY] * len(before),
            shape((rows, inner), BF16),
            place,
            [pltpu.VMEM((rows, gw), F32)],
            "norm",
            grid=(len(blocks),),
            cost=cost(0.2),
            aliases={len(parts) + 3: 0} if before else {},
        )

    mixed = norm([y_own, [y_near]], 0, [])
    mixed = norm([y_far, y_across], 2, [mixed])
    doc_cosine = stats[:, 0] / jnp.sqrt(stats[:, 1] * stats[:, 2] + 1e-06)
    return (mixed, doc_cosine)


def solution(mesh):
    return jax.shard_map(
        on_device,
        mesh=mesh,
        in_specs=(
            P(("groups", "seq"), None),
            P(("groups", "seq"), None),
            P(("groups", "seq"), None),
            P(("groups", "seq"), None),
            P("groups"),
            P(),
            P(),
            P(),
            P(),
            P(),
            P(),
        ),
        out_specs=(P(("groups", "seq"), None), P("groups")),
        check_vma=False,
    )
```

time: 116 us -> 97 us (0.84); the launches traced: 114 us -> 96.7 us
  starting transfers between devices: 42.1 us -> 32.6 us
  local copies, waits for them, and re-layouts: 9.03 us -> 1.02 us
  Pallas kernels: 24.9 us -> 22.8 us
  waiting for transfers between devices: 36.3 us -> 38.3 us
    ppermute x32 -> x22, starting transfers between devices: 42.1 us -> 32.6 us  [the longest x18 17.6 us: swap(): return lax.ppermute(array, 'seq', [(i, i ^ k) for i in range(members)])]
    unnamed x42 -> x24, local copies, waits for them, and re-layouts: 8.95 us -> 0.94 us
    ppermute x32 -> x22, waiting for transfers between devices: 36.3 us -> 38.3 us  [the longest x18 36.4 us: swap(): return lax.ppermute(array, 'seq', [(i, i ^ k) for i in range(members)])]
    pallas_call x12 -> x13, Pallas kernels: 24.9 us -> 22.8 us  [call(): pl.pallas_call(kernel, grid_spec=pltpu.PrefetchScalarGridSpec(num_scalar_...]
  transfers between devices with their start and end apart: 32 -> 22, of which waited for: 12 -> 9; matrix products, arithmetic and copies ran while one was open for 1% -> 1% of each run, Pallas kernels for 16% -> 17%
where the time goes in v2:
time: 97 us; the launch traced here: 96.7 us
  waiting for transfers between devices  38.3 us (39%)
  starting transfers between devices  32.6 us (34%)
  Pallas kernels  22.8 us (24%)
  local copies, waits for them, and re-layouts  1.02 us (1%)
    ppermute x18, waiting for transfers between devices, swap(): return lax.ppermute(array, 'seq', [(i, i ^ k) for i in range(members)])  36.4 us
    pallas_call x13, Pallas kernels, call(): pl.pallas_call(kernel, grid_spec=pltpu.PrefetchScalarGridSpec(num_scalar_...  22.8 us
    ppermute x18, starting transfers between devices, swap(): return lax.ppermute(array, 'seq', [(i, i ^ k) for i in range(members)])  17.6 us
    ppermute x4, starting transfers between devices, onward(): lax.ppermute(array, 'seq', [(i, i + team) for i in range(members - team)])  15.1 us
  transfers between devices with their start and end apart: 22, of which 9 were waited for; matrix products, arithmetic and copies ran while one was open for 1% of the time, Pallas kernels for 17%

profile of v2, /device:TPU:0, one launch (start us, length us, event | category | flops | bytes accessed | tf_op | source)
XLA Modules:
  0.0 96.7 jit_solution(12237338333065509826)
XLA Ops:
  0.7 3.2 %pack.1 = (bf16[128,1408]{1,0:T(8,128)(2,1)}, bf16[128,1408]{1,0:T(8,128)(2,1)}, bf16[128,2944]{1,0:T(8,128)(2,1)}, bf16[128,768]{1,0:T(8,128)(2,1)}, bf16[128,7...) custom-call(s32[1]{0:T(128)} %bitcast.rank_ref, ...), custom_call_target="tpu_custom_call" | custom-call | flops 2000000000 | bytes 6000000 | tf_op jit(solution)/shard_map/pack/pallas_call | solution.py:33
  3.9 0.5 collective-permute-start
  4.4 2.6 %collective-permute-start.1 = (bf16[128,1408]{1,0:T(8,128)(2,1)}, bf16[128,1408]{1,0:T(8,128)(2,1)S(1)}, u32[]{:S(2)}, u32[]{:S(2)}) collective-permute-start(bf16[128,1408]{1,0:T(8,128)(2,1)} %get-tuple-element.40), channel_id=1, source_target_pairs={{0,2},{1,3},{2,0},{3,1},{4,6},{5,7},{6,4},{7,5},{8,10},{9,11},{10,... | collective-permute-start | bytes 1081352 | tf_op jit(solution)/shard_map/ppermute | solution.py:431
  7.0 0.1 collective-permute-start.2
  7.1 1.7 %collective-permute-start.6 = (bf16[128,768]{1,0:T(8,128)(2,1)}, bf16[128,768]{1,0:T(8,128)(2,1)S(1)}, u32[]{:S(2)}, u32[]{:S(2)}) collective-permute-start(bf16[128,768]{1,0:T(8,128)(2,1)} %get-tuple-element.52), channel_id=1, source_target_pairs={{0,2},{1,3},{2,0},{3,1},{4,6},{5,7},{6,4},{7,5},{8,10},{9,11},{10,... | collective-permute-start | bytes 589832 | tf_op jit(solution)/shard_map/ppermute | solution.py:431
  8.8 0.1 pad_maximum_fusion.refs_6_.refs_7_
  8.9 0.1 fusion.4
  9.0 0.1 pad.4.clone
  9.1 0.1 maximum_maximum_fusion.refs_8_
  9.2 7.3 %collective-permute-done.1.refs_1_.refs_2_ = bf16[128,1408]{1,0:T(8,128)(2,1)S(1)} collective-permute-done((bf16[128,1408]{1,0:T(8,128)(2,1)}, bf16[128,1408]{1,0:T(8,128)(2,1)S(1)}, u32[]{:S(2)}, u32[]{:S(2)}) %collective-permute-start.1) | collective-permute-done | bytes 360480 | tf_op jit(solution)/shard_map/ppermute | solution.py:431
  16.5 1.9 %collective-permute-start.11 = (bf16[128,768]{1,0:T(8,128)(2,1)}, bf16[128,768]{1,0:T(8,128)(2,1)S(1)}, u32[]{:S(2)}, u32[]{:S(2)}) collective-permute-start(bf16[128,768]{1,0:T(8,128)(2,1)} %get-tuple-element.60), channel_id=1, source_target_pairs={{0,2},{1,3},{2,0},{3,1},{4,6},{5,7},{6,4},{7,5},{8,10},{9,11},{10,... | collective-permute-start | bytes 589832 | tf_op jit(solution)/shard_map/ppermute | solution.py:431
  18.4 5.3 %collective-permute-done.2.refs_2_.refs_3_ = bf16[128,1408]{1,0:T(8,128)(2,1)S(1)} collective-permute-done((bf16[128,1408]{1,0:T(8,128)(2,1)}, bf16[128,1408]{1,0:T(8,128)(2,1)S(1)}, u32[]{:S(2)}, u32[]{:S(2)}) %collective-permute-start.2) | collective-permute-done | bytes 360480 | tf_op jit(solution)/shard_map/ppermute | solution.py:431
  23.8 1.8 %collective-permute-start.12 = (bf16[128,768]{1,0:T(8,128)(2,1)}, bf16[128,768]{1,0:T(8,128)(2,1)S(1)}, u32[]{:S(2)}, u32[]{:S(2)}) collective-permute-start(bf16[128,768]{1,0:T(8,128)(2,1)} %get-tuple-element.61), channel_id=1, source_target_pairs={{0,3},{1,2},{2,1},{3,0},{4,7},{5,6},{6,5},{7,4},{8,11},{9,10},{10,... | collective-permute-start | bytes 589832 | tf_op jit(solution)/shard_map/ppermute | solution.py:431
  25.6 0.9 copy-done.5
  26.5 0.1 relay.1
  26.6 3.6 %collective-permute-start.3 = (bf16[16,2560]{1,0:T(8,128)(2,1)S(1)}, bf16[16,2560]{1,0:T(8,128)(2,1)S(1)}, u32[]{:S(2)}, u32[]{:S(2)}) collective-permute-start(bf16[16,2560]{1,0:T(8,128)(2,1)S(1)} %relay.1), channel_id=1, source_target_pairs={{0,4},{1,5},{2,6},{3,7},{4,8},{5,9},{6,10},{7,11},{8,12},{9,13},{1... | collective-permute-start | bytes 245768 | tf_op jit(solution)/shard_map/ppermute | solution.py:434
  30.3 0.1 shift.1.refs_4_.refs_5_
  30.4 0.0 copy-start.2
  30.4 1.9 %collective-permute-done.3.refs_3_.refs_4_ = bf16[16,2560]{1,0:T(8,128)(2,1)S(1)} collective-permute-done((bf16[16,2560]{1,0:T(8,128)(2,1)S(1)}, bf16[16,2560]{1,0:T(8,128)(2,1)S(1)}, u32[]{:S(2)}, u32[]{:S(2)}) %collective-permute-start.3) | collective-permute-done | bytes 81952 | tf_op jit(solution)/shard_map/ppermute | solution.py:434
  32.3 2.2 %bc.1 = (bf16[512,512]{1,0:T(8,128)(2,1)S(1)}, bf16[256,512]{1,0:T(8,128)(2,1)S(1)}, bf16[512,256]{1,0:T(8,128)(2,1)S(1)}, bf16[512,128]{1,0:T(8,128)(2,1)S(1)}, bf16[16,128]{1,0:T(8,128)(2,1)S(1)}) custom-call(s32[1]{0:T(128)} %bitcast.rank_ref, bf16[128,2048]{1,0:T(8,128)(2,1)S(1)} %copy-done.3, bf16[128,128]{1,0:T(8,128)(2,1)S(1)} %copy-done.4, ...), custom_call_target="tpu_custom_call" | custom-call | flops 4000000000 | bytes 12000000 | tf_op jit(solution)/shard_map/bc/pallas_call | solution.py:33
  34.5 2.1 %mix.3 = (bf16[512,512]{1,0:T(8,128)(2,1)S(1)}, f32[512,512]{1,0:T(8,128)S(1)}, bf16[256,512]{1,0:T(8,128)(2,1)S(1)}) custom-call(s32[1]{0:T(128)} %bitcast.rank_ref, bf16[128,8192]{1,0:T(8,128)(2,1)S(1)} %copy-done.2, bf16[128,2944]{1,0:T(8,128)(2,1)S(1)} %collective-permute-done.refs_0_.refs_1_, ...), custom_call_target="tpu_custom_call" | custom-call | flops 4000000000 | bytes 12000000 | tf_op jit(solution)/shard_map/mix/pallas_call | solution.py:33
  36.6 4.3 %collective-permute-start.4 = (bf16[256,512]{1,0:T(8,128)(2,1)S(1)}, bf16[256,512]{1,0:T(8,128)(2,1)S(1)}, u32[]{:S(2)}, u32[]{:S(2)}) collective-permute-start(bf16[256,512]{1,0:T(8,128)(2,1)S(1)} %get-tuple-element.47), channel_id=1, source_target_pairs={{0,4},{1,5},{2,6},{3,7},{4,8},{5,9},{6,10},{7,11},{8,12},{9,13},{1... | collective-permute-start | bytes 786440 | tf_op jit(solution)/shard_map/ppermute | solution.py:434
  40.9 3.1 %mix.4 = (bf16[512,768]{1,0:T(8,128)(2,1)S(1)}, f32[512,768]{1,0:T(8,128)S(1)}, bf16[256,768]{1,0:T(8,128)(2,1)S(1)}) custom-call(s32[1]{0:T(128)} %bitcast.rank_ref, bf16[128,8192]{1,0:T(8,128)(2,1)S(1)} %copy-done.2, bf16[128,2944]{1,0:T(8,128)(2,1)S(1)} %collective-permute-done.refs_0_.refs_1_, bf16[128,768]{1,0:T(8,128)(2,1)S(1)} %collective-permute-done.6.refs_2_, ...), custom_call_target="tpu_custom_call" | custom-call | flops 4000000000 | bytes 12000000 | tf_op jit(solution)/shard_map/mix/pallas_call | solution.py:33
  44.0 3.5 %collective-permute-start.8 = (bf16[256,768]{1,0:T(8,128)(2,1)S(1)}, bf16[256,768]{1,0:T(8,128)(2,1)S(1)}, u32[]{:S(2)}, u32[]{:S(2)}) collective-permute-start(bf16[256,768]{1,0:T(8,128)(2,1)S(1)} %get-tuple-element.54), channel_id=1, source_target_pairs={{0,4},{1,5},{2,6},{3,7},{4,8},{5,9},{6,10},{7,11},{8,12},{9,13},{1... | collective-permute-start | bytes 1179656 | tf_op jit(solution)/shard_map/ppermute | solution.py:434
  47.5 1.6 %carry.3 = (bf16[128,512]{1,0:T(8,128)(2,1)S(1)}, bf16[128,2048]{1,0:T(8,128)(2,1)S(1)}, bf16[128,512]{1,0:T(8,128)(2,1)S(1)}, bf16[128,512]{1,0:T(8,128)(2,1)S(1)}, f32[16,128]{1,0:T(8,128)S(1)}) custom-call(s32[1]{0:T(128)} %bitcast.rank_ref, bf16[256,512]{1,0:T(8,128)(2,1)S(1)} %collective-permute-done.4.st_ref, f32[512,512]{1,0:T(8,128)S(1)} %get-tuple-element.48.yl_ref, ...), custom_call_target="tpu_custom_call" | custom-call | flops 3000000000 | bytes 9000000 | tf_op jit(solution)/shard_map/carry/pallas_call | solution.py:33
  49.1 0.6 collective-permute-start.5
  49.7 3.1 %mix.5 = (bf16[512,768]{1,0:T(8,128)(2,1)S(1)}, f32[512,768]{1,0:T(8,128)S(1)}, bf16[256,768]{1,0:T(8,128)(2,1)S(1)}) custom-call(s32[1]{0:T(128)} %bitcast.rank_ref, bf16[128,8192]{1,0:T(8,128)(2,1)S(1)} %copy-done.2, bf16[128,2944]{1,0:T(8,128)(2,1)S(1)} %collective-permute-done.refs_0_.refs_1_, bf16[128,768]{1,0:T(8,128)(2,1)S(1)} %collective-permute-done.11.refs_2_, ...), custom_call_target="tpu_custom_call" | custom-call | flops 4000000000 | bytes 12000000 | tf_op jit(solution)/shard_map/mix/pallas_call | solution.py:33
  52.8 3.7 %collective-permute-start.13 = (bf16[256,768]{1,0:T(8,128)(2,1)S(1)}, bf16[256,768]{1,0:T(8,128)(2,1)S(1)}, u32[]{:S(2)}, u32[]{:S(2)}) collective-permute-start(bf16[256,768]{1,0:T(8,128)(2,1)S(1)} %get-tuple-element.63), channel_id=1, source_target_pairs={{0,4},{1,5},{2,6},{3,7},{4,8},{5,9},{6,10},{7,11},{8,12},{9,13},{1... | collective-permute-start | bytes 1179656 | tf_op jit(solution)/shard_map/ppermute | solution.py:434
  56.5 1.9 %carry.4 = (bf16[128,768]{1,0:T(8,128)(2,1)S(1)}, bf16[128,2048]{1,0:T(8,128)(2,1)S(1)}, bf16[128,768]{1,0:T(8,128)(2,1)S(1)}, bf16[128,768]{1,0:T(8,128)(2,1)S(1)}, f32[16,128]{1,0:T(8,128)S(1)}) custom-call(s32[1]{0:T(128)} %bitcast.rank_ref, bf16[256,768]{1,0:T(8,128)(2,1)S(1)} %collective-permute-done.8.st_ref, ...), custom_call_target="tpu_custom_call", output_to_operand_aliasing={{1}: (8, {})} | custom-call | flops 3000000000 | bytes 9000000 | tf_op jit(solution)/shard_map/carry/pallas_call | solution.py:33
  58.4 1.6 %collective-permute-start.10 = (bf16[128,768]{1,0:T(8,128)(2,1)S(1)}, bf16[128,768]{1,0:T(8,128)(2,1)S(1)}, u32[]{:S(2)}, u32[]{:S(2)}) collective-permute-start(bf16[128,768]{1,0:T(8,128)(2,1)S(1)} %get-tuple-element.59), channel_id=1, source_target_pairs={{0,2},{1,3},{2,0},{3,1},{4,6},{5,7},{6,4},{7,5},{8,10},{9,11},{10,... | collective-permute-start | bytes 589832 | tf_op jit(solution)/shard_map/ppermute | solution.py:431
  60.0 1.2 %collective-permute-start.14 = (bf16[128,768]{1,0:T(8,128)(2,1)S(1)}, bf16[128,768]{1,0:T(8,128)(2,1)S(1)}, u32[]{:S(2)}, u32[]{:S(2)}) collective-permute-start(bf16[128,768]{1,0:T(8,128)(2,1)S(1)} %get-tuple-element.67), channel_id=1, source_target_pairs={{0,3},{1,2},{2,1},{3,0},{4,7},{5,6},{6,5},{7,4},{8,11},{9,10},{10,... | collective-permute-start | bytes 589832 | tf_op jit(solution)/shard_map/ppermute | solution.py:431
  61.1 4.8 %collective-permute-done.10.refs_1_ = bf16[128,768]{1,0:T(8,128)(2,1)S(1)} collective-permute-done((bf16[128,768]{1,0:T(8,128)(2,1)S(1)}, bf16[128,768]{1,0:T(8,128)(2,1)S(1)}, u32[]{:S(2)}, u32[]{:S(2)}) %collective-permute-start.10) | collective-permute-done | bytes 196640 | tf_op jit(solution)/shard_map/ppermute | solution.py:431
  66.0 4.5 %collective-permute-done.14.refs_2_.refs_4_ = bf16[128,768]{1,0:T(8,128)(2,1)S(1)} collective-permute-done((bf16[128,768]{1,0:T(8,128)(2,1)S(1)}, bf16[128,768]{1,0:T(8,128)(2,1)S(1)}, u32[]{:S(2)}, u32[]{:S(2)}) %collective-permute-start.14) | collective-permute-done | bytes 196640 | tf_op jit(solution)/shard_map/ppermute | solution.py:431
  70.5 1.9 %carry.5 = (bf16[128,768]{1,0:T(8,128)(2,1)S(1)}, bf16[128,2048]{1,0:T(8,128)(2,1)S(1)}, bf16[128,768]{1,0:T(8,128)(2,1)S(1)}, bf16[128,768]{1,0:T(8,128)(2,1)S(1)}, f32[16,128]{1,0:T(8,128)S(1)}) custom-call(s32[1]{0:T(128)} %bitcast.rank_ref, bf16[256,768]{1,0:T(8,128)(2,1)S(1)} %collective-permute-done.13.st_ref, ...), custom_call_target="tpu_custom_call", output_to_operand_aliasing={{1}: (8, {})} | custom-call | flops 3000000000 | bytes 9000000 | tf_op jit(solution)/shard_map/carry/pallas_call | solution.py:33
  72.4 0.1 collective-permute-start.17
  72.4 0.7 collective-permute-start.15
  73.1 1.2 %collective-permute-start.16 = (bf16[128,768]{1,0:T(8,128)(2,1)S(1)}, bf16[128,768]{1,0:T(8,128)(2,1)S(1)}, u32[]{:S(2)}, u32[]{:S(2)}) collective-permute-start(bf16[128,768]{1,0:T(8,128)(2,1)S(1)} %get-tuple-element.69), channel_id=1, source_target_pairs={{0,3},{1,2},{2,1},{3,0},{4,7},{5,6},{6,5},{7,4},{8,11},{9,10},{10,... | collective-permute-start | bytes 589832 | tf_op jit(solution)/shard_map/ppermute | solution.py:431
  74.3 0.3 collective-permute-start.18
  74.6 0.8 collective-permute-done.18
  75.5 0.6 collective-permute-start.19
  76.1 8.0 %collective-permute-done.19 = f32[16,128]{1,0:T(8,128)S(1)} collective-permute-done((f32[16,128]{1,0:T(8,128)S(1)}, f32[16,128]{1,0:T(8,128)S(1)}, u32[]{:S(2)}, u32[]{:S(2)}) %collective-permute-start.19) | collective-permute-done | bytes 8224 | tf_op jit(solution)/shard_map/ppermute | solution.py:431
  84.1 0.6 collective-permute-start.20
  84.7 3.1 %collective-permute-done.20 = f32[16,128]{1,0:T(8,128)S(1)} collective-permute-done((f32[16,128]{1,0:T(8,128)S(1)}, f32[16,128]{1,0:T(8,128)S(1)}, u32[]{:S(2)}, u32[]{:S(2)}) %collective-permute-start.20) | collective-permute-done | bytes 8224 | tf_op jit(solution)/shard_map/ppermute | solution.py:431
  87.8 2.1 %collective-permute-start.21 = (f32[16,128]{1,0:T(8,128)S(1)}, f32[16,128]{1,0:T(8,128)S(1)}, u32[]{:S(2)}, u32[]{:S(2)}) collective-permute-start(f32[16,128]{1,0:T(8,128)S(1)} %add.30), channel_id=1, source_target_pairs={{0,8},{1,9},{2,10},{3,11},{4,12},{5,13},{6,14},{7,15},{8,0},{9,1},... | collective-permute-start | bytes 24584 | tf_op jit(solution)/shard_map/ppermute | solution.py:431
  89.9 2.5 %collective-permute-done.21 = f32[16,128]{1,0:T(8,128)S(1)} collective-permute-done((f32[16,128]{1,0:T(8,128)S(1)}, f32[16,128]{1,0:T(8,128)S(1)}, u32[]{:S(2)}, u32[]{:S(2)}) %collective-permute-start.21) | collective-permute-done | bytes 8224 | tf_op jit(solution)/shard_map/ppermute | solution.py:431
  92.4 0.7 fusion.3
  93.1 1.8 %norm.2.refs_8_ = bf16[128,8192]{1,0:T(8,128)(2,1)} custom-call(s32[1]{0:T(128)} %bitcast.rank_ref, bf16[128,512]{1,0:T(8,128)(2,1)S(1)} %get-tuple-element.70.refs_0_, bf16[128,768]{1,0:T(8,128)(2,1)S(1)} %get-tuple-element.71.refs_1_, bf16[128,768]{1,0:T(8,128)(2,1)S(1)} %get-tuple-element.72.refs_2_, ...), custom_call_target="tpu_custom_call" | custom-call | flops 200000000 | bytes 600000 | tf_op jit(solution)/shard_map/norm/pallas_call | solution.py:33
  94.9 1.8 %norm.3 = bf16[128,8192]{1,0:T(8,128)(2,1)} custom-call(s32[1]{0:T(128)} %bitcast.rank_ref, bf16[128,512]{1,0:T(8,128)(2,1)S(1)} %collective-permute-done.5.refs_1_.refs_0_, bf16[128,768]{1,0:T(8,128)(2,1)S(1)} %collective-permute-done.10.refs_1_, bf16[128,768]{1,0:T(8,128)(2,1)S(1)} %collective-permute-done.15.refs_2_, ...), custom_call_target="tpu_custom_call", output_to_operand_aliasing={{}: (9, {})} | custom-call | flops 200000000 | bytes 600000 | tf_op jit(solution)/shard_map/norm/pallas_call | solution.py:33
  (44 shorter events, 0.1 us)
Async XLA Ops:
  0.6 8.2 %copy-start.6 = (f32[4,10240]{1,0:T(4,128)S(1)}, f32[4,10240]{1,0:T(4,128)}, u32[]{:S(2)}) copy-start(f32[4,10240]{1,0:T(4,128)} %param.16) | copy-start | bytes 491524
  0.7 8.2 %copy-start.7 = (f32[10240]{0:T(1024)S(1)}, f32[10240]{0:T(1024)}, u32[]{:S(2)}) copy-start(f32[10240]{0:T(1024)} %param.17) | copy-start | bytes 122884
  0.7 8.3 %copy-start.8 = (s32[2048]{0:T(1024)S(1)}, s32[2048]{0:T(1024)}, u32[]{:S(2)}) copy-start(s32[2048]{0:T(1024)} %param.15) | copy-start | bytes 24580
  0.7 8.4 %copy-start.9 = (f32[128]{0:T(128)S(1)}, f32[128]{0:T(128)}, u32[]{:S(2)}) copy-start(f32[128]{0:T(128)} %param.20) | copy-start | bytes 1540
  0.7 8.4 %copy-start.10 = (f32[128]{0:T(128)S(1)}, f32[128]{0:T(128)}, u32[]{:S(2)}) copy-start(f32[128]{0:T(128)} %param.19) | copy-start | bytes 1540
  0.7 8.4 %copy-start.11 = (f32[128]{0:T(128)S(1)}, f32[128]{0:T(128)}, u32[]{:S(2)}) copy-start(f32[128]{0:T(128)} %param.18) | copy-start | bytes 1540
  3.9 21.7 %collective-permute-start = (bf16[128,2944]{1,0:T(8,128)(2,1)}, bf16[128,2944]{1,0:T(8,128)(2,1)S(1)}, u32[]{:S(2)}, u32[]{:S(2)}) collective-permute-start(bf16[128,2944]{1,0:T(8,128)(2,1)} %get-tuple-element.39), channel_id=1, source_target_pairs={{0,1},{1,0},{2,3},{3,2},{4,5},{5,4},{6,7},{7,6},{8,9},{9,8},{10,11... | collective-permute-start | bytes 2261000 | tf_op jit(solution)/shard_map/ppermute | solution.py:431
  4.4 12.1 %collective-permute-start.1 = (bf16[128,1408]{1,0:T(8,128)(2,1)}, bf16[128,1408]{1,0:T(8,128)(2,1)S(1)}, u32[]{:S(2)}, u32[]{:S(2)}) collective-permute-start(bf16[128,1408]{1,0:T(8,128)(2,1)} %get-tuple-element.40), channel_id=1, source_target_pairs={{0,2},{1,3},{2,0},{3,1},{4,6},{5,7},{6,4},{7,5},{8,10},{9,11},{10,... | collective-permute-start | bytes 1081352 | tf_op jit(solution)/shard_map/ppermute | solution.py:431
  7.0 16.8 %collective-permute-start.2 = (bf16[128,1408]{1,0:T(8,128)(2,1)}, bf16[128,1408]{1,0:T(8,128)(2,1)S(1)}, u32[]{:S(2)}, u32[]{:S(2)}) collective-permute-start(bf16[128,1408]{1,0:T(8,128)(2,1)} %get-tuple-element.41), channel_id=1, source_target_pairs={{0,3},{1,2},{2,1},{3,0},{4,7},{5,6},{6,5},{7,4},{8,11},{9,10},{10,... | collective-permute-start | bytes 1081352 | tf_op jit(solution)/shard_map/ppermute | solution.py:431
  7.1 33.8 %collective-permute-start.6 = (bf16[128,768]{1,0:T(8,128)(2,1)}, bf16[128,768]{1,0:T(8,128)(2,1)S(1)}, u32[]{:S(2)}, u32[]{:S(2)}) collective-permute-start(bf16[128,768]{1,0:T(8,128)(2,1)} %get-tuple-element.52), channel_id=1, source_target_pairs={{0,2},{1,3},{2,0},{3,1},{4,6},{5,7},{6,4},{7,5},{8,10},{9,11},{10,... | collective-permute-start | bytes 589832 | tf_op jit(solution)/shard_map/ppermute | solution.py:431
  8.8 32.1 %collective-permute-start.7 = (bf16[128,768]{1,0:T(8,128)(2,1)}, bf16[128,768]{1,0:T(8,128)(2,1)S(1)}, u32[]{:S(2)}, u32[]{:S(2)}) collective-permute-start(bf16[128,768]{1,0:T(8,128)(2,1)} %get-tuple-element.53), channel_id=1, source_target_pairs={{0,3},{1,2},{2,1},{3,0},{4,7},{5,6},{6,5},{7,4},{8,11},{9,10},{10,... | collective-permute-start | bytes 589832 | tf_op jit(solution)/shard_map/ppermute | solution.py:431
  16.5 33.2 %collective-permute-start.11 = (bf16[128,768]{1,0:T(8,128)(2,1)}, bf16[128,768]{1,0:T(8,128)(2,1)S(1)}, u32[]{:S(2)}, u32[]{:S(2)}) collective-permute-start(bf16[128,768]{1,0:T(8,128)(2,1)} %get-tuple-element.60), channel_id=1, source_target_pairs={{0,2},{1,3},{2,0},{3,1},{4,6},{5,7},{6,4},{7,5},{8,10},{9,11},{10,... | collective-permute-start | bytes 589832 | tf_op jit(solution)/shard_map/ppermute | solution.py:431
  23.8 25.9 %collective-permute-start.12 = (bf16[128,768]{1,0:T(8,128)(2,1)}, bf16[128,768]{1,0:T(8,128)(2,1)S(1)}, u32[]{:S(2)}, u32[]{:S(2)}) collective-permute-start(bf16[128,768]{1,0:T(8,128)(2,1)} %get-tuple-element.61), channel_id=1, source_target_pairs={{0,3},{1,2},{2,1},{3,0},{4,7},{5,6},{6,5},{7,4},{8,11},{9,10},{10,... | collective-permute-start | bytes 589832 | tf_op jit(solution)/shard_map/ppermute | solution.py:431
  25.6 0.9 copy-start.5
  26.6 5.7 %copy-start.3 = (bf16[128,2048]{1,0:T(8,128)(2,1)S(1)}, bf16[128,2048]{1,0:T(8,128)(2,1)}, u32[]{:S(2)}) copy-start(bf16[128,2048]{1,0:T(8,128)(2,1)} %bc_ref.3) | copy-start | bytes 1572868
  26.6 5.7 %copy-start.4 = (bf16[128,128]{1,0:T(8,128)(2,1)S(1)}, bf16[128,128]{1,0:T(8,128)(2,1)}, u32[]{:S(2)}) copy-start(bf16[128,128]{1,0:T(8,128)(2,1)} %dt_ref.3) | copy-start | bytes 98308
  26.6 5.7 %collective-permute-start.3 = (bf16[16,2560]{1,0:T(8,128)(2,1)S(1)}, bf16[16,2560]{1,0:T(8,128)(2,1)S(1)}, u32[]{:S(2)}, u32[]{:S(2)}) collective-permute-start(bf16[16,2560]{1,0:T(8,128)(2,1)S(1)} %relay.1), channel_id=1, source_target_pairs={{0,4},{1,5},{2,6},{3,7},{4,8},{5,9},{6,10},{7,11},{8,12},{9,13},{1... | collective-permute-start | bytes 245768 | tf_op jit(solution)/shard_map/ppermute | solution.py:434
  30.4 4.1 %copy-start.2 = (bf16[128,8192]{1,0:T(8,128)(2,1)S(1)}, bf16[128,8192]{1,0:T(8,128)(2,1)}, u32[]{:S(2)}) copy-start(bf16[128,8192]{1,0:T(8,128)(2,1)} %refs_0_.5) | copy-start | bytes 6291460
  36.6 10.9 %collective-permute-start.4 = (bf16[256,512]{1,0:T(8,128)(2,1)S(1)}, bf16[256,512]{1,0:T(8,128)(2,1)S(1)}, u32[]{:S(2)}, u32[]{:S(2)}) collective-permute-start(bf16[256,512]{1,0:T(8,128)(2,1)S(1)} %get-tuple-element.47), channel_id=1, source_target_pairs={{0,4},{1,5},{2,6},{3,7},{4,8},{5,9},{6,10},{7,11},{8,12},{9,13},{1... | collective-permute-start | bytes 786440 | tf_op jit(solution)/shard_map/ppermute | solution.py:434
  44.0 12.5 %collective-permute-start.8 = (bf16[256,768]{1,0:T(8,128)(2,1)S(1)}, bf16[256,768]{1,0:T(8,128)(2,1)S(1)}, u32[]{:S(2)}, u32[]{:S(2)}) collective-permute-start(bf16[256,768]{1,0:T(8,128)(2,1)S(1)} %get-tuple-element.54), channel_id=1, source_target_pairs={{0,4},{1,5},{2,6},{3,7},{4,8},{5,9},{6,10},{7,11},{8,12},{9,13},{1... | collective-permute-start | bytes 1179656 | tf_op jit(solution)/shard_map/ppermute | solution.py:434
  49.1 7.4 %collective-permute-start.5 = (bf16[128,512]{1,0:T(8,128)(2,1)S(1)}, bf16[128,512]{1,0:T(8,128)(2,1)S(1)}, u32[]{:S(2)}, u32[]{:S(2)}) collective-permute-start(bf16[128,512]{1,0:T(8,128)(2,1)S(1)} %get-tuple-element.51), channel_id=1, source_target_pairs={{0,2},{1,3},{2,0},{3,1},{4,6},{5,7},{6,4},{7,5},{8,10},{9,11},{10,... | collective-permute-start | bytes 393224 | tf_op jit(solution)/shard_map/ppermute | solution.py:431
  49.7 6.8 %collective-permute-start.9 = (bf16[128,512]{1,0:T(8,128)(2,1)S(1)}, bf16[128,512]{1,0:T(8,128)(2,1)S(1)}, u32[]{:S(2)}, u32[]{:S(2)}) collective-permute-start(bf16[128,512]{1,0:T(8,128)(2,1)S(1)} %get-tuple-element.58), channel_id=1, source_target_pairs={{0,3},{1,2},{2,1},{3,0},{4,7},{5,6},{6,5},{7,4},{8,11},{9,10},{10,... | collective-permute-start | bytes 393224 | tf_op jit(solution)/shard_map/ppermute | solution.py:431
  52.8 17.7 %collective-permute-start.13 = (bf16[256,768]{1,0:T(8,128)(2,1)S(1)}, bf16[256,768]{1,0:T(8,128)(2,1)S(1)}, u32[]{:S(2)}, u32[]{:S(2)}) collective-permute-start(bf16[256,768]{1,0:T(8,128)(2,1)S(1)} %get-tuple-element.63), channel_id=1, source_target_pairs={{0,4},{1,5},{2,6},{3,7},{4,8},{5,9},{6,10},{7,11},{8,12},{9,13},{1... | collective-permute-start | bytes 1179656 | tf_op jit(solution)/shard_map/ppermute | solution.py:434
  58.4 7.6 %collective-permute-start.10 = (bf16[128,768]{1,0:T(8,128)(2,1)S(1)}, bf16[128,768]{1,0:T(8,128)(2,1)S(1)}, u32[]{:S(2)}, u32[]{:S(2)}) collective-permute-start(bf16[128,768]{1,0:T(8,128)(2,1)S(1)} %get-tuple-element.59), channel_id=1, source_target_pairs={{0,2},{1,3},{2,0},{3,1},{4,6},{5,7},{6,4},{7,5},{8,10},{9,11},{10,... | collective-permute-start | bytes 589832 | tf_op jit(solution)/shard_map/ppermute | solution.py:431
  60.0 10.5 %collective-permute-start.14 = (bf16[128,768]{1,0:T(8,128)(2,1)S(1)}, bf16[128,768]{1,0:T(8,128)(2,1)S(1)}, u32[]{:S(2)}, u32[]{:S(2)}) collective-permute-start(bf16[128,768]{1,0:T(8,128)(2,1)S(1)} %get-tuple-element.67), channel_id=1, source_target_pairs={{0,3},{1,2},{2,1},{3,0},{4,7},{5,6},{6,5},{7,4},{8,11},{9,10},{10,... | collective-permute-start | bytes 589832 | tf_op jit(solution)/shard_map/ppermute | solution.py:431
  70.5 22.6 %copy-start = (bf16[128,8192]{1,0:T(8,128)(2,1)S(1)}, bf16[128,8192]{1,0:T(8,128)(2,1)}, u32[]{:S(2)}) copy-start(bf16[128,8192]{1,0:T(8,128)(2,1)} %refs_6_.1) | copy-start | bytes 6291460
  70.5 22.6 %copy-start.1 = (f32[8192]{0:T(1024)S(1)}, f32[8192]{0:T(1024)}, u32[]{:S(2)}) copy-start(f32[8192]{0:T(1024)} %param.21) | copy-start | bytes 98308
  72.4 20.7 %collective-permute-start.17 = (bf16[128,2048]{1,0:T(8,128)(2,1)S(1)}, bf16[128,2048]{1,0:T(8,128)(2,1)S(1)}, u32[]{:S(2)}, u32[]{:S(2)}) collective-permute-start(bf16[128,2048]{1,0:T(8,128)(2,1)S(1)} %get-tuple-element.73), channel_id=1, source_target_pairs={{0,1},{1,0},{2,3},{3,2},{4,5},{5,4},{6,7},{7,6},{8,9},{9,8},{10,11... | collective-permute-start | bytes 1572872 | tf_op jit(solution)/shard_map/ppermute | solution.py:431
  72.4 22.5 %collective-permute-start.15 = (bf16[128,768]{1,0:T(8,128)(2,1)S(1)}, bf16[128,768]{1,0:T(8,128)(2,1)S(1)}, u32[]{:S(2)}, u32[]{:S(2)}) collective-permute-start(bf16[128,768]{1,0:T(8,128)(2,1)S(1)} %get-tuple-element.68), channel_id=1, source_target_pairs={{0,2},{1,3},{2,0},{3,1},{4,6},{5,7},{6,4},{7,5},{8,10},{9,11},{10,... | collective-permute-start | bytes 589832 | tf_op jit(solution)/shard_map/ppermute | solution.py:431
  73.1 21.8 %collective-permute-start.16 = (bf16[128,768]{1,0:T(8,128)(2,1)S(1)}, bf16[128,768]{1,0:T(8,128)(2,1)S(1)}, u32[]{:S(2)}, u32[]{:S(2)}) collective-permute-start(bf16[128,768]{1,0:T(8,128)(2,1)S(1)} %get-tuple-element.69), channel_id=1, source_target_pairs={{0,3},{1,2},{2,1},{3,0},{4,7},{5,6},{6,5},{7,4},{8,11},{9,10},{10,... | collective-permute-start | bytes 589832 | tf_op jit(solution)/shard_map/ppermute | solution.py:431
  74.3 1.2 %collective-permute-start.18 = (f32[16,128]{1,0:T(8,128)S(1)}, f32[16,128]{1,0:T(8,128)S(1)}, u32[]{:S(2)}, u32[]{:S(2)}) collective-permute-start(f32[16,128]{1,0:T(8,128)S(1)} %sums.1), channel_id=1, source_target_pairs={{0,1},{1,0},{2,3},{3,2},{4,5},{5,4},{6,7},{7,6},{8,9},{9,8},{10,11... | collective-permute-start | bytes 24584 | tf_op jit(solution)/shard_map/ppermute | solution.py:431
  75.5 8.7 %collective-permute-start.19 = (f32[16,128]{1,0:T(8,128)S(1)}, f32[16,128]{1,0:T(8,128)S(1)}, u32[]{:S(2)}, u32[]{:S(2)}) collective-permute-start(f32[16,128]{1,0:T(8,128)S(1)} %add.28), channel_id=1, source_target_pairs={{0,2},{1,3},{2,0},{3,1},{4,6},{5,7},{6,4},{7,5},{8,10},{9,11},{10,... | collective-permute-start | bytes 24584 | tf_op jit(solution)/shard_map/ppermute | solution.py:431
  84.1 3.7 %collective-permute-start.20 = (f32[16,128]{1,0:T(8,128)S(1)}, f32[16,128]{1,0:T(8,128)S(1)}, u32[]{:S(2)}, u32[]{:S(2)}) collective-permute-start(f32[16,128]{1,0:T(8,128)S(1)} %add.29), channel_id=1, source_target_pairs={{0,4},{1,5},{2,6},{3,7},{4,0},{5,1},{6,2},{7,3},{8,12},{9,13},{10,... | collective-permute-start | bytes 24584 | tf_op jit(solution)/shard_map/ppermute | solution.py:431
  87.8 4.6 %collective-permute-start.21 = (f32[16,128]{1,0:T(8,128)S(1)}, f32[16,128]{1,0:T(8,128)S(1)}, u32[]{:S(2)}, u32[]{:S(2)}) collective-permute-start(f32[16,128]{1,0:T(8,128)S(1)} %add.30), channel_id=1, source_target_pairs={{0,8},{1,9},{2,10},{3,11},{4,12},{5,13},{6,14},{7,15},{8,0},{9,1},... | collective-permute-start | bytes 24584 | tf_op jit(solution)/shard_map/ppermute | solution.py:431

commit v3 on v2

--- a/solution.py
+++ b/solution.py
@@ -51,28 +51,26 @@
     return pl.CostEstimate(flops=int(us * 1e9), bytes_accessed=int(us * 3e6), transcendentals=0)
 
 
-def pack_kernel(team, chunks, gw, rank_ref, x_ref, bc_ref, dt_ref, *refs):
+def pack_kernel(team, gw, rank_ref, x_ref, bc_ref, dt_ref, *refs):
     xv_ref, tail_ref, bcv_ref, dtv_ref, in_sems, out_sems = refs[-6:]
     outs = list(refs[:-6])
     rank = rank_ref[0]
     rows = x_ref.shape[0]
     half = bc_ref.shape[1] // 2
     fold = gw * HALO // rows
+    last = pl.ds(rows - HALO, HALO)
 
     def fetch(src, dst, sem):
         made = pltpu.make_async_copy(src, dst, in_sems.at[sem])
         made.start()
         return made
 
-    fetches = [fetch(bc_ref, bcv_ref, 0), fetch(dt_ref, dtv_ref, 1)]
-    x_fetches = {}
-    for k in (2, 3, 1):
-        at = pl.multiple_of((rank ^ k) * gw, LANES)
-        x_fetches[k] = fetch(x_ref.at[:, pl.ds(at, gw)], xv_ref.at[k - 1], 1 + k)
-    at = pl.multiple_of(rank * gw, LANES)
-    last = pl.ds(rows - HALO, HALO)
-    tail_fetch = fetch(x_ref.at[last, pl.ds(at, gw)], tail_ref, 1 + team)
-
+    fetches = [
+        fetch(bc_ref, bcv_ref, 0),
+        fetch(dt_ref, dtv_ref, 1),
+        fetch(x_ref.at[last], tail_ref, 2),
+        fetch(x_ref.at[:, pl.ds(pl.multiple_of((rank ^ 1) * gw, LANES), gw)], xv_ref, 3),
+    ]
     copies = []
 
     def copy(src, dst):
@@ -80,8 +78,16 @@
         made.start()
         copies.append(made)
 
-    for made in fetches:
+    for made in fetches[:3]:
         made.wait()
+    def copy_tail(dest, out):
+        at = pl.multiple_of(dest * gw, LANES)
+        b_at = pl.multiple_of(dest * STATE, LANES)
+        c_at = pl.multiple_of(half + dest * STATE, LANES)
+        copy(tail_ref.at[:, pl.ds(at, gw)], out.at[:, 0:gw])
+        copy(bcv_ref.at[last, pl.ds(b_at, STATE)], out.at[:, gw : gw + STATE])
+        copy(bcv_ref.at[last, pl.ds(c_at, STATE)], out.at[:, gw + STATE : gw + 2 * STATE])
+
     for k in (2, 3, 1):
         out = outs.pop(0)
         at = pl.multiple_of((rank ^ k) * STATE, STATE)
@@ -89,34 +95,47 @@
         at = pl.multiple_of(half + (rank ^ k) * STATE, STATE)
         copy(bcv_ref.at[:, pl.ds(at, STATE)], out.at[:, STATE : 2 * STATE])
         copy(dtv_ref, out.at[:, 2 * STATE : 2 * STATE + LANES])
-        x_fetches[k].wait()
-        first = 2 * STATE + LANES
-        for j in range(rows // HALO):
-            tail = xv_ref.at[k - 1, pl.ds(rows - HALO, HALO), pl.ds(j * fold, fold)]
-            copy(tail, out.at[pl.ds(j * HALO, HALO), first : first + fold])
-        size = gw if k == 1 else chunks[0]
-        copy(xv_ref.at[k - 1, :, pl.ds(0, size)], out.at[:, first + fold : first + fold + size])
-    done = chunks[0]
-    for size in chunks[1:]:
-        for k in (2, 3):
-            copy(xv_ref.at[k - 1, :, pl.ds(done, size)], outs.pop(0))
-        done += size
-    out = outs.pop(0)
-    b_at = pl.multiple_of(rank * STATE, LANES)
-    c_at = pl.multiple_of(half + rank * STATE, LANES)
-    copy(bcv_ref.at[last, pl.ds(b_at, STATE)], out.at[:, gw : gw + STATE])
-    copy(bcv_ref.at[last, pl.ds(c_at, STATE)], out.at[:, gw + STATE : gw + 2 * STATE])
-    tail_fetch.wait()
-    copy(tail_ref, out.at[:, 0:gw])
+    first = 2 * STATE + LANES
+    for j in range(rows // HALO):
+        at = pl.multiple_of((rank ^ 1) * gw + j * fold, LANES)
+        copy(tail_ref.at[:, pl.ds(at, fold)], out.at[pl.ds(j * HALO, HALO), first : first + fold])
+    fetches[3].wait()
+    copy(xv_ref, out.at[:, first + fold : first + fold + gw])
+    for k in (2, 3, 0):
+        copy_tail(rank ^ k, outs.pop(0))
     for made in copies:
         made.wait()
 
 
-def relay_kernel(team, gw, rank_ref, tail_ref, *refs):
-    got = refs[: team - 1]
-    out_ref, sems = refs[team - 1 :]
+def chunk_kernel(chunks, gw, rank_ref, x_ref, after_ref, *refs):
+    xv_ref, in_sems, out_sems = refs[-3:]
+    outs = list(refs[:-3])
     rank = rank_ref[0]
-    rows = got[0].shape[0]
+    fetches, copies = [], []
+    for i, k in enumerate((2, 3)):
+        at = pl.multiple_of((rank ^ k) * gw, LANES)
+        made = pltpu.make_async_copy(x_ref.at[:, pl.ds(at, gw)], xv_ref.at[i], in_sems.at[i])
+        made.start()
+        fetches.append(made)
+    for made in fetches:
+        made.wait()
+    done = 0
+    for size in chunks:
+        for i in range(2):
+            src = xv_ref.at[i, :, pl.ds(done, size)]
+            made = pltpu.make_async_copy(src, outs.pop(0), out_sems.at[len(copies)])
+            made.start()
+            copies.append(made)
+        done += size
+    for made in copies:
+        made.wait()
+
+
+def relay_kernel(team, gw, rank_ref, tail_ref, near_ref, *refs):
+    others = {0: tail_ref, 2: refs[0], 3: refs[1]}
+    out_ref, sems = refs[-2:]
+    rank = rank_ref[0]
+    rows = near_ref.shape[0]
     fold = gw * HALO // rows
     tail = pl.ds(rows - HALO, HALO)
 
@@ -129,20 +148,20 @@
         for made in copies:
             made.wait()
 
-    @pl.when(rank == team - 1)
-    def _():
-        out_ref[...] = tail_ref[...]
-
-    for k in range(1, team):
+    for k, ref in others.items():
 
         @pl.when(rank ^ k == team - 1)
         def _():
-            first = 2 * STATE + LANES
-            pairs = [(got[k - 1].at[tail, 0 : 2 * STATE], out_ref.at[:, gw : gw + 2 * STATE])]
-            for j in range(rows // HALO):
-                src = got[k - 1].at[pl.ds(j * HALO, HALO), first : first + fold]
-                pairs.append((src, out_ref.at[:, j * fold : (j + 1) * fold]))
-            copy_all(pairs)
+            copy_all([(ref, out_ref)])
+
+    @pl.when(rank ^ 1 == team - 1)
+    def _():
+        first = 2 * STATE + LANES
+        pairs = [(near_ref.at[tail, 0 : 2 * STATE], out_ref.at[:, gw : gw + 2 * STATE])]
+        for j in range(rows // HALO):
+            src = near_ref.at[pl.ds(j * HALO, HALO), first : first + fold]
+            pairs.append((src, out_ref.at[:, j * fold : (j + 1) * fold]))
+        copy_all(pairs)
 
 
 def column_of(row):
@@ -331,6 +350,7 @@
     spread_v = spreader(first, width, hdim, own_heads, False)
     spread_u = spreader(first, width, hdim, own_heads, True)
     rows_ref[...] = jnp.dot(row_ref[...], spread_v, preferred_element_type=F32)
+    stat_refs = refs[1:2] if start else []
     sums = jnp.zeros((DOCS, 3 * LANES), F32)
     for k in (1, 2, 3, 0):
         tile = rank ^ k
@@ -362,22 +382,22 @@
     out = jnp.zeros((DOCS, LANES), F32)
     for i in range(3):
         out = jnp.where(lane == i, jnp.sum(sums[:, i * LANES : (i + 1) * LANES], axis=1, keepdims=True), out)
+    for ref in stat_refs:
+        out = out + ref[...]
     stat_ref[...] = out
     near.wait()
 
 
-def sum_kernel(rank_ref, *refs):
-    total = refs[0][...]
-    for ref in refs[1:-1]:
-        total = total + ref[...]
-    refs[-1][...] = total
+def add_kernel(rank_ref, one_ref, other_ref, *refs):
+    refs[-1][...] = one_ref[...] + other_ref[...]
 
 
 def norm_kernel(blocks, rank_ref, *refs):
     y_count = sum(len(block) for block in blocks)
     z_ref, gain_ref = refs[y_count : y_count + 2]
-    out_ref, gated_ref = refs[-2:]
+    out_ref, done_ref, gated_ref = refs[-3:]
     width = z_ref.shape[1]
+    done_ref[...] = jnp.zeros_like(done_ref)
     for step, block in enumerate(blocks):
 
         @pl.when(pl.program_id(0) == step)
@@ -431,27 +451,27 @@
         return lax.ppermute(array, "seq", [(i, i ^ k) for i in range(members)])
 
     def onward(array):
-        return lax.ppermute(array, "seq", [(i, i + team) for i in range(members - team)])
+        return lax.ppermute(array, "seq", [(i, (i + team) % members) for i in range(members)])
 
     shape = jax.ShapeDtypeStruct
     bcd_w = 2 * STATE + LANES
     lead_w = bcd_w + gw * HALO // rows
-    widths = [lead_w + chunks[0]] * 2 + [lead_w + gw] + [size for size in chunks[1:] for _ in range(2)]
+    widths = [bcd_w] * 2 + [lead_w + gw]
     halo_shape = (HALO, gw + 2 * STATE)
     packed = call(
-        functools.partial(pack_kernel, team, chunks, gw),
+        functools.partial(pack_kernel, team, gw),
         rank,
         (x_stream, bc_stream, dt_raw),
         [ANY] * 3,
-        [shape((rows, width), BF16) for width in widths] + [shape(halo_shape, BF16)],
-        [ANY] * (len(widths) + 1),
+        [shape((rows, width), BF16) for width in widths] + [shape(halo_shape, BF16)] * 3,
+        [ANY] * (len(widths) + 3),
         [
-            pltpu.VMEM((team - 1, rows, gw), BF16),
-            pltpu.VMEM((HALO, gw), BF16),
+            pltpu.VMEM((rows, gw), BF16),
+            pltpu.VMEM((HALO, inner), BF16),
             pltpu.VMEM(bc_stream.shape, BF16),
             pltpu.VMEM(dt_raw.shape, BF16),
-            pltpu.SemaphoreType.DMA((2 + team,)),
-            pltpu.SemaphoreType.DMA((3 * (4 + rows // HALO) + 2 * len(chunks) + 3,)),
+            pltpu.SemaphoreType.DMA((4,)),
+            pltpu.SemaphoreType.DMA((9 + rows // HALO + 1 + 9,)),
         ],
         "pack",
         cost=cost(2),
@@ -459,9 +479,22 @@
     )
     near = swap(packed[2], 1)
     lead = [near, swap(packed[0], 2), swap(packed[1], 3)]
-    got = [lead]
-    for q in range(1, len(chunks)):
-        got.append([near, swap(packed[1 + 2 * q], 2), swap(packed[2 + 2 * q], 3)])
+    x_parts = call(
+        functools.partial(chunk_kernel, chunks, gw),
+        rank,
+        (x_stream, near),
+        [ANY] * 2,
+        [shape((rows, size), BF16) for size in chunks for _ in range(2)],
+        [ANY] * (2 * len(chunks)),
+        [
+            pltpu.VMEM((2, rows, gw), BF16),
+            pltpu.SemaphoreType.DMA((2,)),
+            pltpu.SemaphoreType.DMA((2 * len(chunks),)),
+        ],
+        "chunks",
+        cost=cost(2),
+    )
+    got = [[near, swap(x_parts[2 * q], 2), swap(x_parts[2 * q + 1], 3)] for q in range(len(chunks))]
 
     ext_docs = jnp.concatenate([jnp.full((LANES,), -1, jnp.int32), doc_ids])
     docs = lax.dynamic_slice_in_dim(ext_docs, (me // team) * SPAN, SPAN + LANES).astype(F32)[None]
@@ -485,8 +518,8 @@
         call(
             functools.partial(relay_kernel, team, gw),
             rank,
-            (packed[-1], *lead),
-            [whole(halo_shape)] + [ANY] * (team - 1),
+            (packed[5], near, swap(packed[3], 2), swap(packed[4], 3)),
+            [ANY] * 4,
             shape(halo_shape, BF16),
             whole(halo_shape),
             [pltpu.SemaphoreType.DMA((1 + rows // HALO,))],
@@ -535,9 +568,8 @@
 
     def mix(q, after):
         start, size = sum(chunks[:q]), chunks[q]
-        far = lead_w if q == 0 else 0
         xc, y_local, fresh = call(
-            functools.partial(mix_kernel, team, taps, hdim, gw, start, (lead_w + start, far, far)),
+            functools.partial(mix_kernel, team, taps, hdim, gw, start, (lead_w + start, 0, 0)),
             rank,
             (x_stream, *got[q], halo, shift, wb, scores, b_turned, uv, row_pack, *after),
             [ANY]
@@ -573,9 +605,9 @@
                 state = onward((fresh.astype(F32) + kept * state.astype(F32)).astype(BF16))
         return state, y_local, xc
 
-    def carry(q, mixed, y_near, after):
+    def carry(q, mixed, y_near, stats, after):
         start, size = sum(chunks[:q]), chunks[q]
-        before = [y_near] if q else []
+        before = [y_near, stats] if q else []
         return call(
             functools.partial(carry_kernel, team, start, hdim),
             rank,
@@ -589,7 +621,8 @@
                 whole((16, LANES)),
                 whole(docs.shape),
             ]
-            + [ANY] * (len(before) + len(after)),
+            + ([ANY, whole((DOCS, LANES))] if q else [])
+            + [ANY] * len(after),
             [shape((rows, size), BF16), shape((rows, gw), BF16)]
             + [shape((rows, size), BF16)] * 2
             + [shape((DOCS, LANES), F32)],
@@ -600,34 +633,17 @@
             aliases={8: 1} if q else {},
         )
 
-    y_own, y_far, y_across, stats, y_near = [], [], [], [], None
+    y_own, y_far, y_across, stats, y_near = [], [], [], None, None
     ready = [mix(0, []), mix(1, [])]
     for q in range(len(chunks)):
         after = [y_far[q - 1], y_across[q - 1]] if q else []
-        own, y_near, far, across, sums = carry(q, ready[q], y_near, after)
+        own, y_near, far, across, stats = carry(q, ready[q], y_near, stats, after)
         y_own.append(own)
         y_far.append(swap(far, 2))
         y_across.append(swap(across, 3))
-        stats.append(sums)
         if q + 2 < len(chunks):
-            ready.append(mix(q + 2, [sums]))
+            ready.append(mix(q + 2, [stats]))
     y_near = swap(y_near, 1)
-
-    stats = call(
-        sum_kernel,
-        rank,
-        tuple(stats),
-        [whole((DOCS, LANES))] * len(stats),
-        shape((DOCS, LANES), F32),
-        whole((DOCS, LANES)),
-        [],
-        "sums",
-        cost=cost(0.1),
-    )
-    step = 1
-    while step < members:
-        stats = stats + swap(stats, step)
-        step *= 2
 
     gain = norm_gain[None]
 
@@ -645,17 +661,38 @@
             [whole(array.shape) for array in parts]
             + [place, pl.BlockSpec((1, gw), lambda i, pref: (0, pref[0] ^ (first + i)))]
             + [ANY] * len(before),
-            shape((rows, inner), BF16),
-            place,
+            [shape((rows, inner), BF16), shape((8, LANES), F32)],
+            [place, whole((8, LANES))],
             [pltpu.VMEM((rows, gw), F32)],
             "norm",
             grid=(len(blocks),),
-            cost=cost(0.2),
+            cost=cost(2),
             aliases={len(parts) + 3: 0} if before else {},
         )
 
-    mixed = norm([y_own, [y_near]], 0, [])
-    mixed = norm([y_far, y_across], 2, [mixed])
+    mixed, near_done = norm([y_own, [y_near]], 0, [])
+    mixed, far_done = norm([y_far, y_across], 2, [mixed])
+
+    steps = [1 << place for place in range((members - 1).bit_length())]
+    within = (team - 1).bit_length()
+    flips = steps[within:] + steps[:within]
+    for i, flip in enumerate(flips):
+        came = swap(stats, flip)
+        after = {len(flips) - 3: [near_done], len(flips) - 2: [far_done]}.get(i, [])
+        if after:
+            stats = call(
+                add_kernel,
+                rank,
+                (stats, came, *after),
+                [whole((DOCS, LANES))] * 2 + [ANY] * len(after),
+                shape((DOCS, LANES), F32),
+                whole((DOCS, LANES)),
+                [],
+                "add",
+                cost=cost(0.1),
+            )
+        else:
+            stats = stats + came
     doc_cosine = stats[:, 0] / jnp.sqrt(stats[:, 1] * stats[:, 2] + 1e-06)
     return (mixed, doc_cosine)
 

time: 97 us -> 80.7 us (0.83)
  waiting for transfers between devices: 38.3 us -> 28.5 us
  starting transfers between devices: 32.6 us -> 26.7 us
    ppermute x18 -> x22, waiting for transfers between devices: 36.4 us -> 26.4 us  [swap(): return lax.ppermute(array, 'seq', [(i, i ^ k) for i in range(members)])]
    ppermute x4, starting transfers between devices: 15.1 us -> 7.31 us  [onward(): lax.ppermute(array, 'seq', [(i, (i + team) % members) for i in range(memb...]
    ppermute x18 -> x22, starting transfers between devices: 17.6 us -> 19.4 us  [swap(): return lax.ppermute(array, 'seq', [(i, i ^ k) for i in range(members)])]
    pallas_call x13 -> x15, Pallas kernels: 22.8 us -> 23.3 us  [call(): pl.pallas_call(kernel, grid_spec=pltpu.PrefetchScalarGridSpec(num_scalar_...]
  transfers between devices with their start and end apart: 22 -> 26, of which waited for: 9 -> 14; matrix products, arithmetic and copies ran while one was open for 1% -> 0% of each run, Pallas kernels for 17% -> 23%
where the time goes in v3:
time: 80.7 us; the launch traced here: 80.5 us
  waiting for transfers between devices  28.5 us (35%)
  starting transfers between devices  26.7 us (33%)
  Pallas kernels  23.3 us (29%)
  other arithmetic  0.94 us (1%)
  between operations  0.9 us (1%)
    ppermute x22, waiting for transfers between devices, swap(): return lax.ppermute(array, 'seq', [(i, i ^ k) for i in range(members)])  26.4 us
    pallas_call x15, Pallas kernels, call(): pl.pallas_call(kernel, grid_spec=pltpu.PrefetchScalarGridSpec(num_scalar_...  23.3 us
    ppermute x22, starting transfers between devices, swap(): return lax.ppermute(array, 'seq', [(i, i ^ k) for i in range(members)])  19.4 us
    ppermute x4, starting transfers between devices, onward(): lax.ppermute(array, 'seq', [(i, (i + team) % members) for i in range(memb...  7.31 us
    ppermute x4, waiting for transfers between devices, onward(): lax.ppermute(array, 'seq', [(i, (i + team) % members) for i in range(memb...  2.12 us
  transfers between devices with their start and end apart: 26, of which 14 were waited for; matrix products, arithmetic and copies ran while one was open for 0% of the time, Pallas kernels for 23%

profile of v3, /device:TPU:0, one launch (start us, length us, event | category | flops | bytes accessed | tf_op | source)
XLA Modules:
  0.0 80.5 jit_solution(15764812075508821121)
XLA Ops:
  0.7 2.5 %pack.1 = (bf16[128,640]{1,0:T(8,128)(2,1)}, bf16[128,640]{1,0:T(8,128)(2,1)}, bf16[128,2944]{1,0:T(8,128)(2,1)}, bf16[16,2560]{1,0:T(8,128)(2,1)}, bf16[16,2560]{1,0:T(8,128)(2,1)}, /*index=5*/bf16[16,2560]{1,0:T(8,128)(2,1)}) custom-call(s32[1]{0:T(128)} %bitcast.rank_ref, bf16[128,8192]{1,0:T(8,128)(2,1)} %refs_0_.5, bf16[128,2048]{1,0:T(8,128)(2,1)} %bc_ref.3, ...), custom_call_target="tpu_custom_call" | custom-call | flops 2000000000 | bytes 6000000 | tf_op jit(solution)/shard_map/pack/pallas_call | solution.py:33
  3.3 0.5 collective-permute-start
  3.8 2.6 %collective-permute-start.3 = (bf16[16,2560]{1,0:T(8,128)(2,1)}, bf16[16,2560]{1,0:T(8,128)(2,1)S(1)}, u32[]{:S(2)}, u32[]{:S(2)}) collective-permute-start(bf16[16,2560]{1,0:T(8,128)(2,1)} %get-tuple-element.51), channel_id=1, source_target_pairs={{0,2},{1,3},{2,0},{3,1},{4,6},{5,7},{6,4},{7,5},{8,10},{9,11},{10,... | collective-permute-start | bytes 245768 | tf_op jit(solution)/shard_map/ppermute | solution.py:451
  6.4 1.7 %collective-permute-start.6 = (bf16[128,640]{1,0:T(8,128)(2,1)}, bf16[128,640]{1,0:T(8,128)(2,1)S(1)}, u32[]{:S(2)}, u32[]{:S(2)}) collective-permute-start(bf16[128,640]{1,0:T(8,128)(2,1)} %get-tuple-element.53), channel_id=1, source_target_pairs={{0,2},{1,3},{2,0},{3,1},{4,6},{5,7},{6,4},{7,5},{8,10},{9,11},{10,... | collective-permute-start | bytes 491528 | tf_op jit(solution)/shard_map/ppermute | solution.py:451
  8.6 0.1 shift.1.refs_4_.refs_5_
  8.7 0.9 %collective-permute-done.3.refs_0_ = bf16[16,2560]{1,0:T(8,128)(2,1)S(1)} collective-permute-done((bf16[16,2560]{1,0:T(8,128)(2,1)}, bf16[16,2560]{1,0:T(8,128)(2,1)S(1)}, u32[]{:S(2)}, u32[]{:S(2)}) %collective-permute-start.3) | collective-permute-done | bytes 81952 | tf_op jit(solution)/shard_map/ppermute | solution.py:451
  9.6 1.6 %collective-permute-done.4.refs_1_ = bf16[16,2560]{1,0:T(8,128)(2,1)S(1)} collective-permute-done((bf16[16,2560]{1,0:T(8,128)(2,1)}, bf16[16,2560]{1,0:T(8,128)(2,1)S(1)}, u32[]{:S(2)}, u32[]{:S(2)}) %collective-permute-start.4) | collective-permute-done | bytes 81952 | tf_op jit(solution)/shard_map/ppermute | solution.py:451
  11.2 0.2 relay.1
  11.4 1.7 %collective-permute-start.5 = (bf16[16,2560]{1,0:T(8,128)(2,1)S(1)}, bf16[16,2560]{1,0:T(8,128)(2,1)S(1)}, u32[]{:S(2)}, u32[]{:S(2)}) collective-permute-start(bf16[16,2560]{1,0:T(8,128)(2,1)S(1)} %relay.1), channel_id=1, source_target_pairs={{0,4},{1,5},{2,6},{3,7},{4,8},{5,9},{6,10},{7,11},{8,12},{9,13},{1... | collective-permute-start | bytes 245768 | tf_op jit(solution)/shard_map/ppermute | solution.py:454
  13.2 0.3 chunks.1
  13.5 1.4 %collective-permute-start.1 = (bf16[128,512]{1,0:T(8,128)(2,1)S(1)}, bf16[128,512]{1,0:T(8,128)(2,1)S(1)}, u32[]{:S(2)}, u32[]{:S(2)}) collective-permute-start(bf16[128,512]{1,0:T(8,128)(2,1)S(1)} %get-tuple-element.48), channel_id=1, source_target_pairs={{0,2},{1,3},{2,0},{3,1},{4,6},{5,7},{6,4},{7,5},{8,10},{9,11},{10,... | collective-permute-start | bytes 393224 | tf_op jit(solution)/shard_map/ppermute | solution.py:451
  14.9 0.2 collective-permute-start.2
  15.1 0.1 collective-permute-done.6.refs_1_
  15.2 1.9 %collective-permute-start.10 = (bf16[128,768]{1,0:T(8,128)(2,1)S(1)}, bf16[128,768]{1,0:T(8,128)(2,1)S(1)}, u32[]{:S(2)}, u32[]{:S(2)}) collective-permute-start(bf16[128,768]{1,0:T(8,128)(2,1)S(1)} %get-tuple-element.64), channel_id=1, source_target_pairs={{0,2},{1,3},{2,0},{3,1},{4,6},{5,7},{6,4},{7,5},{8,10},{9,11},{10,... | collective-permute-start | bytes 589832 | tf_op jit(solution)/shard_map/ppermute | solution.py:451
  17.1 1.1 %collective-permute-done.7.refs_2_ = bf16[128,640]{1,0:T(8,128)(2,1)S(1)} collective-permute-done((bf16[128,640]{1,0:T(8,128)(2,1)}, bf16[128,640]{1,0:T(8,128)(2,1)S(1)}, u32[]{:S(2)}, u32[]{:S(2)}) %collective-permute-start.7) | collective-permute-done | bytes 163872 | tf_op jit(solution)/shard_map/ppermute | solution.py:451
  18.2 1.8 %collective-permute-start.11 = (bf16[128,768]{1,0:T(8,128)(2,1)S(1)}, bf16[128,768]{1,0:T(8,128)(2,1)S(1)}, u32[]{:S(2)}, u32[]{:S(2)}) collective-permute-start(bf16[128,768]{1,0:T(8,128)(2,1)S(1)} %get-tuple-element.65), channel_id=1, source_target_pairs={{0,3},{1,2},{2,1},{3,0},{4,7},{5,6},{6,5},{7,4},{8,11},{9,10},{10,... | collective-permute-start | bytes 589832 | tf_op jit(solution)/shard_map/ppermute | solution.py:451
  20.0 0.1 collective-permute-start.15
  20.2 2.5 %bc.1 = (bf16[512,512]{1,0:T(8,128)(2,1)S(1)}, bf16[256,512]{1,0:T(8,128)(2,1)S(1)}, bf16[512,256]{1,0:T(8,128)(2,1)S(1)}, bf16[512,128]{1,0:T(8,128)(2,1)S(1)}, bf16[16,128]{1,0:T(8,128)(2,1)S(1)}) custom-call(s32[1]{0:T(128)} %bitcast.rank_ref, bf16[128,2048]{1,0:T(8,128)(2,1)S(1)} %copy-done.2, bf16[128,128]{1,0:T(8,128)(2,1)S(1)} %copy-done.3, ...), custom_call_target="tpu_custom_call" | custom-call | flops 4000000000 | bytes 12000000 | tf_op jit(solution)/shard_map/bc/pallas_call | solution.py:33
  22.7 1.1 %collective-permute-start.16 = (bf16[128,768]{1,0:T(8,128)(2,1)S(1)}, bf16[128,768]{1,0:T(8,128)(2,1)S(1)}, u32[]{:S(2)}, u32[]{:S(2)}) collective-permute-start(bf16[128,768]{1,0:T(8,128)(2,1)S(1)} %get-tuple-element.74), channel_id=1, source_target_pairs={{0,3},{1,2},{2,1},{3,0},{4,7},{5,6},{6,5},{7,4},{8,11},{9,10},{10,... | collective-permute-start | bytes 589832 | tf_op jit(solution)/shard_map/ppermute | solution.py:451
  23.8 2.4 %mix.3 = (bf16[512,512]{1,0:T(8,128)(2,1)S(1)}, f32[512,512]{1,0:T(8,128)S(1)}, bf16[256,512]{1,0:T(8,128)(2,1)S(1)}) custom-call(s32[1]{0:T(128)} %bitcast.rank_ref, bf16[128,8192]{1,0:T(8,128)(2,1)S(1)} %copy-done, bf16[128,2944]{1,0:T(8,128)(2,1)S(1)} %collective-permute-done.after_ref.near_ref.refs_0_.refs_1_, ...), custom_call_target="tpu_custom_call" | custom-call | flops 4000000000 | bytes 12000000 | tf_op jit(solution)/shard_map/mix/pallas_call | solution.py:33
  26.2 1.8 %collective-permute-start.8 = (bf16[256,512]{1,0:T(8,128)(2,1)S(1)}, bf16[256,512]{1,0:T(8,128)(2,1)S(1)}, u32[]{:S(2)}, u32[]{:S(2)}) collective-permute-start(bf16[256,512]{1,0:T(8,128)(2,1)S(1)} %get-tuple-element.59), channel_id=1, source_target_pairs={{0,4},{1,5},{2,6},{3,7},{4,8},{5,9},{6,10},{7,11},{8,12},{9,13},{1... | collective-permute-start | bytes 786440 | tf_op jit(solution)/shard_map/ppermute | solution.py:454
  28.0 0.5 collective-permute-done.10.refs_2_
  28.5 3.6 %collective-permute-done.11.refs_3_ = bf16[128,768]{1,0:T(8,128)(2,1)S(1)} collective-permute-done((bf16[128,768]{1,0:T(8,128)(2,1)S(1)}, bf16[128,768]{1,0:T(8,128)(2,1)S(1)}, u32[]{:S(2)}, u32[]{:S(2)}) %collective-permute-start.11) | collective-permute-done | bytes 196640 | tf_op jit(solution)/shard_map/ppermute | solution.py:451
  32.2 3.1 %mix.4 = (bf16[512,768]{1,0:T(8,128)(2,1)S(1)}, f32[512,768]{1,0:T(8,128)S(1)}, bf16[256,768]{1,0:T(8,128)(2,1)S(1)}) custom-call(s32[1]{0:T(128)} %bitcast.rank_ref, bf16[128,8192]{1,0:T(8,128)(2,1)S(1)} %copy-done, bf16[128,2944]{1,0:T(8,128)(2,1)S(1)} %collective-permute-done.after_ref.near_ref.refs_0_.refs_1_, ...), custom_call_target="tpu_custom_call" | custom-call | flops 4000000000 | bytes 12000000 | tf_op jit(solution)/shard_map/mix/pallas_call | solution.py:33
  35.3 1.8 %collective-permute-start.12 = (bf16[256,768]{1,0:T(8,128)(2,1)S(1)}, bf16[256,768]{1,0:T(8,128)(2,1)S(1)}, u32[]{:S(2)}, u32[]{:S(2)}) collective-permute-start(bf16[256,768]{1,0:T(8,128)(2,1)S(1)} %get-tuple-element.66), channel_id=1, source_target_pairs={{0,4},{1,5},{2,6},{3,7},{4,8},{5,9},{6,10},{7,11},{8,12},{9,13},{1... | collective-permute-start | bytes 1179656 | tf_op jit(solution)/shard_map/ppermute | solution.py:454
  37.1 1.6 %carry.3 = (bf16[128,512]{1,0:T(8,128)(2,1)S(1)}, bf16[128,2048]{1,0:T(8,128)(2,1)S(1)}, bf16[128,512]{1,0:T(8,128)(2,1)S(1)}, bf16[128,512]{1,0:T(8,128)(2,1)S(1)}, f32[16,128]{1,0:T(8,128)S(1)}) custom-call(s32[1]{0:T(128)} %bitcast.rank_ref, bf16[256,512]{1,0:T(8,128)(2,1)S(1)} %collective-permute-done.8.st_ref, f32[512,512]{1,0:T(8,128)S(1)} %get-tuple-element.60.yl_ref, ...), custom_call_target="tpu_custom_call" | custom-call | flops 3000000000 | bytes 9000000 | tf_op jit(solution)/shard_map/carry/pallas_call | solution.py:33
  38.8 1.5 %collective-permute-start.9 = (bf16[128,512]{1,0:T(8,128)(2,1)S(1)}, bf16[128,512]{1,0:T(8,128)(2,1)S(1)}, u32[]{:S(2)}, u32[]{:S(2)}) collective-permute-start(bf16[128,512]{1,0:T(8,128)(2,1)S(1)} %get-tuple-element.63), channel_id=1, source_target_pairs={{0,2},{1,3},{2,0},{3,1},{4,6},{5,7},{6,4},{7,5},{8,10},{9,11},{10,... | collective-permute-start | bytes 393224 | tf_op jit(solution)/shard_map/ppermute | solution.py:451
  40.3 0.4 collective-permute-start.13
  40.6 3.1 %mix.5 = (bf16[512,768]{1,0:T(8,128)(2,1)S(1)}, f32[512,768]{1,0:T(8,128)S(1)}, bf16[256,768]{1,0:T(8,128)(2,1)S(1)}) custom-call(s32[1]{0:T(128)} %bitcast.rank_ref, bf16[128,8192]{1,0:T(8,128)(2,1)S(1)} %copy-done, bf16[128,2944]{1,0:T(8,128)(2,1)S(1)} %collective-permute-done.after_ref.near_ref.refs_0_.refs_1_, ...), custom_call_target="tpu_custom_call" | custom-call | flops 4000000000 | bytes 12000000 | tf_op jit(solution)/shard_map/mix/pallas_call | solution.py:33
  43.7 2.0 %collective-permute-start.17 = (bf16[256,768]{1,0:T(8,128)(2,1)S(1)}, bf16[256,768]{1,0:T(8,128)(2,1)S(1)}, u32[]{:S(2)}, u32[]{:S(2)}) collective-permute-start(bf16[256,768]{1,0:T(8,128)(2,1)S(1)} %get-tuple-element.75), channel_id=1, source_target_pairs={{0,4},{1,5},{2,6},{3,7},{4,8},{5,9},{6,10},{7,11},{8,12},{9,13},{1... | collective-permute-start | bytes 1179656 | tf_op jit(solution)/shard_map/ppermute | solution.py:454
  45.7 1.3 %collective-permute-done.13.refs_3_ = bf16[128,512]{1,0:T(8,128)(2,1)S(1)} collective-permute-done((bf16[128,512]{1,0:T(8,128)(2,1)S(1)}, bf16[128,512]{1,0:T(8,128)(2,1)S(1)}, u32[]{:S(2)}, u32[]{:S(2)}) %collective-permute-start.13) | collective-permute-done | bytes 131104 | tf_op jit(solution)/shard_map/ppermute | solution.py:451
  47.0 2.1 %collective-permute-done.12.st_ref = bf16[256,768]{1,0:T(8,128)(2,1)S(1)} collective-permute-done((bf16[256,768]{1,0:T(8,128)(2,1)S(1)}, bf16[256,768]{1,0:T(8,128)(2,1)S(1)}, u32[]{:S(2)}, u32[]{:S(2)}) %collective-permute-start.12) | collective-permute-done | bytes 393248 | tf_op jit(solution)/shard_map/ppermute | solution.py:454
  49.1 1.9 %carry.4 = (bf16[128,768]{1,0:T(8,128)(2,1)S(1)}, bf16[128,2048]{1,0:T(8,128)(2,1)S(1)}, bf16[128,768]{1,0:T(8,128)(2,1)S(1)}, bf16[128,768]{1,0:T(8,128)(2,1)S(1)}, f32[16,128]{1,0:T(8,128)S(1)}) custom-call(s32[1]{0:T(128)} %bitcast.rank_ref, bf16[256,768]{1,0:T(8,128)(2,1)S(1)} %collective-permute-done.12.st_ref, ...), custom_call_target="tpu_custom_call", output_to_operand_aliasing={{1}: (8, {})} | custom-call | flops 3000000000 | bytes 9000000 | tf_op jit(solution)/shard_map/carry/pallas_call | solution.py:33
  51.0 1.6 %collective-permute-start.14 = (bf16[128,768]{1,0:T(8,128)(2,1)S(1)}, bf16[128,768]{1,0:T(8,128)(2,1)S(1)}, u32[]{:S(2)}, u32[]{:S(2)}) collective-permute-start(bf16[128,768]{1,0:T(8,128)(2,1)S(1)} %get-tuple-element.72), channel_id=1, source_target_pairs={{0,2},{1,3},{2,0},{3,1},{4,6},{5,7},{6,4},{7,5},{8,10},{9,11},{10,... | collective-permute-start | bytes 589832 | tf_op jit(solution)/shard_map/ppermute | solution.py:451
  52.5 6.2 %collective-permute-done.14.refs_2_.refs_1_ = bf16[128,768]{1,0:T(8,128)(2,1)S(1)} collective-permute-done((bf16[128,768]{1,0:T(8,128)(2,1)S(1)}, bf16[128,768]{1,0:T(8,128)(2,1)S(1)}, u32[]{:S(2)}, u32[]{:S(2)}) %collective-permute-start.14) | collective-permute-done | bytes 196640 | tf_op jit(solution)/shard_map/ppermute | solution.py:451
  58.8 2.5 %collective-permute-done.18.refs_3_.refs_4_ = bf16[128,768]{1,0:T(8,128)(2,1)S(1)} collective-permute-done((bf16[128,768]{1,0:T(8,128)(2,1)S(1)}, bf16[128,768]{1,0:T(8,128)(2,1)S(1)}, u32[]{:S(2)}, u32[]{:S(2)}) %collective-permute-start.18) | collective-permute-done | bytes 196640 | tf_op jit(solution)/shard_map/ppermute | solution.py:451
  61.3 1.9 %carry.5 = (bf16[128,768]{1,0:T(8,128)(2,1)S(1)}, bf16[128,2048]{1,0:T(8,128)(2,1)S(1)}, bf16[128,768]{1,0:T(8,128)(2,1)S(1)}, bf16[128,768]{1,0:T(8,128)(2,1)S(1)}, f32[16,128]{1,0:T(8,128)S(1)}) custom-call(s32[1]{0:T(128)} %bitcast.rank_ref, bf16[256,768]{1,0:T(8,128)(2,1)S(1)} %collective-permute-done.17.st_ref, ...), custom_call_target="tpu_custom_call", output_to_operand_aliasing={{1}: (8, {})} | custom-call | flops 3000000000 | bytes 9000000 | tf_op jit(solution)/shard_map/carry/pallas_call | solution.py:33
  63.2 0.7 collective-permute-start.21
  64.0 1.5 %collective-permute-start.19 = (bf16[128,768]{1,0:T(8,128)(2,1)S(1)}, bf16[128,768]{1,0:T(8,128)(2,1)S(1)}, u32[]{:S(2)}, u32[]{:S(2)}) collective-permute-start(bf16[128,768]{1,0:T(8,128)(2,1)S(1)} %get-tuple-element.81), channel_id=1, source_target_pairs={{0,2},{1,3},{2,0},{3,1},{4,6},{5,7},{6,4},{7,5},{8,10},{9,11},{10,... | collective-permute-start | bytes 589832 | tf_op jit(solution)/shard_map/ppermute | solution.py:451
  65.5 2.1 %collective-permute-done.22 = f32[16,128]{1,0:T(8,128)S(1)} collective-permute-done((f32[16,128]{1,0:T(8,128)S(1)}, f32[16,128]{1,0:T(8,128)S(1)}, u32[]{:S(2)}, u32[]{:S(2)}) %collective-permute-start.22) | collective-permute-done | bytes 8224 | tf_op jit(solution)/shard_map/ppermute | solution.py:451
  67.6 0.8 %collective-permute-start.23 = (f32[16,128]{1,0:T(8,128)S(1)}, f32[16,128]{1,0:T(8,128)S(1)}, u32[]{:S(2)}, u32[]{:S(2)}) collective-permute-start(f32[16,128]{1,0:T(8,128)S(1)} %add.24.one_ref), channel_id=1, source_target_pairs={{0,8},{1,9},{2,10},{3,11},{4,12},{5,13},{6,14},{7,15},{8,0},{9,1},... | collective-permute-start | bytes 24584 | tf_op jit(solution)/shard_map/ppermute | solution.py:451
  68.5 1.8 %norm.2 = (bf16[128,8192]{1,0:T(8,128)(2,1)}, f32[8,128]{1,0:T(8,128)S(1)}) custom-call(s32[1]{0:T(128)} %bitcast.rank_ref, bf16[128,512]{1,0:T(8,128)(2,1)S(1)} %get-tuple-element.83.refs_0_, bf16[128,768]{1,0:T(8,128)(2,1)S(1)} %get-tuple-element.84.refs_1_, bf16[128,768]{1,0:T(8,128)(2,1)S(1)} %get-tuple-element.85.refs_2_, ...), custom_call_target="tpu_custom_call" | custom-call | flops 2000000000 | bytes 6000000 | tf_op jit(solution)/shard_map/norm/pallas_call | solution.py:33
  70.3 1.9 %collective-permute-done.23.other_ref = f32[16,128]{1,0:T(8,128)S(1)} collective-permute-done((f32[16,128]{1,0:T(8,128)S(1)}, f32[16,128]{1,0:T(8,128)S(1)}, u32[]{:S(2)}, u32[]{:S(2)}) %collective-permute-start.23) | collective-permute-done | bytes 8224 | tf_op jit(solution)/shard_map/ppermute | solution.py:451
  72.2 2.2 %collective-permute-done.20.refs_5_ = bf16[128,768]{1,0:T(8,128)(2,1)S(1)} collective-permute-done((bf16[128,768]{1,0:T(8,128)(2,1)S(1)}, bf16[128,768]{1,0:T(8,128)(2,1)S(1)}, u32[]{:S(2)}, u32[]{:S(2)}) %collective-permute-start.20) | collective-permute-done | bytes 196640 | tf_op jit(solution)/shard_map/ppermute | solution.py:451
  74.3 1.8 %norm.3 = (bf16[128,8192]{1,0:T(8,128)(2,1)}, f32[8,128]{1,0:T(8,128)S(1)}) custom-call(s32[1]{0:T(128)} %bitcast.rank_ref, bf16[128,512]{1,0:T(8,128)(2,1)S(1)} %collective-permute-done.9.refs_2_.refs_0_, bf16[128,768]{1,0:T(8,128)(2,1)S(1)} %collective-permute-done.14.refs_2_.refs_1_, ...), custom_call_target="tpu_custom_call", output_to_operand_aliasing={{0}: (9, {})} | custom-call | flops 2000000000 | bytes 6000000 | tf_op jit(solution)/shard_map/norm/pallas_call | solution.py:33
  76.1 1.5 %collective-permute-start.25 = (f32[16,128]{1,0:T(8,128)S(1)}, f32[16,128]{1,0:T(8,128)S(1)}, u32[]{:S(2)}, u32[]{:S(2)}) collective-permute-start(f32[16,128]{1,0:T(8,128)S(1)} %add.36), channel_id=1, source_target_pairs={{0,2},{1,3},{2,0},{3,1},{4,6},{5,7},{6,4},{7,5},{8,10},{9,11},{10,... | collective-permute-start | bytes 24584 | tf_op jit(solution)/shard_map/ppermute | solution.py:451
  77.6 2.2 %collective-permute-done.25 = f32[16,128]{1,0:T(8,128)S(1)} collective-permute-done((f32[16,128]{1,0:T(8,128)S(1)}, f32[16,128]{1,0:T(8,128)S(1)}, u32[]{:S(2)}, u32[]{:S(2)}) %collective-permute-start.25) | collective-permute-done | bytes 8224 | tf_op jit(solution)/shard_map/ppermute | solution.py:451
  79.8 0.7 fusion.3
  (52 shorter events, 0.6 us)
Async XLA Ops:
  0.6 7.5 %copy-start.6 = (f32[4,10240]{1,0:T(4,128)S(1)}, f32[4,10240]{1,0:T(4,128)}, u32[]{:S(2)}) copy-start(f32[4,10240]{1,0:T(4,128)} %param.16) | copy-start | bytes 491524
  0.7 7.5 %copy-start.7 = (f32[10240]{0:T(1024)S(1)}, f32[10240]{0:T(1024)}, u32[]{:S(2)}) copy-start(f32[10240]{0:T(1024)} %param.17) | copy-start | bytes 122884
  0.7 7.6 %copy-start.8 = (s32[2048]{0:T(1024)S(1)}, s32[2048]{0:T(1024)}, u32[]{:S(2)}) copy-start(s32[2048]{0:T(1024)} %param.15) | copy-start | bytes 24580
  0.7 7.8 %copy-start.9 = (f32[128]{0:T(128)S(1)}, f32[128]{0:T(128)}, u32[]{:S(2)}) copy-start(f32[128]{0:T(128)} %param.20) | copy-start | bytes 1540
  0.7 7.8 %copy-start.10 = (f32[128]{0:T(128)S(1)}, f32[128]{0:T(128)}, u32[]{:S(2)}) copy-start(f32[128]{0:T(128)} %param.19) | copy-start | bytes 1540
  0.7 7.8 %copy-start.11 = (f32[128]{0:T(128)S(1)}, f32[128]{0:T(128)}, u32[]{:S(2)}) copy-start(f32[128]{0:T(128)} %param.18) | copy-start | bytes 1540
  3.3 7.9 %collective-permute-start = (bf16[128,2944]{1,0:T(8,128)(2,1)}, bf16[128,2944]{1,0:T(8,128)(2,1)S(1)}, u32[]{:S(2)}, u32[]{:S(2)}) collective-permute-start(bf16[128,2944]{1,0:T(8,128)(2,1)} %get-tuple-element.47), channel_id=1, source_target_pairs={{0,1},{1,0},{2,3},{3,2},{4,5},{5,4},{6,7},{7,6},{8,9},{9,8},{10,11... | collective-permute-start | bytes 2261000 | tf_op jit(solution)/shard_map/ppermute | solution.py:451
  3.8 5.8 %collective-permute-start.3 = (bf16[16,2560]{1,0:T(8,128)(2,1)}, bf16[16,2560]{1,0:T(8,128)(2,1)S(1)}, u32[]{:S(2)}, u32[]{:S(2)}) collective-permute-start(bf16[16,2560]{1,0:T(8,128)(2,1)} %get-tuple-element.51), channel_id=1, source_target_pairs={{0,2},{1,3},{2,0},{3,1},{4,6},{5,7},{6,4},{7,5},{8,10},{9,11},{10,... | collective-permute-start | bytes 245768 | tf_op jit(solution)/shard_map/ppermute | solution.py:451
  6.4 4.8 %collective-permute-start.4 = (bf16[16,2560]{1,0:T(8,128)(2,1)}, bf16[16,2560]{1,0:T(8,128)(2,1)S(1)}, u32[]{:S(2)}, u32[]{:S(2)}) collective-permute-start(bf16[16,2560]{1,0:T(8,128)(2,1)} %get-tuple-element.52), channel_id=1, source_target_pairs={{0,3},{1,2},{2,1},{3,0},{4,7},{5,6},{6,5},{7,4},{8,11},{9,10},{10,... | collective-permute-start | bytes 245768 | tf_op jit(solution)/shard_map/ppermute | solution.py:451
  6.4 8.7 %collective-permute-start.6 = (bf16[128,640]{1,0:T(8,128)(2,1)}, bf16[128,640]{1,0:T(8,128)(2,1)S(1)}, u32[]{:S(2)}, u32[]{:S(2)}) collective-permute-start(bf16[128,640]{1,0:T(8,128)(2,1)} %get-tuple-element.53), channel_id=1, source_target_pairs={{0,2},{1,3},{2,0},{3,1},{4,6},{5,7},{6,4},{7,5},{8,10},{9,11},{10,... | collective-permute-start | bytes 491528 | tf_op jit(solution)/shard_map/ppermute | solution.py:451
  8.2 10.0 %collective-permute-start.7 = (bf16[128,640]{1,0:T(8,128)(2,1)}, bf16[128,640]{1,0:T(8,128)(2,1)S(1)}, u32[]{:S(2)}, u32[]{:S(2)}) collective-permute-start(bf16[128,640]{1,0:T(8,128)(2,1)} %get-tuple-element.54), channel_id=1, source_target_pairs={{0,3},{1,2},{2,1},{3,0},{4,7},{5,6},{6,5},{7,4},{8,11},{9,10},{10,... | collective-permute-start | bytes 491528 | tf_op jit(solution)/shard_map/ppermute | solution.py:451
  8.6 2.7 %copy-start.5 = (bf16[16,2560]{1,0:T(8,128)(2,1)S(1)}, bf16[16,2560]{1,0:T(8,128)(2,1)}, u32[]{:S(2)}) copy-start(bf16[16,2560]{1,0:T(8,128)(2,1)} %get-tuple-element.50.tail_ref) | copy-start | bytes 245764
  8.7 4.5 %copy-start = (bf16[128,8192]{1,0:T(8,128)(2,1)S(1)}, bf16[128,8192]{1,0:T(8,128)(2,1)}, u32[]{:S(2)}) copy-start(bf16[128,8192]{1,0:T(8,128)(2,1)} %refs_0_.5) | copy-start | bytes 6291460
  11.4 8.8 %copy-start.2 = (bf16[128,2048]{1,0:T(8,128)(2,1)S(1)}, bf16[128,2048]{1,0:T(8,128)(2,1)}, u32[]{:S(2)}) copy-start(bf16[128,2048]{1,0:T(8,128)(2,1)} %bc_ref.3) | copy-start | bytes 1572868
  11.4 8.7 %copy-start.3 = (bf16[128,128]{1,0:T(8,128)(2,1)S(1)}, bf16[128,128]{1,0:T(8,128)(2,1)}, u32[]{:S(2)}) copy-start(bf16[128,128]{1,0:T(8,128)(2,1)} %dt_ref.3) | copy-start | bytes 98308
  11.4 8.6 %collective-permute-start.5 = (bf16[16,2560]{1,0:T(8,128)(2,1)S(1)}, bf16[16,2560]{1,0:T(8,128)(2,1)S(1)}, u32[]{:S(2)}, u32[]{:S(2)}) collective-permute-start(bf16[16,2560]{1,0:T(8,128)(2,1)S(1)} %relay.1), channel_id=1, source_target_pairs={{0,4},{1,5},{2,6},{3,7},{4,8},{5,9},{6,10},{7,11},{8,12},{9,13},{1... | collective-permute-start | bytes 245768 | tf_op jit(solution)/shard_map/ppermute | solution.py:454
  13.5 9.2 %collective-permute-start.1 = (bf16[128,512]{1,0:T(8,128)(2,1)S(1)}, bf16[128,512]{1,0:T(8,128)(2,1)S(1)}, u32[]{:S(2)}, u32[]{:S(2)}) collective-permute-start(bf16[128,512]{1,0:T(8,128)(2,1)S(1)} %get-tuple-element.48), channel_id=1, source_target_pairs={{0,2},{1,3},{2,0},{3,1},{4,6},{5,7},{6,4},{7,5},{8,10},{9,11},{10,... | collective-permute-start | bytes 393224 | tf_op jit(solution)/shard_map/ppermute | solution.py:451
  14.9 8.9 %collective-permute-start.2 = (bf16[128,512]{1,0:T(8,128)(2,1)S(1)}, bf16[128,512]{1,0:T(8,128)(2,1)S(1)}, u32[]{:S(2)}, u32[]{:S(2)}) collective-permute-start(bf16[128,512]{1,0:T(8,128)(2,1)S(1)} %get-tuple-element.49), channel_id=1, source_target_pairs={{0,3},{1,2},{2,1},{3,0},{4,7},{5,6},{6,5},{7,4},{8,11},{9,10},{10,... | collective-permute-start | bytes 393224 | tf_op jit(solution)/shard_map/ppermute | solution.py:451
  15.2 13.3 %collective-permute-start.10 = (bf16[128,768]{1,0:T(8,128)(2,1)S(1)}, bf16[128,768]{1,0:T(8,128)(2,1)S(1)}, u32[]{:S(2)}, u32[]{:S(2)}) collective-permute-start(bf16[128,768]{1,0:T(8,128)(2,1)S(1)} %get-tuple-element.64), channel_id=1, source_target_pairs={{0,2},{1,3},{2,0},{3,1},{4,6},{5,7},{6,4},{7,5},{8,10},{9,11},{10,... | collective-permute-start | bytes 589832 | tf_op jit(solution)/shard_map/ppermute | solution.py:451
  18.2 13.9 %collective-permute-start.11 = (bf16[128,768]{1,0:T(8,128)(2,1)S(1)}, bf16[128,768]{1,0:T(8,128)(2,1)S(1)}, u32[]{:S(2)}, u32[]{:S(2)}) collective-permute-start(bf16[128,768]{1,0:T(8,128)(2,1)S(1)} %get-tuple-element.65), channel_id=1, source_target_pairs={{0,3},{1,2},{2,1},{3,0},{4,7},{5,6},{6,5},{7,4},{8,11},{9,10},{10,... | collective-permute-start | bytes 589832 | tf_op jit(solution)/shard_map/ppermute | solution.py:451
  20.0 20.6 %collective-permute-start.15 = (bf16[128,768]{1,0:T(8,128)(2,1)S(1)}, bf16[128,768]{1,0:T(8,128)(2,1)S(1)}, u32[]{:S(2)}, u32[]{:S(2)}) collective-permute-start(bf16[128,768]{1,0:T(8,128)(2,1)S(1)} %get-tuple-element.73), channel_id=1, source_target_pairs={{0,2},{1,3},{2,0},{3,1},{4,6},{5,7},{6,4},{7,5},{8,10},{9,11},{10,... | collective-permute-start | bytes 589832 | tf_op jit(solution)/shard_map/ppermute | solution.py:451
  22.7 17.9 %collective-permute-start.16 = (bf16[128,768]{1,0:T(8,128)(2,1)S(1)}, bf16[128,768]{1,0:T(8,128)(2,1)S(1)}, u32[]{:S(2)}, u32[]{:S(2)}) collective-permute-start(bf16[128,768]{1,0:T(8,128)(2,1)S(1)} %get-tuple-element.74), channel_id=1, source_target_pairs={{0,3},{1,2},{2,1},{3,0},{4,7},{5,6},{6,5},{7,4},{8,11},{9,10},{10,... | collective-permute-start | bytes 589832 | tf_op jit(solution)/shard_map/ppermute | solution.py:451
  26.2 10.9 %collective-permute-start.8 = (bf16[256,512]{1,0:T(8,128)(2,1)S(1)}, bf16[256,512]{1,0:T(8,128)(2,1)S(1)}, u32[]{:S(2)}, u32[]{:S(2)}) collective-permute-start(bf16[256,512]{1,0:T(8,128)(2,1)S(1)} %get-tuple-element.59), channel_id=1, source_target_pairs={{0,4},{1,5},{2,6},{3,7},{4,8},{5,9},{6,10},{7,11},{8,12},{9,13},{1... | collective-permute-start | bytes 786440 | tf_op jit(solution)/shard_map/ppermute | solution.py:454
  35.3 13.8 %collective-permute-start.12 = (bf16[256,768]{1,0:T(8,128)(2,1)S(1)}, bf16[256,768]{1,0:T(8,128)(2,1)S(1)}, u32[]{:S(2)}, u32[]{:S(2)}) collective-permute-start(bf16[256,768]{1,0:T(8,128)(2,1)S(1)} %get-tuple-element.66), channel_id=1, source_target_pairs={{0,4},{1,5},{2,6},{3,7},{4,8},{5,9},{6,10},{7,11},{8,12},{9,13},{1... | collective-permute-start | bytes 1179656 | tf_op jit(solution)/shard_map/ppermute | solution.py:454
  38.8 6.9 %collective-permute-start.9 = (bf16[128,512]{1,0:T(8,128)(2,1)S(1)}, bf16[128,512]{1,0:T(8,128)(2,1)S(1)}, u32[]{:S(2)}, u32[]{:S(2)}) collective-permute-start(bf16[128,512]{1,0:T(8,128)(2,1)S(1)} %get-tuple-element.63), channel_id=1, source_target_pairs={{0,2},{1,3},{2,0},{3,1},{4,6},{5,7},{6,4},{7,5},{8,10},{9,11},{10,... | collective-permute-start | bytes 393224 | tf_op jit(solution)/shard_map/ppermute | solution.py:451
  40.3 6.7 %collective-permute-start.13 = (bf16[128,512]{1,0:T(8,128)(2,1)S(1)}, bf16[128,512]{1,0:T(8,128)(2,1)S(1)}, u32[]{:S(2)}, u32[]{:S(2)}) collective-permute-start(bf16[128,512]{1,0:T(8,128)(2,1)S(1)} %get-tuple-element.71), channel_id=1, source_target_pairs={{0,3},{1,2},{2,1},{3,0},{4,7},{5,6},{6,5},{7,4},{8,11},{9,10},{10,... | collective-permute-start | bytes 393224 | tf_op jit(solution)/shard_map/ppermute | solution.py:451
  43.7 15.1 %collective-permute-start.17 = (bf16[256,768]{1,0:T(8,128)(2,1)S(1)}, bf16[256,768]{1,0:T(8,128)(2,1)S(1)}, u32[]{:S(2)}, u32[]{:S(2)}) collective-permute-start(bf16[256,768]{1,0:T(8,128)(2,1)S(1)} %get-tuple-element.75), channel_id=1, source_target_pairs={{0,4},{1,5},{2,6},{3,7},{4,8},{5,9},{6,10},{7,11},{8,12},{9,13},{1... | collective-permute-start | bytes 1179656 | tf_op jit(solution)/shard_map/ppermute | solution.py:454
  51.0 7.8 %collective-permute-start.14 = (bf16[128,768]{1,0:T(8,128)(2,1)S(1)}, bf16[128,768]{1,0:T(8,128)(2,1)S(1)}, u32[]{:S(2)}, u32[]{:S(2)}) collective-permute-start(bf16[128,768]{1,0:T(8,128)(2,1)S(1)} %get-tuple-element.72), channel_id=1, source_target_pairs={{0,2},{1,3},{2,0},{3,1},{4,6},{5,7},{6,4},{7,5},{8,10},{9,11},{10,... | collective-permute-start | bytes 589832 | tf_op jit(solution)/shard_map/ppermute | solution.py:451
  52.5 8.8 %collective-permute-start.18 = (bf16[128,768]{1,0:T(8,128)(2,1)S(1)}, bf16[128,768]{1,0:T(8,128)(2,1)S(1)}, u32[]{:S(2)}, u32[]{:S(2)}) collective-permute-start(bf16[128,768]{1,0:T(8,128)(2,1)S(1)} %get-tuple-element.80), channel_id=1, source_target_pairs={{0,3},{1,2},{2,1},{3,0},{4,7},{5,6},{6,5},{7,4},{8,11},{9,10},{10,... | collective-permute-start | bytes 589832 | tf_op jit(solution)/shard_map/ppermute | solution.py:451
  61.3 7.1 %copy-start.1 = (bf16[128,8192]{1,0:T(8,128)(2,1)S(1)}, bf16[128,8192]{1,0:T(8,128)(2,1)}, u32[]{:S(2)}) copy-start(bf16[128,8192]{1,0:T(8,128)(2,1)} %refs_6_.1) | copy-start | bytes 6291460
  61.3 7.1 %copy-start.4 = (f32[8192]{0:T(1024)S(1)}, f32[8192]{0:T(1024)}, u32[]{:S(2)}) copy-start(f32[8192]{0:T(1024)} %param.21) | copy-start | bytes 98308
  63.2 5.2 %collective-permute-start.21 = (bf16[128,2048]{1,0:T(8,128)(2,1)S(1)}, bf16[128,2048]{1,0:T(8,128)(2,1)S(1)}, u32[]{:S(2)}, u32[]{:S(2)}) collective-permute-start(bf16[128,2048]{1,0:T(8,128)(2,1)S(1)} %get-tuple-element.86), channel_id=1, source_target_pairs={{0,1},{1,0},{2,3},{3,2},{4,5},{5,4},{6,7},{7,6},{8,9},{9,8},{10,11... | collective-permute-start | bytes 1572872 | tf_op jit(solution)/shard_map/ppermute | solution.py:451
  64.0 3.7 %collective-permute-start.22 = (f32[16,128]{1,0:T(8,128)S(1)}, f32[16,128]{1,0:T(8,128)S(1)}, u32[]{:S(2)}, u32[]{:S(2)}) collective-permute-start(f32[16,128]{1,0:T(8,128)S(1)} %get-tuple-element.89), channel_id=1, source_target_pairs={{0,4},{1,5},{2,6},{3,7},{4,0},{5,1},{6,2},{7,3},{8,12},{9,13},{10,... | collective-permute-start | bytes 24584 | tf_op jit(solution)/shard_map/ppermute | solution.py:451
  64.0 8.2 %collective-permute-start.19 = (bf16[128,768]{1,0:T(8,128)(2,1)S(1)}, bf16[128,768]{1,0:T(8,128)(2,1)S(1)}, u32[]{:S(2)}, u32[]{:S(2)}) collective-permute-start(bf16[128,768]{1,0:T(8,128)(2,1)S(1)} %get-tuple-element.81), channel_id=1, source_target_pairs={{0,2},{1,3},{2,0},{3,1},{4,6},{5,7},{6,4},{7,5},{8,10},{9,11},{10,... | collective-permute-start | bytes 589832 | tf_op jit(solution)/shard_map/ppermute | solution.py:451
  65.4 8.9 %collective-permute-start.20 = (bf16[128,768]{1,0:T(8,128)(2,1)S(1)}, bf16[128,768]{1,0:T(8,128)(2,1)S(1)}, u32[]{:S(2)}, u32[]{:S(2)}) collective-permute-start(bf16[128,768]{1,0:T(8,128)(2,1)S(1)} %get-tuple-element.82), channel_id=1, source_target_pairs={{0,3},{1,2},{2,1},{3,0},{4,7},{5,6},{6,5},{7,4},{8,11},{9,10},{10,... | collective-permute-start | bytes 589832 | tf_op jit(solution)/shard_map/ppermute | solution.py:451
  67.6 4.5 %collective-permute-start.23 = (f32[16,128]{1,0:T(8,128)S(1)}, f32[16,128]{1,0:T(8,128)S(1)}, u32[]{:S(2)}, u32[]{:S(2)}) collective-permute-start(f32[16,128]{1,0:T(8,128)S(1)} %add.24.one_ref), channel_id=1, source_target_pairs={{0,8},{1,9},{2,10},{3,11},{4,12},{5,13},{6,14},{7,15},{8,0},{9,1},... | collective-permute-start | bytes 24584 | tf_op jit(solution)/shard_map/ppermute | solution.py:451
  72.2 4.0 %collective-permute-start.24 = (f32[16,128]{1,0:T(8,128)S(1)}, f32[16,128]{1,0:T(8,128)S(1)}, u32[]{:S(2)}, u32[]{:S(2)}) collective-permute-start(f32[16,128]{1,0:T(8,128)S(1)} %add.35.one_ref), channel_id=1, source_target_pairs={{0,1},{1,0},{2,3},{3,2},{4,5},{5,4},{6,7},{7,6},{8,9},{9,8},{10,11... | collective-permute-start | bytes 24584 | tf_op jit(solution)/shard_map/ppermute | solution.py:451
  76.1 3.7 %collective-permute-start.25 = (f32[16,128]{1,0:T(8,128)S(1)}, f32[16,128]{1,0:T(8,128)S(1)}, u32[]{:S(2)}, u32[]{:S(2)}) collective-permute-start(f32[16,128]{1,0:T(8,128)S(1)} %add.36), channel_id=1, source_target_pairs={{0,2},{1,3},{2,0},{3,1},{4,6},{5,7},{6,4},{7,5},{8,10},{9,11},{10,... | collective-permute-start | bytes 24584 | tf_op jit(solution)/shard_map/ppermute | solution.py:451

commit v4 on v3

--- a/solution.py
+++ b/solution.py
@@ -51,13 +51,24 @@
     return pl.CostEstimate(flops=int(us * 1e9), bytes_accessed=int(us * 3e6), transcendentals=0)
 
 
+def halve(x, b, c):
+    full = jnp.concatenate([part.astype(F32)[HALO // 2 :] for part in (x, b, c)], axis=1)
+    width = full.shape[1] // 2
+    return jnp.concatenate([full[:, :width], full[:, width:]], axis=0).astype(BF16)
+
+
+def whole_halo(halo):
+    half = HALO // 2
+    full = jnp.concatenate([halo.astype(F32)[:half], halo.astype(F32)[half:]], axis=1)
+    return jnp.concatenate([jnp.zeros_like(full), full], axis=0).astype(BF16)
+
+
 def pack_kernel(team, gw, rank_ref, x_ref, bc_ref, dt_ref, *refs):
-    xv_ref, tail_ref, bcv_ref, dtv_ref, in_sems, out_sems = refs[-6:]
-    outs = list(refs[:-6])
+    xv_ref, tail_ref, bcv_ref, dtv_ref, held_ref, in_sems, out_sems = refs[-7:]
+    outs = list(refs[:-7])
     rank = rank_ref[0]
     rows = x_ref.shape[0]
     half = bc_ref.shape[1] // 2
-    fold = gw * HALO // rows
     last = pl.ds(rows - HALO, HALO)
 
     def fetch(src, dst, sem):
@@ -80,14 +91,6 @@
 
     for made in fetches[:3]:
         made.wait()
-    def copy_tail(dest, out):
-        at = pl.multiple_of(dest * gw, LANES)
-        b_at = pl.multiple_of(dest * STATE, LANES)
-        c_at = pl.multiple_of(half + dest * STATE, LANES)
-        copy(tail_ref.at[:, pl.ds(at, gw)], out.at[:, 0:gw])
-        copy(bcv_ref.at[last, pl.ds(b_at, STATE)], out.at[:, gw : gw + STATE])
-        copy(bcv_ref.at[last, pl.ds(c_at, STATE)], out.at[:, gw + STATE : gw + 2 * STATE])
-
     for k in (2, 3, 1):
         out = outs.pop(0)
         at = pl.multiple_of((rank ^ k) * STATE, STATE)
@@ -96,25 +99,28 @@
         copy(bcv_ref.at[:, pl.ds(at, STATE)], out.at[:, STATE : 2 * STATE])
         copy(dtv_ref, out.at[:, 2 * STATE : 2 * STATE + LANES])
     first = 2 * STATE + LANES
-    for j in range(rows // HALO):
-        at = pl.multiple_of((rank ^ 1) * gw + j * fold, LANES)
-        copy(tail_ref.at[:, pl.ds(at, fold)], out.at[pl.ds(j * HALO, HALO), first : first + fold])
+    for i, k in enumerate((2, 3, 0)):
+        at = pl.multiple_of((rank ^ k) * gw, LANES)
+        b_at = pl.multiple_of((rank ^ k) * STATE, LANES)
+        c_at = pl.multiple_of(half + (rank ^ k) * STATE, LANES)
+        held_ref[i] = halve(
+            tail_ref[:, pl.ds(at, gw)], bcv_ref[last, pl.ds(b_at, STATE)], bcv_ref[last, pl.ds(c_at, STATE)]
+        )
+        copy(held_ref.at[i], outs.pop(0))
     fetches[3].wait()
-    copy(xv_ref, out.at[:, first + fold : first + fold + gw])
-    for k in (2, 3, 0):
-        copy_tail(rank ^ k, outs.pop(0))
+    copy(xv_ref, out.at[:, first : first + gw])
     for made in copies:
         made.wait()
 
 
-def chunk_kernel(chunks, gw, rank_ref, x_ref, after_ref, *refs):
+def chunk_kernel(chunks, start, gw, rank_ref, x_ref, after_ref, *refs):
     xv_ref, in_sems, out_sems = refs[-3:]
     outs = list(refs[:-3])
     rank = rank_ref[0]
     fetches, copies = [], []
     for i, k in enumerate((2, 3)):
-        at = pl.multiple_of((rank ^ k) * gw, LANES)
-        made = pltpu.make_async_copy(x_ref.at[:, pl.ds(at, gw)], xv_ref.at[i], in_sems.at[i])
+        at = pl.multiple_of((rank ^ k) * gw + start, LANES)
+        made = pltpu.make_async_copy(x_ref.at[:, pl.ds(at, sum(chunks))], xv_ref.at[i], in_sems.at[i])
         made.start()
         fetches.append(made)
     for made in fetches:
@@ -133,35 +139,30 @@
 
 def relay_kernel(team, gw, rank_ref, tail_ref, near_ref, *refs):
     others = {0: tail_ref, 2: refs[0], 3: refs[1]}
-    out_ref, sems = refs[-2:]
+    out_ref, near_tail_ref, sem = refs[-3:]
     rank = rank_ref[0]
     rows = near_ref.shape[0]
-    fold = gw * HALO // rows
-    tail = pl.ds(rows - HALO, HALO)
-
-    def copy_all(pairs):
-        copies = []
-        for i, (src, dst) in enumerate(pairs):
-            made = pltpu.make_async_copy(src, dst, sems.at[i])
-            made.start()
-            copies.append(made)
-        for made in copies:
-            made.wait()
+
+    def copy(src, dst):
+        made = pltpu.make_async_copy(src, dst, sem)
+        made.start()
+        made.wait()
 
     for k, ref in others.items():
 
         @pl.when(rank ^ k == team - 1)
         def _():
-            copy_all([(ref, out_ref)])
+            copy(ref, out_ref)
 
     @pl.when(rank ^ 1 == team - 1)
     def _():
+        copy(near_ref.at[pl.ds(rows - HALO, HALO)], near_tail_ref)
         first = 2 * STATE + LANES
-        pairs = [(near_ref.at[tail, 0 : 2 * STATE], out_ref.at[:, gw : gw + 2 * STATE])]
-        for j in range(rows // HALO):
-            src = near_ref.at[pl.ds(j * HALO, HALO), first : first + fold]
-            pairs.append((src, out_ref.at[:, j * fold : (j + 1) * fold]))
-        copy_all(pairs)
+        out_ref[...] = halve(
+            near_tail_ref[:, first : first + gw],
+            near_tail_ref[:, 0:STATE],
+            near_tail_ref[:, STATE : 2 * STATE],
+        )
 
 
 def column_of(row):
@@ -227,7 +228,7 @@
     c_at = pl.multiple_of(half + rank * STATE, LANES)
     own = [(bc_ref.at[:, pl.ds(b_at, STATE)], 0), (bc_ref.at[:, pl.ds(c_at, STATE)], STATE), (dt_ref, 2 * STATE)]
     others = [[(ref.at[:, 0 : 2 * STATE + LANES], 0)] for ref in got]
-    gather_rows(rank, [own] + others, raw_ref, halo_ref[:, gw : gw + 2 * STATE], sems)
+    gather_rows(rank, [own] + others, raw_ref, whole_halo(halo_ref[...])[:, gw : gw + 2 * STATE], sems)
 
     lane = iota((LANES, LANES), 1)
     part = lane // own_heads
@@ -311,7 +312,7 @@
     sources = [[(x_ref.at[:, pl.ds(at, width)], 0)]]
     for ref, place in zip(got, places):
         sources.append([(ref.at[:, place : place + width], 0)])
-    gather_rows(rank, sources, raw_ref, halo_ref[:, cols], sems)
+    gather_rows(rank, sources, raw_ref, whole_halo(halo_ref[...])[:, cols], sems)
     spread_v = spreader(first, width, hdim, own_heads, False)
     spread_u = spreader(first, width, hdim, own_heads, True)
     rows = jnp.dot(row_ref[...], spread_v, preferred_element_type=F32)
@@ -388,8 +389,8 @@
     near.wait()
 
 
-def add_kernel(rank_ref, one_ref, other_ref, *refs):
-    refs[-1][...] = one_ref[...] + other_ref[...]
+def add_kernel(rank_ref, one_ref, other_ref, after_ref, out_ref):
+    out_ref[...] = one_ref[...] + other_ref[...]
 
 
 def norm_kernel(blocks, rank_ref, *refs):
@@ -455,9 +456,8 @@
 
     shape = jax.ShapeDtypeStruct
     bcd_w = 2 * STATE + LANES
-    lead_w = bcd_w + gw * HALO // rows
-    widths = [bcd_w] * 2 + [lead_w + gw]
-    halo_shape = (HALO, gw + 2 * STATE)
+    widths = [bcd_w] * 2 + [bcd_w + gw]
+    halo_shape = (HALO, gw // 2 + STATE)
     packed = call(
         functools.partial(pack_kernel, team, gw),
         rank,
@@ -470,8 +470,9 @@
             pltpu.VMEM((HALO, inner), BF16),
             pltpu.VMEM(bc_stream.shape, BF16),
             pltpu.VMEM(dt_raw.shape, BF16),
+            pltpu.VMEM((3, *halo_shape), BF16),
             pltpu.SemaphoreType.DMA((4,)),
-            pltpu.SemaphoreType.DMA((9 + rows // HALO + 1 + 9,)),
+            pltpu.SemaphoreType.DMA((13,)),
         ],
         "pack",
         cost=cost(2),
@@ -479,22 +480,26 @@
     )
     near = swap(packed[2], 1)
     lead = [near, swap(packed[0], 2), swap(packed[1], 3)]
-    x_parts = call(
-        functools.partial(chunk_kernel, chunks, gw),
-        rank,
-        (x_stream, near),
-        [ANY] * 2,
-        [shape((rows, size), BF16) for size in chunks for _ in range(2)],
-        [ANY] * (2 * len(chunks)),
-        [
-            pltpu.VMEM((2, rows, gw), BF16),
-            pltpu.SemaphoreType.DMA((2,)),
-            pltpu.SemaphoreType.DMA((2 * len(chunks),)),
-        ],
-        "chunks",
-        cost=cost(2),
-    )
-    got = [[near, swap(x_parts[2 * q], 2), swap(x_parts[2 * q + 1], 3)] for q in range(len(chunks))]
+    def send_chunks(first, count, after):
+        sizes = chunks[first : first + count]
+        parts = call(
+            functools.partial(chunk_kernel, sizes, sum(chunks[:first]), gw),
+            rank,
+            (x_stream, after),
+            [ANY] * 2,
+            [shape((rows, size), BF16) for size in sizes for _ in range(2)],
+            [ANY] * (2 * count),
+            [
+                pltpu.VMEM((2, rows, sum(sizes)), BF16),
+                pltpu.SemaphoreType.DMA((2,)),
+                pltpu.SemaphoreType.DMA((2 * count,)),
+            ],
+            "chunks",
+            cost=cost(1),
+        )
+        return [[near, swap(parts[2 * q], 2), swap(parts[2 * q + 1], 3)] for q in range(count)]
+
+    got = send_chunks(0, len(chunks) - 1, near)
 
     ext_docs = jnp.concatenate([jnp.full((LANES,), -1, jnp.int32), doc_ids])
     docs = lax.dynamic_slice_in_dim(ext_docs, (me // team) * SPAN, SPAN + LANES).astype(F32)[None]
@@ -522,7 +527,7 @@
             [ANY] * 4,
             shape(halo_shape, BF16),
             whole(halo_shape),
-            [pltpu.SemaphoreType.DMA((1 + rows // HALO,))],
+            [pltpu.VMEM((HALO, bcd_w + gw), BF16), pltpu.SemaphoreType.DMA],
             "relay",
             cost=cost(1),
         )
@@ -569,7 +574,7 @@
     def mix(q, after):
         start, size = sum(chunks[:q]), chunks[q]
         xc, y_local, fresh = call(
-            functools.partial(mix_kernel, team, taps, hdim, gw, start, (lead_w + start, 0, 0)),
+            functools.partial(mix_kernel, team, taps, hdim, gw, start, (bcd_w + start, 0, 0)),
             rank,
             (x_stream, *got[q], halo, shift, wb, scores, b_turned, uv, row_pack, *after),
             [ANY]
@@ -595,6 +600,8 @@
             "mix",
             cost=cost(4),
         )
+        if q == 0:
+            got.extend(send_chunks(len(chunks) - 1, 1, fresh))
         state = onward(fresh)
         if hops > 1:
             first, count, own_heads = start // hdim, size // hdim, heads // team
@@ -671,20 +678,18 @@
         )
 
     mixed, near_done = norm([y_own, [y_near]], 0, [])
-    mixed, far_done = norm([y_far, y_across], 2, [mixed])
+    mixed, _ = norm([y_far, y_across], 2, [mixed])
 
     steps = [1 << place for place in range((members - 1).bit_length())]
     within = (team - 1).bit_length()
-    flips = steps[within:] + steps[:within]
-    for i, flip in enumerate(flips):
+    for i, flip in enumerate(steps[within:] + steps[:within]):
         came = swap(stats, flip)
-        after = {len(flips) - 3: [near_done], len(flips) - 2: [far_done]}.get(i, [])
-        if after:
+        if i == 1:
             stats = call(
                 add_kernel,
                 rank,
-                (stats, came, *after),
-                [whole((DOCS, LANES))] * 2 + [ANY] * len(after),
+                (stats, came, near_done),
+                [whole((DOCS, LANES))] * 2 + [ANY],
                 shape((DOCS, LANES), F32),
                 whole((DOCS, LANES)),
                 [],

time: 80.7 us -> 76.2 us (0.944)
  waiting for transfers between devices: 28.5 us -> 26.1 us
  starting transfers between devices: 26.7 us -> 24.5 us
    ppermute x22, waiting for transfers between devices: 26.4 us -> 23.9 us  [swap(): return lax.ppermute(array, 'seq', [(i, i ^ k) for i in range(members)])]
    ppermute x22, starting transfers between devices: 19.4 us -> 17.8 us  [swap(): return lax.ppermute(array, 'seq', [(i, i ^ k) for i in range(members)])]
  transfers between devices with their start and end apart: 26 -> 26, of which waited for: 14 -> 14; matrix products, arithmetic and copies ran while one was open for 0% -> 0% of each run, Pallas kernels for 23% -> 25%
where the time goes in v4:
time: 76.2 us; the launch traced here: 76.1 us
  waiting for transfers between devices  26.1 us (34%)
  starting transfers between devices  24.5 us (32%)
  Pallas kernels  23.5 us (31%)
  other arithmetic  0.94 us (1%)
  between operations  0.9 us (1%)
    ppermute x22, waiting for transfers between devices, swap(): return lax.ppermute(array, 'seq', [(i, i ^ k) for i in range(members)])  23.9 us
    pallas_call x15, Pallas kernels, call(): pl.pallas_call(kernel, grid_spec=pltpu.PrefetchScalarGridSpec(num_scalar_...  23.5 us
    ppermute x22, starting transfers between devices, swap(): return lax.ppermute(array, 'seq', [(i, i ^ k) for i in range(members)])  17.8 us
    ppermute x4, starting transfers between devices, onward(): lax.ppermute(array, 'seq', [(i, (i + team) % members) for i in range(memb...  6.71 us
    ppermute x4, waiting for transfers between devices, onward(): lax.ppermute(array, 'seq', [(i, (i + team) % members) for i in range(memb...  2.26 us
  transfers between devices with their start and end apart: 26, of which 14 were waited for; matrix products, arithmetic and copies ran while one was open for 0% of the time, Pallas kernels for 25%

profile of v4, /device:TPU:0, one launch (start us, length us, event | category | flops | bytes accessed | tf_op | source)
XLA Modules:
  0.0 76.1 jit_solution(11466290718191275254)
XLA Ops:
  0.7 2.4 %pack.1 = (bf16[128,640]{1,0:T(8,128)(2,1)}, bf16[128,640]{1,0:T(8,128)(2,1)}, bf16[128,2688]{1,0:T(8,128)(2,1)}, bf16[16,1280]{1,0:T(8,128)(2,1)}, bf16[16,1280]{1,0:T(8,128)(2,1)}, /*index=5*/bf16[16,1280]{1,0:T(8,128)(2,1)}) custom-call(s32[1]{0:T(128)} %bitcast.rank_ref, bf16[128,8192]{1,0:T(8,128)(2,1)} %refs_0_.5, bf16[128,2048]{1,0:T(8,128)(2,1)} %bc_ref.3, ...), custom_call_target="tpu_custom_call" | custom-call | flops 2000000000 | bytes 6000000 | tf_op jit(solution)/shard_map/pack/pallas_call | solution.py:33
  3.1 0.5 collective-permute-start
  3.6 2.6 %collective-permute-start.3 = (bf16[16,1280]{1,0:T(8,128)(2,1)}, bf16[16,1280]{1,0:T(8,128)(2,1)S(1)}, u32[]{:S(2)}, u32[]{:S(2)}) collective-permute-start(bf16[16,1280]{1,0:T(8,128)(2,1)} %get-tuple-element.50), channel_id=1, source_target_pairs={{0,2},{1,3},{2,0},{3,1},{4,6},{5,7},{6,4},{7,5},{8,10},{9,11},{10,... | collective-permute-start | bytes 122888 | tf_op jit(solution)/shard_map/ppermute | solution.py:452
  6.3 1.7 %collective-permute-start.6 = (bf16[128,640]{1,0:T(8,128)(2,1)}, bf16[128,640]{1,0:T(8,128)(2,1)S(1)}, u32[]{:S(2)}, u32[]{:S(2)}) collective-permute-start(bf16[128,640]{1,0:T(8,128)(2,1)} %get-tuple-element.52), channel_id=1, source_target_pairs={{0,2},{1,3},{2,0},{3,1},{4,6},{5,7},{6,4},{7,5},{8,10},{9,11},{10,... | collective-permute-start | bytes 491528 | tf_op jit(solution)/shard_map/ppermute | solution.py:452
  8.6 1.4 %collective-permute-done.4.refs_1_ = bf16[16,1280]{1,0:T(8,128)(2,1)S(1)} collective-permute-done((bf16[16,1280]{1,0:T(8,128)(2,1)}, bf16[16,1280]{1,0:T(8,128)(2,1)S(1)}, u32[]{:S(2)}, u32[]{:S(2)}) %collective-permute-start.4) | collective-permute-done | bytes 40992 | tf_op jit(solution)/shard_map/ppermute | solution.py:452
  10.1 1.6 %collective-permute-start.5 = (bf16[16,1280]{1,0:T(8,128)(2,1)S(1)}, bf16[16,1280]{1,0:T(8,128)(2,1)S(1)}, u32[]{:S(2)}, u32[]{:S(2)}) collective-permute-start(bf16[16,1280]{1,0:T(8,128)(2,1)S(1)} %relay.1), channel_id=1, source_target_pairs={{0,4},{1,5},{2,6},{3,7},{4,8},{5,9},{6,10},{7,11},{8,12},{9,13},{1... | collective-permute-start | bytes 122888 | tf_op jit(solution)/shard_map/ppermute | solution.py:455
  11.9 0.9 %collective-permute-start.1 = (bf16[128,512]{1,0:T(8,128)(2,1)S(1)}, bf16[128,512]{1,0:T(8,128)(2,1)S(1)}, u32[]{:S(2)}, u32[]{:S(2)}) collective-permute-start(bf16[128,512]{1,0:T(8,128)(2,1)S(1)} %get-tuple-element.47), channel_id=1, source_target_pairs={{0,2},{1,3},{2,0},{3,1},{4,6},{5,7},{6,4},{7,5},{8,10},{9,11},{10,... | collective-permute-start | bytes 393224 | tf_op jit(solution)/shard_map/ppermute | solution.py:452
  12.9 0.5 collective-permute-start.2
  13.4 0.6 collective-permute-done.6.refs_1_
  14.0 1.2 %collective-permute-start.10 = (bf16[128,768]{1,0:T(8,128)(2,1)S(1)}, bf16[128,768]{1,0:T(8,128)(2,1)S(1)}, u32[]{:S(2)}, u32[]{:S(2)}) collective-permute-start(bf16[128,768]{1,0:T(8,128)(2,1)S(1)} %get-tuple-element.63), channel_id=1, source_target_pairs={{0,2},{1,3},{2,0},{3,1},{4,6},{5,7},{6,4},{7,5},{8,10},{9,11},{10,... | collective-permute-start | bytes 589832 | tf_op jit(solution)/shard_map/ppermute | solution.py:452
  15.2 1.8 %collective-permute-done.7.refs_2_ = bf16[128,640]{1,0:T(8,128)(2,1)S(1)} collective-permute-done((bf16[128,640]{1,0:T(8,128)(2,1)}, bf16[128,640]{1,0:T(8,128)(2,1)S(1)}, u32[]{:S(2)}, u32[]{:S(2)}) %collective-permute-start.7) | collective-permute-done | bytes 163872 | tf_op jit(solution)/shard_map/ppermute | solution.py:452
  17.0 1.1 %collective-permute-start.11 = (bf16[128,768]{1,0:T(8,128)(2,1)S(1)}, bf16[128,768]{1,0:T(8,128)(2,1)S(1)}, u32[]{:S(2)}, u32[]{:S(2)}) collective-permute-start(bf16[128,768]{1,0:T(8,128)(2,1)S(1)} %get-tuple-element.64), channel_id=1, source_target_pairs={{0,3},{1,2},{2,1},{3,0},{4,7},{5,6},{6,5},{7,4},{8,11},{9,10},{10,... | collective-permute-start | bytes 589832 | tf_op jit(solution)/shard_map/ppermute | solution.py:452
  18.2 2.6 %bc.1 = (bf16[512,512]{1,0:T(8,128)(2,1)S(1)}, bf16[256,512]{1,0:T(8,128)(2,1)S(1)}, bf16[512,256]{1,0:T(8,128)(2,1)S(1)}, bf16[512,128]{1,0:T(8,128)(2,1)S(1)}, bf16[16,128]{1,0:T(8,128)(2,1)S(1)}) custom-call(s32[1]{0:T(128)} %bitcast.rank_ref, bf16[128,2048]{1,0:T(8,128)(2,1)S(1)} %copy-done.2, bf16[128,128]{1,0:T(8,128)(2,1)S(1)} %copy-done.3, ...), custom_call_target="tpu_custom_call" | custom-call | flops 4000000000 | bytes 12000000 | tf_op jit(solution)/shard_map/bc/pallas_call | solution.py:33
  20.8 1.9 %collective-permute-done.2.refs_3_ = bf16[128,512]{1,0:T(8,128)(2,1)S(1)} collective-permute-done((bf16[128,512]{1,0:T(8,128)(2,1)S(1)}, bf16[128,512]{1,0:T(8,128)(2,1)S(1)}, u32[]{:S(2)}, u32[]{:S(2)}) %collective-permute-start.2) | collective-permute-done | bytes 131104 | tf_op jit(solution)/shard_map/ppermute | solution.py:452
  22.6 2.4 %mix.3 = (bf16[512,512]{1,0:T(8,128)(2,1)S(1)}, f32[512,512]{1,0:T(8,128)S(1)}, bf16[256,512]{1,0:T(8,128)(2,1)S(1)}) custom-call(s32[1]{0:T(128)} %bitcast.rank_ref, bf16[128,8192]{1,0:T(8,128)(2,1)S(1)} %copy-done, bf16[128,2688]{1,0:T(8,128)(2,1)S(1)} %collective-permute-done.after_ref.near_ref.refs_0_.refs_1_, ...), custom_call_target="tpu_custom_call" | custom-call | flops 4000000000 | bytes 12000000 | tf_op jit(solution)/shard_map/mix/pallas_call | solution.py:33
  25.0 1.6 %collective-permute-start.8 = (bf16[256,512]{1,0:T(8,128)(2,1)S(1)}, bf16[256,512]{1,0:T(8,128)(2,1)S(1)}, u32[]{:S(2)}, u32[]{:S(2)}) collective-permute-start(bf16[256,512]{1,0:T(8,128)(2,1)S(1)} %get-tuple-element.58.after_ref), channel_id=1, source_target_pairs={{0,4},{1,5},{2,6},{3,7},{4,8},{5,9},{6,10},{7,11},{8,12},{9,13},{1... | collective-permute-start | bytes 786440 | tf_op jit(solution)/shard_map/ppermute | solution.py:455
  26.7 0.6 chunks.3
  27.3 0.8 %collective-permute-start.15 = (bf16[128,768]{1,0:T(8,128)(2,1)S(1)}, bf16[128,768]{1,0:T(8,128)(2,1)S(1)}, u32[]{:S(2)}, u32[]{:S(2)}) collective-permute-start(bf16[128,768]{1,0:T(8,128)(2,1)S(1)} %get-tuple-element.72), channel_id=1, source_target_pairs={{0,2},{1,3},{2,0},{3,1},{4,6},{5,7},{6,4},{7,5},{8,10},{9,11},{10,... | collective-permute-start | bytes 589832 | tf_op jit(solution)/shard_map/ppermute | solution.py:452
  28.1 0.7 collective-permute-start.16
  28.8 2.3 %collective-permute-done.11.refs_3_ = bf16[128,768]{1,0:T(8,128)(2,1)S(1)} collective-permute-done((bf16[128,768]{1,0:T(8,128)(2,1)S(1)}, bf16[128,768]{1,0:T(8,128)(2,1)S(1)}, u32[]{:S(2)}, u32[]{:S(2)}) %collective-permute-start.11) | collective-permute-done | bytes 196640 | tf_op jit(solution)/shard_map/ppermute | solution.py:452
  31.1 3.1 %mix.4 = (bf16[512,768]{1,0:T(8,128)(2,1)S(1)}, f32[512,768]{1,0:T(8,128)S(1)}, bf16[256,768]{1,0:T(8,128)(2,1)S(1)}) custom-call(s32[1]{0:T(128)} %bitcast.rank_ref, bf16[128,8192]{1,0:T(8,128)(2,1)S(1)} %copy-done, bf16[128,2688]{1,0:T(8,128)(2,1)S(1)} %collective-permute-done.after_ref.near_ref.refs_0_.refs_1_, ...), custom_call_target="tpu_custom_call" | custom-call | flops 4000000000 | bytes 12000000 | tf_op jit(solution)/shard_map/mix/pallas_call | solution.py:33
  34.2 1.6 %collective-permute-start.12 = (bf16[256,768]{1,0:T(8,128)(2,1)S(1)}, bf16[256,768]{1,0:T(8,128)(2,1)S(1)}, u32[]{:S(2)}, u32[]{:S(2)}) collective-permute-start(bf16[256,768]{1,0:T(8,128)(2,1)S(1)} %get-tuple-element.65), channel_id=1, source_target_pairs={{0,4},{1,5},{2,6},{3,7},{4,8},{5,9},{6,10},{7,11},{8,12},{9,13},{1... | collective-permute-start | bytes 1179656 | tf_op jit(solution)/shard_map/ppermute | solution.py:455
  35.8 1.6 %carry.3 = (bf16[128,512]{1,0:T(8,128)(2,1)S(1)}, bf16[128,2048]{1,0:T(8,128)(2,1)S(1)}, bf16[128,512]{1,0:T(8,128)(2,1)S(1)}, bf16[128,512]{1,0:T(8,128)(2,1)S(1)}, f32[16,128]{1,0:T(8,128)S(1)}) custom-call(s32[1]{0:T(128)} %bitcast.rank_ref, bf16[256,512]{1,0:T(8,128)(2,1)S(1)} %collective-permute-done.8.st_ref, f32[512,512]{1,0:T(8,128)S(1)} %get-tuple-element.59.yl_ref, ...), custom_call_target="tpu_custom_call" | custom-call | flops 3000000000 | bytes 9000000 | tf_op jit(solution)/shard_map/carry/pallas_call | solution.py:33
  37.4 0.9 %collective-permute-start.9 = (bf16[128,512]{1,0:T(8,128)(2,1)S(1)}, bf16[128,512]{1,0:T(8,128)(2,1)S(1)}, u32[]{:S(2)}, u32[]{:S(2)}) collective-permute-start(bf16[128,512]{1,0:T(8,128)(2,1)S(1)} %get-tuple-element.62), channel_id=1, source_target_pairs={{0,2},{1,3},{2,0},{3,1},{4,6},{5,7},{6,4},{7,5},{8,10},{9,11},{10,... | collective-permute-start | bytes 393224 | tf_op jit(solution)/shard_map/ppermute | solution.py:452
  38.4 0.8 %collective-permute-start.13 = (bf16[128,512]{1,0:T(8,128)(2,1)S(1)}, bf16[128,512]{1,0:T(8,128)(2,1)S(1)}, u32[]{:S(2)}, u32[]{:S(2)}) collective-permute-start(bf16[128,512]{1,0:T(8,128)(2,1)S(1)} %get-tuple-element.70), channel_id=1, source_target_pairs={{0,3},{1,2},{2,1},{3,0},{4,7},{5,6},{6,5},{7,4},{8,11},{9,10},{10,... | collective-permute-start | bytes 393224 | tf_op jit(solution)/shard_map/ppermute | solution.py:452
  39.2 0.3 collective-permute-done.16.refs_3_
  39.5 3.1 %mix.5 = (bf16[512,768]{1,0:T(8,128)(2,1)S(1)}, f32[512,768]{1,0:T(8,128)S(1)}, bf16[256,768]{1,0:T(8,128)(2,1)S(1)}) custom-call(s32[1]{0:T(128)} %bitcast.rank_ref, bf16[128,8192]{1,0:T(8,128)(2,1)S(1)} %copy-done, bf16[128,2688]{1,0:T(8,128)(2,1)S(1)} %collective-permute-done.after_ref.near_ref.refs_0_.refs_1_, ...), custom_call_target="tpu_custom_call" | custom-call | flops 4000000000 | bytes 12000000 | tf_op jit(solution)/shard_map/mix/pallas_call | solution.py:33
  42.6 1.8 %collective-permute-start.17 = (bf16[256,768]{1,0:T(8,128)(2,1)S(1)}, bf16[256,768]{1,0:T(8,128)(2,1)S(1)}, u32[]{:S(2)}, u32[]{:S(2)}) collective-permute-start(bf16[256,768]{1,0:T(8,128)(2,1)S(1)} %get-tuple-element.74), channel_id=1, source_target_pairs={{0,4},{1,5},{2,6},{3,7},{4,8},{5,9},{6,10},{7,11},{8,12},{9,13},{1... | collective-permute-start | bytes 1179656 | tf_op jit(solution)/shard_map/ppermute | solution.py:455
  44.4 1.1 %collective-permute-done.13.refs_3_ = bf16[128,512]{1,0:T(8,128)(2,1)S(1)} collective-permute-done((bf16[128,512]{1,0:T(8,128)(2,1)S(1)}, bf16[128,512]{1,0:T(8,128)(2,1)S(1)}, u32[]{:S(2)}, u32[]{:S(2)}) %collective-permute-start.13) | collective-permute-done | bytes 131104 | tf_op jit(solution)/shard_map/ppermute | solution.py:452
  45.5 2.3 %collective-permute-done.12.st_ref = bf16[256,768]{1,0:T(8,128)(2,1)S(1)} collective-permute-done((bf16[256,768]{1,0:T(8,128)(2,1)S(1)}, bf16[256,768]{1,0:T(8,128)(2,1)S(1)}, u32[]{:S(2)}, u32[]{:S(2)}) %collective-permute-start.12) | collective-permute-done | bytes 393248 | tf_op jit(solution)/shard_map/ppermute | solution.py:455
  47.7 1.9 %carry.4 = (bf16[128,768]{1,0:T(8,128)(2,1)S(1)}, bf16[128,2048]{1,0:T(8,128)(2,1)S(1)}, bf16[128,768]{1,0:T(8,128)(2,1)S(1)}, bf16[128,768]{1,0:T(8,128)(2,1)S(1)}, f32[16,128]{1,0:T(8,128)S(1)}) custom-call(s32[1]{0:T(128)} %bitcast.rank_ref, bf16[256,768]{1,0:T(8,128)(2,1)S(1)} %collective-permute-done.12.st_ref, ...), custom_call_target="tpu_custom_call", output_to_operand_aliasing={{1}: (8, {})} | custom-call | flops 3000000000 | bytes 9000000 | tf_op jit(solution)/shard_map/carry/pallas_call | solution.py:33
  49.6 0.8 collective-permute-start.14
  50.4 0.5 collective-permute-start.18
  50.9 6.6 %collective-permute-done.14.refs_2_.refs_1_ = bf16[128,768]{1,0:T(8,128)(2,1)S(1)} collective-permute-done((bf16[128,768]{1,0:T(8,128)(2,1)S(1)}, bf16[128,768]{1,0:T(8,128)(2,1)S(1)}, u32[]{:S(2)}, u32[]{:S(2)}) %collective-permute-start.14) | collective-permute-done | bytes 196640 | tf_op jit(solution)/shard_map/ppermute | solution.py:452
  57.5 1.9 %collective-permute-done.18.refs_3_.refs_4_ = bf16[128,768]{1,0:T(8,128)(2,1)S(1)} collective-permute-done((bf16[128,768]{1,0:T(8,128)(2,1)S(1)}, bf16[128,768]{1,0:T(8,128)(2,1)S(1)}, u32[]{:S(2)}, u32[]{:S(2)}) %collective-permute-start.18) | collective-permute-done | bytes 196640 | tf_op jit(solution)/shard_map/ppermute | solution.py:452
  59.4 1.9 %carry.5 = (bf16[128,768]{1,0:T(8,128)(2,1)S(1)}, bf16[128,2048]{1,0:T(8,128)(2,1)S(1)}, bf16[128,768]{1,0:T(8,128)(2,1)S(1)}, bf16[128,768]{1,0:T(8,128)(2,1)S(1)}, f32[16,128]{1,0:T(8,128)S(1)}) custom-call(s32[1]{0:T(128)} %bitcast.rank_ref, bf16[256,768]{1,0:T(8,128)(2,1)S(1)} %collective-permute-done.17.st_ref, ...), custom_call_target="tpu_custom_call", output_to_operand_aliasing={{1}: (8, {})} | custom-call | flops 3000000000 | bytes 9000000 | tf_op jit(solution)/shard_map/carry/pallas_call | solution.py:33
  61.3 1.0 %collective-permute-start.21 = (bf16[128,2048]{1,0:T(8,128)(2,1)S(1)}, bf16[128,2048]{1,0:T(8,128)(2,1)S(1)}, u32[]{:S(2)}, u32[]{:S(2)}) collective-permute-start(bf16[128,2048]{1,0:T(8,128)(2,1)S(1)} %get-tuple-element.85), channel_id=1, source_target_pairs={{0,1},{1,0},{2,3},{3,2},{4,5},{5,4},{6,7},{7,6},{8,9},{9,8},{10,11... | collective-permute-start | bytes 1572872 | tf_op jit(solution)/shard_map/ppermute | solution.py:452
  62.4 1.2 %collective-permute-start.19 = (bf16[128,768]{1,0:T(8,128)(2,1)S(1)}, bf16[128,768]{1,0:T(8,128)(2,1)S(1)}, u32[]{:S(2)}, u32[]{:S(2)}) collective-permute-start(bf16[128,768]{1,0:T(8,128)(2,1)S(1)} %get-tuple-element.80), channel_id=1, source_target_pairs={{0,2},{1,3},{2,0},{3,1},{4,6},{5,7},{6,4},{7,5},{8,10},{9,11},{10,... | collective-permute-start | bytes 589832 | tf_op jit(solution)/shard_map/ppermute | solution.py:452
  63.5 0.3 collective-permute-start.20
  63.8 2.1 %collective-permute-done.22 = f32[16,128]{1,0:T(8,128)S(1)} collective-permute-done((f32[16,128]{1,0:T(8,128)S(1)}, f32[16,128]{1,0:T(8,128)S(1)}, u32[]{:S(2)}, u32[]{:S(2)}) %collective-permute-start.22) | collective-permute-done | bytes 8224 | tf_op jit(solution)/shard_map/ppermute | solution.py:452
  66.0 1.0 %collective-permute-start.23 = (f32[16,128]{1,0:T(8,128)S(1)}, f32[16,128]{1,0:T(8,128)S(1)}, u32[]{:S(2)}, u32[]{:S(2)}) collective-permute-start(f32[16,128]{1,0:T(8,128)S(1)} %add.26.one_ref), channel_id=1, source_target_pairs={{0,8},{1,9},{2,10},{3,11},{4,12},{5,13},{6,14},{7,15},{8,0},{9,1},... | collective-permute-start | bytes 24584 | tf_op jit(solution)/shard_map/ppermute | solution.py:452
  67.0 1.8 %norm.2 = (bf16[128,8192]{1,0:T(8,128)(2,1)}, f32[8,128]{1,0:T(8,128)S(1)}) custom-call(s32[1]{0:T(128)} %bitcast.rank_ref, bf16[128,512]{1,0:T(8,128)(2,1)S(1)} %get-tuple-element.82.refs_0_, bf16[128,768]{1,0:T(8,128)(2,1)S(1)} %get-tuple-element.83.refs_1_, bf16[128,768]{1,0:T(8,128)(2,1)S(1)} %get-tuple-element.84.refs_2_, ...), custom_call_target="tpu_custom_call" | custom-call | flops 2000000000 | bytes 6000000 | tf_op jit(solution)/shard_map/norm/pallas_call | solution.py:33
  68.8 1.7 %collective-permute-done.23.other_ref = f32[16,128]{1,0:T(8,128)S(1)} collective-permute-done((f32[16,128]{1,0:T(8,128)S(1)}, f32[16,128]{1,0:T(8,128)S(1)}, u32[]{:S(2)}, u32[]{:S(2)}) %collective-permute-start.23) | collective-permute-done | bytes 8224 | tf_op jit(solution)/shard_map/ppermute | solution.py:452
  70.5 1.2 %collective-permute-done.24 = f32[16,128]{1,0:T(8,128)S(1)} collective-permute-done((f32[16,128]{1,0:T(8,128)S(1)}, f32[16,128]{1,0:T(8,128)S(1)}, u32[]{:S(2)}, u32[]{:S(2)}) %collective-permute-start.24) | collective-permute-done | bytes 8224 | tf_op jit(solution)/shard_map/ppermute | solution.py:452
  71.7 1.0 %collective-permute-start.25 = (f32[16,128]{1,0:T(8,128)S(1)}, f32[16,128]{1,0:T(8,128)S(1)}, u32[]{:S(2)}, u32[]{:S(2)}) collective-permute-start(f32[16,128]{1,0:T(8,128)S(1)} %add.27), channel_id=1, source_target_pairs={{0,2},{1,3},{2,0},{3,1},{4,6},{5,7},{6,4},{7,5},{8,10},{9,11},{10,... | collective-permute-start | bytes 24584 | tf_op jit(solution)/shard_map/ppermute | solution.py:452
  72.7 1.8 %norm.3 = (bf16[128,8192]{1,0:T(8,128)(2,1)}, f32[8,128]{1,0:T(8,128)}) custom-call(s32[1]{0:T(128)} %bitcast.rank_ref, bf16[128,512]{1,0:T(8,128)(2,1)S(1)} %collective-permute-done.9.refs_2_.refs_0_, bf16[128,768]{1,0:T(8,128)(2,1)S(1)} %collective-permute-done.14.refs_2_.refs_1_, ...), custom_call_target="tpu_custom_call", output_to_operand_aliasing={{0}: (9, {})} | custom-call | flops 2000000000 | bytes 6000000 | tf_op jit(solution)/shard_map/norm/pallas_call | solution.py:33
  74.5 0.9 %collective-permute-done.25 = f32[16,128]{1,0:T(8,128)S(1)} collective-permute-done((f32[16,128]{1,0:T(8,128)S(1)}, f32[16,128]{1,0:T(8,128)S(1)}, u32[]{:S(2)}, u32[]{:S(2)}) %collective-permute-start.25) | collective-permute-done | bytes 8224 | tf_op jit(solution)/shard_map/ppermute | solution.py:452
  75.4 0.7 fusion.3
  (53 shorter events, 0.9 us)
Async XLA Ops:
  0.6 7.4 %copy-start.6 = (f32[4,10240]{1,0:T(4,128)S(1)}, f32[4,10240]{1,0:T(4,128)}, u32[]{:S(2)}) copy-start(f32[4,10240]{1,0:T(4,128)} %param.16) | copy-start | bytes 491524
  0.7 7.4 %copy-start.7 = (f32[10240]{0:T(1024)S(1)}, f32[10240]{0:T(1024)}, u32[]{:S(2)}) copy-start(f32[10240]{0:T(1024)} %param.17) | copy-start | bytes 122884
  0.7 7.4 %copy-start.8 = (s32[2048]{0:T(1024)S(1)}, s32[2048]{0:T(1024)}, u32[]{:S(2)}) copy-start(s32[2048]{0:T(1024)} %param.15) | copy-start | bytes 24580
  0.7 7.6 %copy-start.9 = (f32[128]{0:T(128)S(1)}, f32[128]{0:T(128)}, u32[]{:S(2)}) copy-start(f32[128]{0:T(128)} %param.20) | copy-start | bytes 1540
  0.7 7.6 %copy-start.10 = (f32[128]{0:T(128)S(1)}, f32[128]{0:T(128)}, u32[]{:S(2)}) copy-start(f32[128]{0:T(128)} %param.19) | copy-start | bytes 1540
  0.7 7.6 %copy-start.11 = (f32[128]{0:T(128)S(1)}, f32[128]{0:T(128)}, u32[]{:S(2)}) copy-start(f32[128]{0:T(128)} %param.18) | copy-start | bytes 1540
  3.1 6.9 %collective-permute-start = (bf16[128,2688]{1,0:T(8,128)(2,1)}, bf16[128,2688]{1,0:T(8,128)(2,1)S(1)}, u32[]{:S(2)}, u32[]{:S(2)}) collective-permute-start(bf16[128,2688]{1,0:T(8,128)(2,1)} %get-tuple-element.46), channel_id=1, source_target_pairs={{0,1},{1,0},{2,3},{3,2},{4,5},{5,4},{6,7},{7,6},{8,9},{9,8},{10,11... | collective-permute-start | bytes 2064392 | tf_op jit(solution)/shard_map/ppermute | solution.py:452
  3.6 5.0 %collective-permute-start.3 = (bf16[16,1280]{1,0:T(8,128)(2,1)}, bf16[16,1280]{1,0:T(8,128)(2,1)S(1)}, u32[]{:S(2)}, u32[]{:S(2)}) collective-permute-start(bf16[16,1280]{1,0:T(8,128)(2,1)} %get-tuple-element.50), channel_id=1, source_target_pairs={{0,2},{1,3},{2,0},{3,1},{4,6},{5,7},{6,4},{7,5},{8,10},{9,11},{10,... | collective-permute-start | bytes 122888 | tf_op jit(solution)/shard_map/ppermute | solution.py:452
  6.2 3.8 %collective-permute-start.4 = (bf16[16,1280]{1,0:T(8,128)(2,1)}, bf16[16,1280]{1,0:T(8,128)(2,1)S(1)}, u32[]{:S(2)}, u32[]{:S(2)}) collective-permute-start(bf16[16,1280]{1,0:T(8,128)(2,1)} %get-tuple-element.51), channel_id=1, source_target_pairs={{0,3},{1,2},{2,1},{3,0},{4,7},{5,6},{6,5},{7,4},{8,11},{9,10},{10,... | collective-permute-start | bytes 122888 | tf_op jit(solution)/shard_map/ppermute | solution.py:452
  6.3 7.8 %collective-permute-start.6 = (bf16[128,640]{1,0:T(8,128)(2,1)}, bf16[128,640]{1,0:T(8,128)(2,1)S(1)}, u32[]{:S(2)}, u32[]{:S(2)}) collective-permute-start(bf16[128,640]{1,0:T(8,128)(2,1)} %get-tuple-element.52), channel_id=1, source_target_pairs={{0,2},{1,3},{2,0},{3,1},{4,6},{5,7},{6,4},{7,5},{8,10},{9,11},{10,... | collective-permute-start | bytes 491528 | tf_op jit(solution)/shard_map/ppermute | solution.py:452
  8.0 9.0 %collective-permute-start.7 = (bf16[128,640]{1,0:T(8,128)(2,1)}, bf16[128,640]{1,0:T(8,128)(2,1)S(1)}, u32[]{:S(2)}, u32[]{:S(2)}) collective-permute-start(bf16[128,640]{1,0:T(8,128)(2,1)} %get-tuple-element.53), channel_id=1, source_target_pairs={{0,3},{1,2},{2,1},{3,0},{4,7},{5,6},{6,5},{7,4},{8,11},{9,10},{10,... | collective-permute-start | bytes 491528 | tf_op jit(solution)/shard_map/ppermute | solution.py:452
  8.4 1.6 %copy-start.5 = (bf16[16,1280]{1,0:T(8,128)(2,1)S(1)}, bf16[16,1280]{1,0:T(8,128)(2,1)}, u32[]{:S(2)}) copy-start(bf16[16,1280]{1,0:T(8,128)(2,1)} %get-tuple-element.49.tail_ref) | copy-start | bytes 122884
  8.5 3.2 %copy-start = (bf16[128,8192]{1,0:T(8,128)(2,1)S(1)}, bf16[128,8192]{1,0:T(8,128)(2,1)}, u32[]{:S(2)}) copy-start(bf16[128,8192]{1,0:T(8,128)(2,1)} %refs_0_.5) | copy-start | bytes 6291460
  10.1 8.1 %copy-start.2 = (bf16[128,2048]{1,0:T(8,128)(2,1)S(1)}, bf16[128,2048]{1,0:T(8,128)(2,1)}, u32[]{:S(2)}) copy-start(bf16[128,2048]{1,0:T(8,128)(2,1)} %bc_ref.3) | copy-start | bytes 1572868
  10.1 8.1 %copy-start.3 = (bf16[128,128]{1,0:T(8,128)(2,1)S(1)}, bf16[128,128]{1,0:T(8,128)(2,1)}, u32[]{:S(2)}) copy-start(bf16[128,128]{1,0:T(8,128)(2,1)} %dt_ref.3) | copy-start | bytes 98308
  10.1 8.1 %collective-permute-start.5 = (bf16[16,1280]{1,0:T(8,128)(2,1)S(1)}, bf16[16,1280]{1,0:T(8,128)(2,1)S(1)}, u32[]{:S(2)}, u32[]{:S(2)}) collective-permute-start(bf16[16,1280]{1,0:T(8,128)(2,1)S(1)} %relay.1), channel_id=1, source_target_pairs={{0,4},{1,5},{2,6},{3,7},{4,8},{5,9},{6,10},{7,11},{8,12},{9,13},{1... | collective-permute-start | bytes 122888 | tf_op jit(solution)/shard_map/ppermute | solution.py:455
  11.9 8.8 %collective-permute-start.1 = (bf16[128,512]{1,0:T(8,128)(2,1)S(1)}, bf16[128,512]{1,0:T(8,128)(2,1)S(1)}, u32[]{:S(2)}, u32[]{:S(2)}) collective-permute-start(bf16[128,512]{1,0:T(8,128)(2,1)S(1)} %get-tuple-element.47), channel_id=1, source_target_pairs={{0,2},{1,3},{2,0},{3,1},{4,6},{5,7},{6,4},{7,5},{8,10},{9,11},{10,... | collective-permute-start | bytes 393224 | tf_op jit(solution)/shard_map/ppermute | solution.py:452
  12.9 9.8 %collective-permute-start.2 = (bf16[128,512]{1,0:T(8,128)(2,1)S(1)}, bf16[128,512]{1,0:T(8,128)(2,1)S(1)}, u32[]{:S(2)}, u32[]{:S(2)}) collective-permute-start(bf16[128,512]{1,0:T(8,128)(2,1)S(1)} %get-tuple-element.48), channel_id=1, source_target_pairs={{0,3},{1,2},{2,1},{3,0},{4,7},{5,6},{6,5},{7,4},{8,11},{9,10},{10,... | collective-permute-start | bytes 393224 | tf_op jit(solution)/shard_map/ppermute | solution.py:452
  14.0 14.7 %collective-permute-start.10 = (bf16[128,768]{1,0:T(8,128)(2,1)S(1)}, bf16[128,768]{1,0:T(8,128)(2,1)S(1)}, u32[]{:S(2)}, u32[]{:S(2)}) collective-permute-start(bf16[128,768]{1,0:T(8,128)(2,1)S(1)} %get-tuple-element.63), channel_id=1, source_target_pairs={{0,2},{1,3},{2,0},{3,1},{4,6},{5,7},{6,4},{7,5},{8,10},{9,11},{10,... | collective-permute-start | bytes 589832 | tf_op jit(solution)/shard_map/ppermute | solution.py:452
  17.0 14.0 %collective-permute-start.11 = (bf16[128,768]{1,0:T(8,128)(2,1)S(1)}, bf16[128,768]{1,0:T(8,128)(2,1)S(1)}, u32[]{:S(2)}, u32[]{:S(2)}) collective-permute-start(bf16[128,768]{1,0:T(8,128)(2,1)S(1)} %get-tuple-element.64), channel_id=1, source_target_pairs={{0,3},{1,2},{2,1},{3,0},{4,7},{5,6},{6,5},{7,4},{8,11},{9,10},{10,... | collective-permute-start | bytes 589832 | tf_op jit(solution)/shard_map/ppermute | solution.py:452
  25.0 10.8 %collective-permute-start.8 = (bf16[256,512]{1,0:T(8,128)(2,1)S(1)}, bf16[256,512]{1,0:T(8,128)(2,1)S(1)}, u32[]{:S(2)}, u32[]{:S(2)}) collective-permute-start(bf16[256,512]{1,0:T(8,128)(2,1)S(1)} %get-tuple-element.58.after_ref), channel_id=1, source_target_pairs={{0,4},{1,5},{2,6},{3,7},{4,8},{5,9},{6,10},{7,11},{8,12},{9,13},{1... | collective-permute-start | bytes 786440 | tf_op jit(solution)/shard_map/ppermute | solution.py:455
  27.3 11.9 %collective-permute-start.15 = (bf16[128,768]{1,0:T(8,128)(2,1)S(1)}, bf16[128,768]{1,0:T(8,128)(2,1)S(1)}, u32[]{:S(2)}, u32[]{:S(2)}) collective-permute-start(bf16[128,768]{1,0:T(8,128)(2,1)S(1)} %get-tuple-element.72), channel_id=1, source_target_pairs={{0,2},{1,3},{2,0},{3,1},{4,6},{5,7},{6,4},{7,5},{8,10},{9,11},{10,... | collective-permute-start | bytes 589832 | tf_op jit(solution)/shard_map/ppermute | solution.py:452
  28.1 11.4 %collective-permute-start.16 = (bf16[128,768]{1,0:T(8,128)(2,1)S(1)}, bf16[128,768]{1,0:T(8,128)(2,1)S(1)}, u32[]{:S(2)}, u32[]{:S(2)}) collective-permute-start(bf16[128,768]{1,0:T(8,128)(2,1)S(1)} %get-tuple-element.73), channel_id=1, source_target_pairs={{0,3},{1,2},{2,1},{3,0},{4,7},{5,6},{6,5},{7,4},{8,11},{9,10},{10,... | collective-permute-start | bytes 589832 | tf_op jit(solution)/shard_map/ppermute | solution.py:452
  34.2 13.6 %collective-permute-start.12 = (bf16[256,768]{1,0:T(8,128)(2,1)S(1)}, bf16[256,768]{1,0:T(8,128)(2,1)S(1)}, u32[]{:S(2)}, u32[]{:S(2)}) collective-permute-start(bf16[256,768]{1,0:T(8,128)(2,1)S(1)} %get-tuple-element.65), channel_id=1, source_target_pairs={{0,4},{1,5},{2,6},{3,7},{4,8},{5,9},{6,10},{7,11},{8,12},{9,13},{1... | collective-permute-start | bytes 1179656 | tf_op jit(solution)/shard_map/ppermute | solution.py:455
  37.4 7.0 %collective-permute-start.9 = (bf16[128,512]{1,0:T(8,128)(2,1)S(1)}, bf16[128,512]{1,0:T(8,128)(2,1)S(1)}, u32[]{:S(2)}, u32[]{:S(2)}) collective-permute-start(bf16[128,512]{1,0:T(8,128)(2,1)S(1)} %get-tuple-element.62), channel_id=1, source_target_pairs={{0,2},{1,3},{2,0},{3,1},{4,6},{5,7},{6,4},{7,5},{8,10},{9,11},{10,... | collective-permute-start | bytes 393224 | tf_op jit(solution)/shard_map/ppermute | solution.py:452
  38.4 7.1 %collective-permute-start.13 = (bf16[128,512]{1,0:T(8,128)(2,1)S(1)}, bf16[128,512]{1,0:T(8,128)(2,1)S(1)}, u32[]{:S(2)}, u32[]{:S(2)}) collective-permute-start(bf16[128,512]{1,0:T(8,128)(2,1)S(1)} %get-tuple-element.70), channel_id=1, source_target_pairs={{0,3},{1,2},{2,1},{3,0},{4,7},{5,6},{6,5},{7,4},{8,11},{9,10},{10,... | collective-permute-start | bytes 393224 | tf_op jit(solution)/shard_map/ppermute | solution.py:452
  42.6 14.9 %collective-permute-start.17 = (bf16[256,768]{1,0:T(8,128)(2,1)S(1)}, bf16[256,768]{1,0:T(8,128)(2,1)S(1)}, u32[]{:S(2)}, u32[]{:S(2)}) collective-permute-start(bf16[256,768]{1,0:T(8,128)(2,1)S(1)} %get-tuple-element.74), channel_id=1, source_target_pairs={{0,4},{1,5},{2,6},{3,7},{4,8},{5,9},{6,10},{7,11},{8,12},{9,13},{1... | collective-permute-start | bytes 1179656 | tf_op jit(solution)/shard_map/ppermute | solution.py:455
  49.6 7.9 %collective-permute-start.14 = (bf16[128,768]{1,0:T(8,128)(2,1)S(1)}, bf16[128,768]{1,0:T(8,128)(2,1)S(1)}, u32[]{:S(2)}, u32[]{:S(2)}) collective-permute-start(bf16[128,768]{1,0:T(8,128)(2,1)S(1)} %get-tuple-element.71), channel_id=1, source_target_pairs={{0,2},{1,3},{2,0},{3,1},{4,6},{5,7},{6,4},{7,5},{8,10},{9,11},{10,... | collective-permute-start | bytes 589832 | tf_op jit(solution)/shard_map/ppermute | solution.py:452
  50.4 9.0 %collective-permute-start.18 = (bf16[128,768]{1,0:T(8,128)(2,1)S(1)}, bf16[128,768]{1,0:T(8,128)(2,1)S(1)}, u32[]{:S(2)}, u32[]{:S(2)}) collective-permute-start(bf16[128,768]{1,0:T(8,128)(2,1)S(1)} %get-tuple-element.79), channel_id=1, source_target_pairs={{0,3},{1,2},{2,1},{3,0},{4,7},{5,6},{6,5},{7,4},{8,11},{9,10},{10,... | collective-permute-start | bytes 589832 | tf_op jit(solution)/shard_map/ppermute | solution.py:452
  59.4 7.6 %copy-start.1 = (bf16[128,8192]{1,0:T(8,128)(2,1)S(1)}, bf16[128,8192]{1,0:T(8,128)(2,1)}, u32[]{:S(2)}) copy-start(bf16[128,8192]{1,0:T(8,128)(2,1)} %refs_6_.1) | copy-start | bytes 6291460
  59.4 7.6 %copy-start.4 = (f32[8192]{0:T(1024)S(1)}, f32[8192]{0:T(1024)}, u32[]{:S(2)}) copy-start(f32[8192]{0:T(1024)} %param.21) | copy-start | bytes 98308
  61.3 5.7 %collective-permute-start.21 = (bf16[128,2048]{1,0:T(8,128)(2,1)S(1)}, bf16[128,2048]{1,0:T(8,128)(2,1)S(1)}, u32[]{:S(2)}, u32[]{:S(2)}) collective-permute-start(bf16[128,2048]{1,0:T(8,128)(2,1)S(1)} %get-tuple-element.85), channel_id=1, source_target_pairs={{0,1},{1,0},{2,3},{3,2},{4,5},{5,4},{6,7},{7,6},{8,9},{9,8},{10,11... | collective-permute-start | bytes 1572872 | tf_op jit(solution)/shard_map/ppermute | solution.py:452
  62.3 3.7 %collective-permute-start.22 = (f32[16,128]{1,0:T(8,128)S(1)}, f32[16,128]{1,0:T(8,128)S(1)}, u32[]{:S(2)}, u32[]{:S(2)}) collective-permute-start(f32[16,128]{1,0:T(8,128)S(1)} %get-tuple-element.88), channel_id=1, source_target_pairs={{0,4},{1,5},{2,6},{3,7},{4,0},{5,1},{6,2},{7,3},{8,12},{9,13},{10,... | collective-permute-start | bytes 24584 | tf_op jit(solution)/shard_map/ppermute | solution.py:452
  62.4 10.3 %collective-permute-start.19 = (bf16[128,768]{1,0:T(8,128)(2,1)S(1)}, bf16[128,768]{1,0:T(8,128)(2,1)S(1)}, u32[]{:S(2)}, u32[]{:S(2)}) collective-permute-start(bf16[128,768]{1,0:T(8,128)(2,1)S(1)} %get-tuple-element.80), channel_id=1, source_target_pairs={{0,2},{1,3},{2,0},{3,1},{4,6},{5,7},{6,4},{7,5},{8,10},{9,11},{10,... | collective-permute-start | bytes 589832 | tf_op jit(solution)/shard_map/ppermute | solution.py:452
  63.5 9.2 %collective-permute-start.20 = (bf16[128,768]{1,0:T(8,128)(2,1)S(1)}, bf16[128,768]{1,0:T(8,128)(2,1)S(1)}, u32[]{:S(2)}, u32[]{:S(2)}) collective-permute-start(bf16[128,768]{1,0:T(8,128)(2,1)S(1)} %get-tuple-element.81), channel_id=1, source_target_pairs={{0,3},{1,2},{2,1},{3,0},{4,7},{5,6},{6,5},{7,4},{8,11},{9,10},{10,... | collective-permute-start | bytes 589832 | tf_op jit(solution)/shard_map/ppermute | solution.py:452
  66.0 4.5 %collective-permute-start.23 = (f32[16,128]{1,0:T(8,128)S(1)}, f32[16,128]{1,0:T(8,128)S(1)}, u32[]{:S(2)}, u32[]{:S(2)}) collective-permute-start(f32[16,128]{1,0:T(8,128)S(1)} %add.26.one_ref), channel_id=1, source_target_pairs={{0,8},{1,9},{2,10},{3,11},{4,12},{5,13},{6,14},{7,15},{8,0},{9,1},... | collective-permute-start | bytes 24584 | tf_op jit(solution)/shard_map/ppermute | solution.py:452
  70.5 1.2 %collective-permute-start.24 = (f32[16,128]{1,0:T(8,128)S(1)}, f32[16,128]{1,0:T(8,128)S(1)}, u32[]{:S(2)}, u32[]{:S(2)}) collective-permute-start(f32[16,128]{1,0:T(8,128)S(1)} %add.38), channel_id=1, source_target_pairs={{0,1},{1,0},{2,3},{3,2},{4,5},{5,4},{6,7},{7,6},{8,9},{9,8},{10,11... | collective-permute-start | bytes 24584 | tf_op jit(solution)/shard_map/ppermute | solution.py:452
  71.7 3.7 %collective-permute-start.25 = (f32[16,128]{1,0:T(8,128)S(1)}, f32[16,128]{1,0:T(8,128)S(1)}, u32[]{:S(2)}, u32[]{:S(2)}) collective-permute-start(f32[16,128]{1,0:T(8,128)S(1)} %add.27), channel_id=1, source_target_pairs={{0,2},{1,3},{2,0},{3,1},{4,6},{5,7},{6,4},{7,5},{8,10},{9,11},{10,... | collective-permute-start | bytes 24584 | tf_op jit(solution)/shard_map/ppermute | solution.py:452

commit v5 on v4

--- a/solution.py
+++ b/solution.py
@@ -11,7 +11,7 @@
 SPAN = 512
 DOCS = 16
 HALO = 16
-PARTS = (2, 3, 3)
+PARTS = (4, 5, 7)
 LANES = 128
 VMEM_LIMIT = 20 * 1024 * 1024
 VMEM_MOST = 60 * 1024 * 1024
@@ -292,9 +292,12 @@
 
 def spreader(first, width, hdim, own_heads, upper):
     row, col = iota((LANES, width), 0), iota((LANES, width), 1)
-    hit = (row % own_heads) == (first + col // hdim)
-    half = (row >= 2 * own_heads) if upper else (row < 2 * own_heads)
-    return jnp.where(hit & half, 1.0, 0.0).astype(BF16)
+    place = 2 * own_heads if upper else 0
+    start = (row - place) * hdim
+    start = jnp.where(row >= place + own_heads, start - own_heads * hdim, start) - first * hdim
+    inside = (row >= place) & (row < place + 2 * own_heads)
+    start = jnp.where(inside, start, 2 * own_heads * hdim)
+    return jnp.where((col >= start) & (col < start + hdim), 1.0, 0.0).astype(BF16)
 
 
 def mix_kernel(team, taps, hdim, gw, start, places, rank_ref, *refs):
@@ -442,7 +445,7 @@
     team = SPAN // rows
     tiles = SPAN // LANES
     gw = inner // team
-    chunks = [gw // 8 * part for part in PARTS]
+    chunks = [gw // 16 * part for part in PARTS]
     me = lax.axis_index("seq")
     rank = jnp.reshape(me % team, (1,)).astype(jnp.int32)
     doc_most = rows * members // 4

time: 76.2 us -> 76.2 us (level)
  waiting for transfers between devices: 26.1 us -> 24.2 us
  starting transfers between devices: 24.5 us -> 25.5 us
  Pallas kernels: 23.5 us -> 24.4 us
    ppermute x22, waiting for transfers between devices: 23.9 us -> 21.9 us  [swap(): return lax.ppermute(array, 'seq', [(i, i ^ k) for i in range(members)])]
    ppermute x22, starting transfers between devices: 17.8 us -> 18.7 us  [swap(): return lax.ppermute(array, 'seq', [(i, i ^ k) for i in range(members)])]
    pallas_call x15, Pallas kernels: 23.5 us -> 24.4 us  [call(): pl.pallas_call(kernel, grid_spec=pltpu.PrefetchScalarGridSpec(num_scalar_...]
  transfers between devices with their start and end apart: 26 -> 26, of which waited for: 14 -> 15; matrix products, arithmetic and copies ran while one was open for 0% -> 0% of each run, Pallas kernels for 25% -> 26%
where the time goes in v5:
time: 76.2 us; the launch traced here: 76 us
  starting transfers between devices  25.5 us (33%)
  Pallas kernels  24.4 us (32%)
  waiting for transfers between devices  24.2 us (32%)
  other arithmetic  0.94 us (1%)
  between operations  0.9 us (1%)
    pallas_call x15, Pallas kernels, call(): pl.pallas_call(kernel, grid_spec=pltpu.PrefetchScalarGridSpec(num_scalar_...  24.4 us
    ppermute x22, waiting for transfers between devices, swap(): return lax.ppermute(array, 'seq', [(i, i ^ k) for i in range(members)])  21.9 us
    ppermute x22, starting transfers between devices, swap(): return lax.ppermute(array, 'seq', [(i, i ^ k) for i in range(members)])  18.7 us
    ppermute x4, starting transfers between devices, onward(): lax.ppermute(array, 'seq', [(i, (i + team) % members) for i in range(memb...  6.71 us
    ppermute x4, waiting for transfers between devices, onward(): lax.ppermute(array, 'seq', [(i, (i + team) % members) for i in range(memb...  2.28 us
  transfers between devices with their start and end apart: 26, of which 15 were waited for; matrix products, arithmetic and copies ran while one was open for 0% of the time, Pallas kernels for 26%

profile of v5, /device:TPU:0, one launch (start us, length us, event | category | flops | bytes accessed | tf_op | source)
XLA Modules:
  0.0 76.0 jit_solution(18299926335148763112)
XLA Ops:
  0.7 2.4 %pack.1 = (bf16[128,640]{1,0:T(8,128)(2,1)}, bf16[128,640]{1,0:T(8,128)(2,1)}, bf16[128,2688]{1,0:T(8,128)(2,1)}, bf16[16,1280]{1,0:T(8,128)(2,1)}, bf16[16,1280]{1,0:T(8,128)(2,1)}, /*index=5*/bf16[16,1280]{1,0:T(8,128)(2,1)}) custom-call(s32[1]{0:T(128)} %bitcast.rank_ref, bf16[128,8192]{1,0:T(8,128)(2,1)} %refs_0_.5, bf16[128,2048]{1,0:T(8,128)(2,1)} %bc_ref.3, ...), custom_call_target="tpu_custom_call" | custom-call | flops 2000000000 | bytes 6000000 | tf_op jit(solution)/shard_map/pack/pallas_call | solution.py:33
  3.1 0.5 collective-permute-start
  3.6 2.6 %collective-permute-start.3 = (bf16[16,1280]{1,0:T(8,128)(2,1)}, bf16[16,1280]{1,0:T(8,128)(2,1)S(1)}, u32[]{:S(2)}, u32[]{:S(2)}) collective-permute-start(bf16[16,1280]{1,0:T(8,128)(2,1)} %get-tuple-element.50), channel_id=1, source_target_pairs={{0,2},{1,3},{2,0},{3,1},{4,6},{5,7},{6,4},{7,5},{8,10},{9,11},{10,... | collective-permute-start | bytes 122888 | tf_op jit(solution)/shard_map/ppermute | solution.py:455
  6.3 1.7 %collective-permute-start.6 = (bf16[128,640]{1,0:T(8,128)(2,1)}, bf16[128,640]{1,0:T(8,128)(2,1)S(1)}, u32[]{:S(2)}, u32[]{:S(2)}) collective-permute-start(bf16[128,640]{1,0:T(8,128)(2,1)} %get-tuple-element.52), channel_id=1, source_target_pairs={{0,2},{1,3},{2,0},{3,1},{4,6},{5,7},{6,4},{7,5},{8,10},{9,11},{10,... | collective-permute-start | bytes 491528 | tf_op jit(solution)/shard_map/ppermute | solution.py:455
  8.6 1.4 %collective-permute-done.4.refs_1_ = bf16[16,1280]{1,0:T(8,128)(2,1)S(1)} collective-permute-done((bf16[16,1280]{1,0:T(8,128)(2,1)}, bf16[16,1280]{1,0:T(8,128)(2,1)S(1)}, u32[]{:S(2)}, u32[]{:S(2)}) %collective-permute-start.4) | collective-permute-done | bytes 40992 | tf_op jit(solution)/shard_map/ppermute | solution.py:455
  10.1 1.6 %collective-permute-start.5 = (bf16[16,1280]{1,0:T(8,128)(2,1)S(1)}, bf16[16,1280]{1,0:T(8,128)(2,1)S(1)}, u32[]{:S(2)}, u32[]{:S(2)}) collective-permute-start(bf16[16,1280]{1,0:T(8,128)(2,1)S(1)} %relay.1), channel_id=1, source_target_pairs={{0,4},{1,5},{2,6},{3,7},{4,8},{5,9},{6,10},{7,11},{8,12},{9,13},{1... | collective-permute-start | bytes 122888 | tf_op jit(solution)/shard_map/ppermute | solution.py:458
  11.9 0.9 %collective-permute-start.1 = (bf16[128,512]{1,0:T(8,128)(2,1)S(1)}, bf16[128,512]{1,0:T(8,128)(2,1)S(1)}, u32[]{:S(2)}, u32[]{:S(2)}) collective-permute-start(bf16[128,512]{1,0:T(8,128)(2,1)S(1)} %get-tuple-element.47), channel_id=1, source_target_pairs={{0,2},{1,3},{2,0},{3,1},{4,6},{5,7},{6,4},{7,5},{8,10},{9,11},{10,... | collective-permute-start | bytes 393224 | tf_op jit(solution)/shard_map/ppermute | solution.py:455
  12.9 0.5 collective-permute-start.2
  13.4 0.6 collective-permute-done.6.refs_1_
  14.0 1.2 %collective-permute-start.10 = (bf16[128,640]{1,0:T(8,128)(2,1)S(1)}, bf16[128,640]{1,0:T(8,128)(2,1)S(1)}, u32[]{:S(2)}, u32[]{:S(2)}) collective-permute-start(bf16[128,640]{1,0:T(8,128)(2,1)S(1)} %get-tuple-element.63), channel_id=1, source_target_pairs={{0,2},{1,3},{2,0},{3,1},{4,6},{5,7},{6,4},{7,5},{8,10},{9,11},{10,... | collective-permute-start | bytes 491528 | tf_op jit(solution)/shard_map/ppermute | solution.py:455
  15.2 1.8 %collective-permute-done.7.refs_2_ = bf16[128,640]{1,0:T(8,128)(2,1)S(1)} collective-permute-done((bf16[128,640]{1,0:T(8,128)(2,1)}, bf16[128,640]{1,0:T(8,128)(2,1)S(1)}, u32[]{:S(2)}, u32[]{:S(2)}) %collective-permute-start.7) | collective-permute-done | bytes 163872 | tf_op jit(solution)/shard_map/ppermute | solution.py:455
  17.0 1.1 %collective-permute-start.11 = (bf16[128,640]{1,0:T(8,128)(2,1)S(1)}, bf16[128,640]{1,0:T(8,128)(2,1)S(1)}, u32[]{:S(2)}, u32[]{:S(2)}) collective-permute-start(bf16[128,640]{1,0:T(8,128)(2,1)S(1)} %get-tuple-element.64), channel_id=1, source_target_pairs={{0,3},{1,2},{2,1},{3,0},{4,7},{5,6},{6,5},{7,4},{8,11},{9,10},{10,... | collective-permute-start | bytes 491528 | tf_op jit(solution)/shard_map/ppermute | solution.py:455
  18.2 2.6 %bc.1 = (bf16[512,512]{1,0:T(8,128)(2,1)S(1)}, bf16[256,512]{1,0:T(8,128)(2,1)S(1)}, bf16[512,256]{1,0:T(8,128)(2,1)S(1)}, bf16[512,128]{1,0:T(8,128)(2,1)S(1)}, bf16[16,128]{1,0:T(8,128)(2,1)S(1)}) custom-call(s32[1]{0:T(128)} %bitcast.rank_ref, bf16[128,2048]{1,0:T(8,128)(2,1)S(1)} %copy-done.2, bf16[128,128]{1,0:T(8,128)(2,1)S(1)} %copy-done.3, ...), custom_call_target="tpu_custom_call" | custom-call | flops 4000000000 | bytes 12000000 | tf_op jit(solution)/shard_map/bc/pallas_call | solution.py:33
  20.8 1.9 %collective-permute-done.2.refs_3_ = bf16[128,512]{1,0:T(8,128)(2,1)S(1)} collective-permute-done((bf16[128,512]{1,0:T(8,128)(2,1)S(1)}, bf16[128,512]{1,0:T(8,128)(2,1)S(1)}, u32[]{:S(2)}, u32[]{:S(2)}) %collective-permute-start.2) | collective-permute-done | bytes 131104 | tf_op jit(solution)/shard_map/ppermute | solution.py:455
  22.6 2.4 %mix.3 = (bf16[512,512]{1,0:T(8,128)(2,1)S(1)}, f32[512,512]{1,0:T(8,128)S(1)}, bf16[256,512]{1,0:T(8,128)(2,1)S(1)}) custom-call(s32[1]{0:T(128)} %bitcast.rank_ref, bf16[128,8192]{1,0:T(8,128)(2,1)S(1)} %copy-done, bf16[128,2688]{1,0:T(8,128)(2,1)S(1)} %collective-permute-done.after_ref.near_ref.refs_0_.refs_1_, ...), custom_call_target="tpu_custom_call" | custom-call | flops 4000000000 | bytes 12000000 | tf_op jit(solution)/shard_map/mix/pallas_call | solution.py:33
  25.1 1.6 %collective-permute-start.8 = (bf16[256,512]{1,0:T(8,128)(2,1)S(1)}, bf16[256,512]{1,0:T(8,128)(2,1)S(1)}, u32[]{:S(2)}, u32[]{:S(2)}) collective-permute-start(bf16[256,512]{1,0:T(8,128)(2,1)S(1)} %get-tuple-element.58.after_ref), channel_id=1, source_target_pairs={{0,4},{1,5},{2,6},{3,7},{4,8},{5,9},{6,10},{7,11},{8,12},{9,13},{1... | collective-permute-start | bytes 786440 | tf_op jit(solution)/shard_map/ppermute | solution.py:458
  26.7 0.7 chunks.3
  27.4 0.8 %collective-permute-start.15 = (bf16[128,896]{1,0:T(8,128)(2,1)S(1)}, bf16[128,896]{1,0:T(8,128)(2,1)S(1)}, u32[]{:S(2)}, u32[]{:S(2)}) collective-permute-start(bf16[128,896]{1,0:T(8,128)(2,1)S(1)} %get-tuple-element.72), channel_id=1, source_target_pairs={{0,2},{1,3},{2,0},{3,1},{4,6},{5,7},{6,4},{7,5},{8,10},{9,11},{10,... | collective-permute-start | bytes 688136 | tf_op jit(solution)/shard_map/ppermute | solution.py:455
  28.2 0.7 collective-permute-start.16
  28.9 0.8 %collective-permute-done.11.refs_3_ = bf16[128,640]{1,0:T(8,128)(2,1)S(1)} collective-permute-done((bf16[128,640]{1,0:T(8,128)(2,1)S(1)}, bf16[128,640]{1,0:T(8,128)(2,1)S(1)}, u32[]{:S(2)}, u32[]{:S(2)}) %collective-permute-start.11) | collective-permute-done | bytes 163872 | tf_op jit(solution)/shard_map/ppermute | solution.py:455
  29.7 2.9 %mix.4 = (bf16[512,640]{1,0:T(8,128)(2,1)S(1)}, f32[512,640]{1,0:T(8,128)S(1)}, bf16[256,640]{1,0:T(8,128)(2,1)S(1)}) custom-call(s32[1]{0:T(128)} %bitcast.rank_ref, bf16[128,8192]{1,0:T(8,128)(2,1)S(1)} %copy-done, bf16[128,2688]{1,0:T(8,128)(2,1)S(1)} %collective-permute-done.after_ref.near_ref.refs_0_.refs_1_, ...), custom_call_target="tpu_custom_call" | custom-call | flops 4000000000 | bytes 12000000 | tf_op jit(solution)/shard_map/mix/pallas_call | solution.py:33
  32.6 1.8 %collective-permute-start.12 = (bf16[256,640]{1,0:T(8,128)(2,1)S(1)}, bf16[256,640]{1,0:T(8,128)(2,1)S(1)}, u32[]{:S(2)}, u32[]{:S(2)}) collective-permute-start(bf16[256,640]{1,0:T(8,128)(2,1)S(1)} %get-tuple-element.65), channel_id=1, source_target_pairs={{0,4},{1,5},{2,6},{3,7},{4,8},{5,9},{6,10},{7,11},{8,12},{9,13},{1... | collective-permute-start | bytes 983048 | tf_op jit(solution)/shard_map/ppermute | solution.py:458
  34.4 1.1 %collective-permute-done.8.st_ref = bf16[256,512]{1,0:T(8,128)(2,1)S(1)} collective-permute-done((bf16[256,512]{1,0:T(8,128)(2,1)S(1)}, bf16[256,512]{1,0:T(8,128)(2,1)S(1)}, u32[]{:S(2)}, u32[]{:S(2)}) %collective-permute-start.8) | collective-permute-done | bytes 262176 | tf_op jit(solution)/shard_map/ppermute | solution.py:458
  35.5 1.6 %carry.3 = (bf16[128,512]{1,0:T(8,128)(2,1)S(1)}, bf16[128,2048]{1,0:T(8,128)(2,1)S(1)}, bf16[128,512]{1,0:T(8,128)(2,1)S(1)}, bf16[128,512]{1,0:T(8,128)(2,1)S(1)}, f32[16,128]{1,0:T(8,128)S(1)}) custom-call(s32[1]{0:T(128)} %bitcast.rank_ref, bf16[256,512]{1,0:T(8,128)(2,1)S(1)} %collective-permute-done.8.st_ref, f32[512,512]{1,0:T(8,128)S(1)} %get-tuple-element.59.yl_ref, ...), custom_call_target="tpu_custom_call" | custom-call | flops 3000000000 | bytes 9000000 | tf_op jit(solution)/shard_map/carry/pallas_call | solution.py:33
  37.2 1.2 %collective-permute-start.9 = (bf16[128,512]{1,0:T(8,128)(2,1)S(1)}, bf16[128,512]{1,0:T(8,128)(2,1)S(1)}, u32[]{:S(2)}, u32[]{:S(2)}) collective-permute-start(bf16[128,512]{1,0:T(8,128)(2,1)S(1)} %get-tuple-element.62), channel_id=1, source_target_pairs={{0,2},{1,3},{2,0},{3,1},{4,6},{5,7},{6,4},{7,5},{8,10},{9,11},{10,... | collective-permute-start | bytes 393224 | tf_op jit(solution)/shard_map/ppermute | solution.py:455
  38.4 0.6 collective-permute-done.16.refs_3_
  39.0 3.9 %mix.5 = (bf16[512,896]{1,0:T(8,128)(2,1)S(1)}, f32[512,896]{1,0:T(8,128)S(1)}, bf16[256,896]{1,0:T(8,128)(2,1)S(1)}) custom-call(s32[1]{0:T(128)} %bitcast.rank_ref, bf16[128,8192]{1,0:T(8,128)(2,1)S(1)} %copy-done, bf16[128,2688]{1,0:T(8,128)(2,1)S(1)} %collective-permute-done.after_ref.near_ref.refs_0_.refs_1_, ...), custom_call_target="tpu_custom_call" | custom-call | flops 4000000000 | bytes 12000000 | tf_op jit(solution)/shard_map/mix/pallas_call | solution.py:33
  43.0 1.6 %collective-permute-start.17 = (bf16[256,896]{1,0:T(8,128)(2,1)S(1)}, bf16[256,896]{1,0:T(8,128)(2,1)S(1)}, u32[]{:S(2)}, u32[]{:S(2)}) collective-permute-start(bf16[256,896]{1,0:T(8,128)(2,1)S(1)} %get-tuple-element.74), channel_id=1, source_target_pairs={{0,4},{1,5},{2,6},{3,7},{4,8},{5,9},{6,10},{7,11},{8,12},{9,13},{1... | collective-permute-start | bytes 1376264 | tf_op jit(solution)/shard_map/ppermute | solution.py:458
  44.6 0.3 collective-permute-done.12.st_ref
  44.9 1.8 %carry.4 = (bf16[128,640]{1,0:T(8,128)(2,1)S(1)}, bf16[128,2048]{1,0:T(8,128)(2,1)S(1)}, bf16[128,640]{1,0:T(8,128)(2,1)S(1)}, bf16[128,640]{1,0:T(8,128)(2,1)S(1)}, f32[16,128]{1,0:T(8,128)S(1)}) custom-call(s32[1]{0:T(128)} %bitcast.rank_ref, bf16[256,640]{1,0:T(8,128)(2,1)S(1)} %collective-permute-done.12.st_ref, ...), custom_call_target="tpu_custom_call", output_to_operand_aliasing={{1}: (8, {})} | custom-call | flops 3000000000 | bytes 9000000 | tf_op jit(solution)/shard_map/carry/pallas_call | solution.py:33
  46.7 1.5 %collective-permute-start.14 = (bf16[128,640]{1,0:T(8,128)(2,1)S(1)}, bf16[128,640]{1,0:T(8,128)(2,1)S(1)}, u32[]{:S(2)}, u32[]{:S(2)}) collective-permute-start(bf16[128,640]{1,0:T(8,128)(2,1)S(1)} %get-tuple-element.71), channel_id=1, source_target_pairs={{0,2},{1,3},{2,0},{3,1},{4,6},{5,7},{6,4},{7,5},{8,10},{9,11},{10,... | collective-permute-start | bytes 491528 | tf_op jit(solution)/shard_map/ppermute | solution.py:455
  48.3 1.2 %collective-permute-start.18 = (bf16[128,640]{1,0:T(8,128)(2,1)S(1)}, bf16[128,640]{1,0:T(8,128)(2,1)S(1)}, u32[]{:S(2)}, u32[]{:S(2)}) collective-permute-start(bf16[128,640]{1,0:T(8,128)(2,1)S(1)} %get-tuple-element.79), channel_id=1, source_target_pairs={{0,3},{1,2},{2,1},{3,0},{4,7},{5,6},{6,5},{7,4},{8,11},{9,10},{10,... | collective-permute-start | bytes 491528 | tf_op jit(solution)/shard_map/ppermute | solution.py:455
  49.5 4.1 %collective-permute-done.14.refs_2_.refs_1_ = bf16[128,640]{1,0:T(8,128)(2,1)S(1)} collective-permute-done((bf16[128,640]{1,0:T(8,128)(2,1)S(1)}, bf16[128,640]{1,0:T(8,128)(2,1)S(1)}, u32[]{:S(2)}, u32[]{:S(2)}) %collective-permute-start.14) | collective-permute-done | bytes 163872 | tf_op jit(solution)/shard_map/ppermute | solution.py:455
  53.6 3.8 %collective-permute-done.18.refs_3_.refs_4_ = bf16[128,640]{1,0:T(8,128)(2,1)S(1)} collective-permute-done((bf16[128,640]{1,0:T(8,128)(2,1)S(1)}, bf16[128,640]{1,0:T(8,128)(2,1)S(1)}, u32[]{:S(2)}, u32[]{:S(2)}) %collective-permute-start.18) | collective-permute-done | bytes 163872 | tf_op jit(solution)/shard_map/ppermute | solution.py:455
  57.4 0.9 %collective-permute-done.17.st_ref = bf16[256,896]{1,0:T(8,128)(2,1)S(1)} collective-permute-done((bf16[256,896]{1,0:T(8,128)(2,1)S(1)}, bf16[256,896]{1,0:T(8,128)(2,1)S(1)}, u32[]{:S(2)}, u32[]{:S(2)}) %collective-permute-start.17) | collective-permute-done | bytes 458784 | tf_op jit(solution)/shard_map/ppermute | solution.py:458
  58.2 2.1 %carry.5 = (bf16[128,896]{1,0:T(8,128)(2,1)S(1)}, bf16[128,2048]{1,0:T(8,128)(2,1)S(1)}, bf16[128,896]{1,0:T(8,128)(2,1)S(1)}, bf16[128,896]{1,0:T(8,128)(2,1)S(1)}, f32[16,128]{1,0:T(8,128)S(1)}) custom-call(s32[1]{0:T(128)} %bitcast.rank_ref, bf16[256,896]{1,0:T(8,128)(2,1)S(1)} %collective-permute-done.17.st_ref, ...), custom_call_target="tpu_custom_call", output_to_operand_aliasing={{1}: (8, {})} | custom-call | flops 3000000000 | bytes 9000000 | tf_op jit(solution)/shard_map/carry/pallas_call | solution.py:33
  60.5 1.3 %collective-permute-start.19 = (bf16[128,896]{1,0:T(8,128)(2,1)S(1)}, bf16[128,896]{1,0:T(8,128)(2,1)S(1)}, u32[]{:S(2)}, u32[]{:S(2)}) collective-permute-start(bf16[128,896]{1,0:T(8,128)(2,1)S(1)} %get-tuple-element.80), channel_id=1, source_target_pairs={{0,2},{1,3},{2,0},{3,1},{4,6},{5,7},{6,4},{7,5},{8,10},{9,11},{10,... | collective-permute-start | bytes 688136 | tf_op jit(solution)/shard_map/ppermute | solution.py:455
  61.8 0.4 collective-permute-start.20
  62.2 0.5 collective-permute-start.22
  62.7 3.2 %collective-permute-done.22 = f32[16,128]{1,0:T(8,128)S(1)} collective-permute-done((f32[16,128]{1,0:T(8,128)S(1)}, f32[16,128]{1,0:T(8,128)S(1)}, u32[]{:S(2)}, u32[]{:S(2)}) %collective-permute-start.22) | collective-permute-done | bytes 8224 | tf_op jit(solution)/shard_map/ppermute | solution.py:455
  65.9 0.7 collective-permute-start.23
  66.6 1.8 %norm.2 = (bf16[128,8192]{1,0:T(8,128)(2,1)}, f32[8,128]{1,0:T(8,128)S(1)}) custom-call(s32[1]{0:T(128)} %bitcast.rank_ref, bf16[128,512]{1,0:T(8,128)(2,1)S(1)} %get-tuple-element.82.refs_0_, bf16[128,640]{1,0:T(8,128)(2,1)S(1)} %get-tuple-element.83.refs_1_, bf16[128,896]{1,0:T(8,128)(2,1)S(1)} %get-tuple-element.84.refs_2_, ...), custom_call_target="tpu_custom_call" | custom-call | flops 2000000000 | bytes 6000000 | tf_op jit(solution)/shard_map/norm/pallas_call | solution.py:33
  68.4 2.0 %collective-permute-done.23.other_ref = f32[16,128]{1,0:T(8,128)S(1)} collective-permute-done((f32[16,128]{1,0:T(8,128)S(1)}, f32[16,128]{1,0:T(8,128)S(1)}, u32[]{:S(2)}, u32[]{:S(2)}) %collective-permute-start.23) | collective-permute-done | bytes 8224 | tf_op jit(solution)/shard_map/ppermute | solution.py:455
  70.5 1.2 %collective-permute-done.24 = f32[16,128]{1,0:T(8,128)S(1)} collective-permute-done((f32[16,128]{1,0:T(8,128)S(1)}, f32[16,128]{1,0:T(8,128)S(1)}, u32[]{:S(2)}, u32[]{:S(2)}) %collective-permute-start.24) | collective-permute-done | bytes 8224 | tf_op jit(solution)/shard_map/ppermute | solution.py:455
  71.6 1.4 %collective-permute-start.25 = (f32[16,128]{1,0:T(8,128)S(1)}, f32[16,128]{1,0:T(8,128)S(1)}, u32[]{:S(2)}, u32[]{:S(2)}) collective-permute-start(f32[16,128]{1,0:T(8,128)S(1)} %add.27), channel_id=1, source_target_pairs={{0,2},{1,3},{2,0},{3,1},{4,6},{5,7},{6,4},{7,5},{8,10},{9,11},{10,... | collective-permute-start | bytes 24584 | tf_op jit(solution)/shard_map/ppermute | solution.py:455
  73.0 1.8 %norm.3 = (bf16[128,8192]{1,0:T(8,128)(2,1)}, f32[8,128]{1,0:T(8,128)}) custom-call(s32[1]{0:T(128)} %bitcast.rank_ref, bf16[128,512]{1,0:T(8,128)(2,1)S(1)} %collective-permute-done.9.refs_2_.refs_0_, bf16[128,640]{1,0:T(8,128)(2,1)S(1)} %collective-permute-done.14.refs_2_.refs_1_, ...), custom_call_target="tpu_custom_call", output_to_operand_aliasing={{0}: (9, {})} | custom-call | flops 2000000000 | bytes 6000000 | tf_op jit(solution)/shard_map/norm/pallas_call | solution.py:33
  74.8 0.5 collective-permute-done.25
  75.3 0.7 fusion.3
  (53 shorter events, 1.1 us)
Async XLA Ops:
  0.6 7.4 %copy-start.6 = (f32[4,10240]{1,0:T(4,128)S(1)}, f32[4,10240]{1,0:T(4,128)}, u32[]{:S(2)}) copy-start(f32[4,10240]{1,0:T(4,128)} %param.16) | copy-start | bytes 491524
  0.7 7.4 %copy-start.7 = (f32[10240]{0:T(1024)S(1)}, f32[10240]{0:T(1024)}, u32[]{:S(2)}) copy-start(f32[10240]{0:T(1024)} %param.17) | copy-start | bytes 122884
  0.7 7.4 %copy-start.8 = (s32[2048]{0:T(1024)S(1)}, s32[2048]{0:T(1024)}, u32[]{:S(2)}) copy-start(s32[2048]{0:T(1024)} %param.15) | copy-start | bytes 24580
  0.7 7.6 %copy-start.9 = (f32[128]{0:T(128)S(1)}, f32[128]{0:T(128)}, u32[]{:S(2)}) copy-start(f32[128]{0:T(128)} %param.20) | copy-start | bytes 1540
  0.7 7.6 %copy-start.10 = (f32[128]{0:T(128)S(1)}, f32[128]{0:T(128)}, u32[]{:S(2)}) copy-start(f32[128]{0:T(128)} %param.19) | copy-start | bytes 1540
  0.7 7.6 %copy-start.11 = (f32[128]{0:T(128)S(1)}, f32[128]{0:T(128)}, u32[]{:S(2)}) copy-start(f32[128]{0:T(128)} %param.18) | copy-start | bytes 1540
  3.1 6.9 %collective-permute-start = (bf16[128,2688]{1,0:T(8,128)(2,1)}, bf16[128,2688]{1,0:T(8,128)(2,1)S(1)}, u32[]{:S(2)}, u32[]{:S(2)}) collective-permute-start(bf16[128,2688]{1,0:T(8,128)(2,1)} %get-tuple-element.46), channel_id=1, source_target_pairs={{0,1},{1,0},{2,3},{3,2},{4,5},{5,4},{6,7},{7,6},{8,9},{9,8},{10,11... | collective-permute-start | bytes 2064392 | tf_op jit(solution)/shard_map/ppermute | solution.py:455
  3.6 5.0 %collective-permute-start.3 = (bf16[16,1280]{1,0:T(8,128)(2,1)}, bf16[16,1280]{1,0:T(8,128)(2,1)S(1)}, u32[]{:S(2)}, u32[]{:S(2)}) collective-permute-start(bf16[16,1280]{1,0:T(8,128)(2,1)} %get-tuple-element.50), channel_id=1, source_target_pairs={{0,2},{1,3},{2,0},{3,1},{4,6},{5,7},{6,4},{7,5},{8,10},{9,11},{10,... | collective-permute-start | bytes 122888 | tf_op jit(solution)/shard_map/ppermute | solution.py:455
  6.2 3.8 %collective-permute-start.4 = (bf16[16,1280]{1,0:T(8,128)(2,1)}, bf16[16,1280]{1,0:T(8,128)(2,1)S(1)}, u32[]{:S(2)}, u32[]{:S(2)}) collective-permute-start(bf16[16,1280]{1,0:T(8,128)(2,1)} %get-tuple-element.51), channel_id=1, source_target_pairs={{0,3},{1,2},{2,1},{3,0},{4,7},{5,6},{6,5},{7,4},{8,11},{9,10},{10,... | collective-permute-start | bytes 122888 | tf_op jit(solution)/shard_map/ppermute | solution.py:455
  6.3 7.8 %collective-permute-start.6 = (bf16[128,640]{1,0:T(8,128)(2,1)}, bf16[128,640]{1,0:T(8,128)(2,1)S(1)}, u32[]{:S(2)}, u32[]{:S(2)}) collective-permute-start(bf16[128,640]{1,0:T(8,128)(2,1)} %get-tuple-element.52), channel_id=1, source_target_pairs={{0,2},{1,3},{2,0},{3,1},{4,6},{5,7},{6,4},{7,5},{8,10},{9,11},{10,... | collective-permute-start | bytes 491528 | tf_op jit(solution)/shard_map/ppermute | solution.py:455
  8.0 9.0 %collective-permute-start.7 = (bf16[128,640]{1,0:T(8,128)(2,1)}, bf16[128,640]{1,0:T(8,128)(2,1)S(1)}, u32[]{:S(2)}, u32[]{:S(2)}) collective-permute-start(bf16[128,640]{1,0:T(8,128)(2,1)} %get-tuple-element.53), channel_id=1, source_target_pairs={{0,3},{1,2},{2,1},{3,0},{4,7},{5,6},{6,5},{7,4},{8,11},{9,10},{10,... | collective-permute-start | bytes 491528 | tf_op jit(solution)/shard_map/ppermute | solution.py:455
  8.4 1.6 %copy-start.5 = (bf16[16,1280]{1,0:T(8,128)(2,1)S(1)}, bf16[16,1280]{1,0:T(8,128)(2,1)}, u32[]{:S(2)}) copy-start(bf16[16,1280]{1,0:T(8,128)(2,1)} %get-tuple-element.49.tail_ref) | copy-start | bytes 122884
  8.5 3.2 %copy-start = (bf16[128,8192]{1,0:T(8,128)(2,1)S(1)}, bf16[128,8192]{1,0:T(8,128)(2,1)}, u32[]{:S(2)}) copy-start(bf16[128,8192]{1,0:T(8,128)(2,1)} %refs_0_.5) | copy-start | bytes 6291460
  10.1 8.1 %copy-start.2 = (bf16[128,2048]{1,0:T(8,128)(2,1)S(1)}, bf16[128,2048]{1,0:T(8,128)(2,1)}, u32[]{:S(2)}) copy-start(bf16[128,2048]{1,0:T(8,128)(2,1)} %bc_ref.3) | copy-start | bytes 1572868
  10.1 8.1 %copy-start.3 = (bf16[128,128]{1,0:T(8,128)(2,1)S(1)}, bf16[128,128]{1,0:T(8,128)(2,1)}, u32[]{:S(2)}) copy-start(bf16[128,128]{1,0:T(8,128)(2,1)} %dt_ref.3) | copy-start | bytes 98308
  10.1 8.1 %collective-permute-start.5 = (bf16[16,1280]{1,0:T(8,128)(2,1)S(1)}, bf16[16,1280]{1,0:T(8,128)(2,1)S(1)}, u32[]{:S(2)}, u32[]{:S(2)}) collective-permute-start(bf16[16,1280]{1,0:T(8,128)(2,1)S(1)} %relay.1), channel_id=1, source_target_pairs={{0,4},{1,5},{2,6},{3,7},{4,8},{5,9},{6,10},{7,11},{8,12},{9,13},{1... | collective-permute-start | bytes 122888 | tf_op jit(solution)/shard_map/ppermute | solution.py:458
  11.9 8.8 %collective-permute-start.1 = (bf16[128,512]{1,0:T(8,128)(2,1)S(1)}, bf16[128,512]{1,0:T(8,128)(2,1)S(1)}, u32[]{:S(2)}, u32[]{:S(2)}) collective-permute-start(bf16[128,512]{1,0:T(8,128)(2,1)S(1)} %get-tuple-element.47), channel_id=1, source_target_pairs={{0,2},{1,3},{2,0},{3,1},{4,6},{5,7},{6,4},{7,5},{8,10},{9,11},{10,... | collective-permute-start | bytes 393224 | tf_op jit(solution)/shard_map/ppermute | solution.py:455
  12.9 9.8 %collective-permute-start.2 = (bf16[128,512]{1,0:T(8,128)(2,1)S(1)}, bf16[128,512]{1,0:T(8,128)(2,1)S(1)}, u32[]{:S(2)}, u32[]{:S(2)}) collective-permute-start(bf16[128,512]{1,0:T(8,128)(2,1)S(1)} %get-tuple-element.48), channel_id=1, source_target_pairs={{0,3},{1,2},{2,1},{3,0},{4,7},{5,6},{6,5},{7,4},{8,11},{9,10},{10,... | collective-permute-start | bytes 393224 | tf_op jit(solution)/shard_map/ppermute | solution.py:455
  14.0 14.8 %collective-permute-start.10 = (bf16[128,640]{1,0:T(8,128)(2,1)S(1)}, bf16[128,640]{1,0:T(8,128)(2,1)S(1)}, u32[]{:S(2)}, u32[]{:S(2)}) collective-permute-start(bf16[128,640]{1,0:T(8,128)(2,1)S(1)} %get-tuple-element.63), channel_id=1, source_target_pairs={{0,2},{1,3},{2,0},{3,1},{4,6},{5,7},{6,4},{7,5},{8,10},{9,11},{10,... | collective-permute-start | bytes 491528 | tf_op jit(solution)/shard_map/ppermute | solution.py:455
  17.0 12.6 %collective-permute-start.11 = (bf16[128,640]{1,0:T(8,128)(2,1)S(1)}, bf16[128,640]{1,0:T(8,128)(2,1)S(1)}, u32[]{:S(2)}, u32[]{:S(2)}) collective-permute-start(bf16[128,640]{1,0:T(8,128)(2,1)S(1)} %get-tuple-element.64), channel_id=1, source_target_pairs={{0,3},{1,2},{2,1},{3,0},{4,7},{5,6},{6,5},{7,4},{8,11},{9,10},{10,... | collective-permute-start | bytes 491528 | tf_op jit(solution)/shard_map/ppermute | solution.py:455
  25.1 10.5 %collective-permute-start.8 = (bf16[256,512]{1,0:T(8,128)(2,1)S(1)}, bf16[256,512]{1,0:T(8,128)(2,1)S(1)}, u32[]{:S(2)}, u32[]{:S(2)}) collective-permute-start(bf16[256,512]{1,0:T(8,128)(2,1)S(1)} %get-tuple-element.58.after_ref), channel_id=1, source_target_pairs={{0,4},{1,5},{2,6},{3,7},{4,8},{5,9},{6,10},{7,11},{8,12},{9,13},{1... | collective-permute-start | bytes 786440 | tf_op jit(solution)/shard_map/ppermute | solution.py:458
  27.4 11.0 %collective-permute-start.15 = (bf16[128,896]{1,0:T(8,128)(2,1)S(1)}, bf16[128,896]{1,0:T(8,128)(2,1)S(1)}, u32[]{:S(2)}, u32[]{:S(2)}) collective-permute-start(bf16[128,896]{1,0:T(8,128)(2,1)S(1)} %get-tuple-element.72), channel_id=1, source_target_pairs={{0,2},{1,3},{2,0},{3,1},{4,6},{5,7},{6,4},{7,5},{8,10},{9,11},{10,... | collective-permute-start | bytes 688136 | tf_op jit(solution)/shard_map/ppermute | solution.py:455
  28.2 10.9 %collective-permute-start.16 = (bf16[128,896]{1,0:T(8,128)(2,1)S(1)}, bf16[128,896]{1,0:T(8,128)(2,1)S(1)}, u32[]{:S(2)}, u32[]{:S(2)}) collective-permute-start(bf16[128,896]{1,0:T(8,128)(2,1)S(1)} %get-tuple-element.73), channel_id=1, source_target_pairs={{0,3},{1,2},{2,1},{3,0},{4,7},{5,6},{6,5},{7,4},{8,11},{9,10},{10,... | collective-permute-start | bytes 688136 | tf_op jit(solution)/shard_map/ppermute | solution.py:455
  32.6 12.3 %collective-permute-start.12 = (bf16[256,640]{1,0:T(8,128)(2,1)S(1)}, bf16[256,640]{1,0:T(8,128)(2,1)S(1)}, u32[]{:S(2)}, u32[]{:S(2)}) collective-permute-start(bf16[256,640]{1,0:T(8,128)(2,1)S(1)} %get-tuple-element.65), channel_id=1, source_target_pairs={{0,4},{1,5},{2,6},{3,7},{4,8},{5,9},{6,10},{7,11},{8,12},{9,13},{1... | collective-permute-start | bytes 983048 | tf_op jit(solution)/shard_map/ppermute | solution.py:458
  37.2 7.7 %collective-permute-start.9 = (bf16[128,512]{1,0:T(8,128)(2,1)S(1)}, bf16[128,512]{1,0:T(8,128)(2,1)S(1)}, u32[]{:S(2)}, u32[]{:S(2)}) collective-permute-start(bf16[128,512]{1,0:T(8,128)(2,1)S(1)} %get-tuple-element.62), channel_id=1, source_target_pairs={{0,2},{1,3},{2,0},{3,1},{4,6},{5,7},{6,4},{7,5},{8,10},{9,11},{10,... | collective-permute-start | bytes 393224 | tf_op jit(solution)/shard_map/ppermute | solution.py:455
  38.4 6.5 %collective-permute-start.13 = (bf16[128,512]{1,0:T(8,128)(2,1)S(1)}, bf16[128,512]{1,0:T(8,128)(2,1)S(1)}, u32[]{:S(2)}, u32[]{:S(2)}) collective-permute-start(bf16[128,512]{1,0:T(8,128)(2,1)S(1)} %get-tuple-element.70), channel_id=1, source_target_pairs={{0,3},{1,2},{2,1},{3,0},{4,7},{5,6},{6,5},{7,4},{8,11},{9,10},{10,... | collective-permute-start | bytes 393224 | tf_op jit(solution)/shard_map/ppermute | solution.py:455
  43.0 15.2 %collective-permute-start.17 = (bf16[256,896]{1,0:T(8,128)(2,1)S(1)}, bf16[256,896]{1,0:T(8,128)(2,1)S(1)}, u32[]{:S(2)}, u32[]{:S(2)}) collective-permute-start(bf16[256,896]{1,0:T(8,128)(2,1)S(1)} %get-tuple-element.74), channel_id=1, source_target_pairs={{0,4},{1,5},{2,6},{3,7},{4,8},{5,9},{6,10},{7,11},{8,12},{9,13},{1... | collective-permute-start | bytes 1376264 | tf_op jit(solution)/shard_map/ppermute | solution.py:458
  46.7 6.8 %collective-permute-start.14 = (bf16[128,640]{1,0:T(8,128)(2,1)S(1)}, bf16[128,640]{1,0:T(8,128)(2,1)S(1)}, u32[]{:S(2)}, u32[]{:S(2)}) collective-permute-start(bf16[128,640]{1,0:T(8,128)(2,1)S(1)} %get-tuple-element.71), channel_id=1, source_target_pairs={{0,2},{1,3},{2,0},{3,1},{4,6},{5,7},{6,4},{7,5},{8,10},{9,11},{10,... | collective-permute-start | bytes 491528 | tf_op jit(solution)/shard_map/ppermute | solution.py:455
  48.3 9.1 %collective-permute-start.18 = (bf16[128,640]{1,0:T(8,128)(2,1)S(1)}, bf16[128,640]{1,0:T(8,128)(2,1)S(1)}, u32[]{:S(2)}, u32[]{:S(2)}) collective-permute-start(bf16[128,640]{1,0:T(8,128)(2,1)S(1)} %get-tuple-element.79), channel_id=1, source_target_pairs={{0,3},{1,2},{2,1},{3,0},{4,7},{5,6},{6,5},{7,4},{8,11},{9,10},{10,... | collective-permute-start | bytes 491528 | tf_op jit(solution)/shard_map/ppermute | solution.py:455
  58.2 8.4 %copy-start.1 = (bf16[128,8192]{1,0:T(8,128)(2,1)S(1)}, bf16[128,8192]{1,0:T(8,128)(2,1)}, u32[]{:S(2)}) copy-start(bf16[128,8192]{1,0:T(8,128)(2,1)} %refs_6_.1) | copy-start | bytes 6291460
  58.2 8.4 %copy-start.4 = (f32[8192]{0:T(1024)S(1)}, f32[8192]{0:T(1024)}, u32[]{:S(2)}) copy-start(f32[8192]{0:T(1024)} %param.21) | copy-start | bytes 98308
  60.3 6.3 %collective-permute-start.21 = (bf16[128,2048]{1,0:T(8,128)(2,1)S(1)}, bf16[128,2048]{1,0:T(8,128)(2,1)S(1)}, u32[]{:S(2)}, u32[]{:S(2)}) collective-permute-start(bf16[128,2048]{1,0:T(8,128)(2,1)S(1)} %get-tuple-element.85), channel_id=1, source_target_pairs={{0,1},{1,0},{2,3},{3,2},{4,5},{5,4},{6,7},{7,6},{8,9},{9,8},{10,11... | collective-permute-start | bytes 1572872 | tf_op jit(solution)/shard_map/ppermute | solution.py:455
  60.5 12.5 %collective-permute-start.19 = (bf16[128,896]{1,0:T(8,128)(2,1)S(1)}, bf16[128,896]{1,0:T(8,128)(2,1)S(1)}, u32[]{:S(2)}, u32[]{:S(2)}) collective-permute-start(bf16[128,896]{1,0:T(8,128)(2,1)S(1)} %get-tuple-element.80), channel_id=1, source_target_pairs={{0,2},{1,3},{2,0},{3,1},{4,6},{5,7},{6,4},{7,5},{8,10},{9,11},{10,... | collective-permute-start | bytes 688136 | tf_op jit(solution)/shard_map/ppermute | solution.py:455
  61.8 11.2 %collective-permute-start.20 = (bf16[128,896]{1,0:T(8,128)(2,1)S(1)}, bf16[128,896]{1,0:T(8,128)(2,1)S(1)}, u32[]{:S(2)}, u32[]{:S(2)}) collective-permute-start(bf16[128,896]{1,0:T(8,128)(2,1)S(1)} %get-tuple-element.81), channel_id=1, source_target_pairs={{0,3},{1,2},{2,1},{3,0},{4,7},{5,6},{6,5},{7,4},{8,11},{9,10},{10,... | collective-permute-start | bytes 688136 | tf_op jit(solution)/shard_map/ppermute | solution.py:455
  62.2 3.7 %collective-permute-start.22 = (f32[16,128]{1,0:T(8,128)S(1)}, f32[16,128]{1,0:T(8,128)S(1)}, u32[]{:S(2)}, u32[]{:S(2)}) collective-permute-start(f32[16,128]{1,0:T(8,128)S(1)} %get-tuple-element.88), channel_id=1, source_target_pairs={{0,4},{1,5},{2,6},{3,7},{4,0},{5,1},{6,2},{7,3},{8,12},{9,13},{10,... | collective-permute-start | bytes 24584 | tf_op jit(solution)/shard_map/ppermute | solution.py:455
  65.9 4.6 %collective-permute-start.23 = (f32[16,128]{1,0:T(8,128)S(1)}, f32[16,128]{1,0:T(8,128)S(1)}, u32[]{:S(2)}, u32[]{:S(2)}) collective-permute-start(f32[16,128]{1,0:T(8,128)S(1)} %add.26.one_ref), channel_id=1, source_target_pairs={{0,8},{1,9},{2,10},{3,11},{4,12},{5,13},{6,14},{7,15},{8,0},{9,1},... | collective-permute-start | bytes 24584 | tf_op jit(solution)/shard_map/ppermute | solution.py:455
  70.5 1.2 %collective-permute-start.24 = (f32[16,128]{1,0:T(8,128)S(1)}, f32[16,128]{1,0:T(8,128)S(1)}, u32[]{:S(2)}, u32[]{:S(2)}) collective-permute-start(f32[16,128]{1,0:T(8,128)S(1)} %add.38), channel_id=1, source_target_pairs={{0,1},{1,0},{2,3},{3,2},{4,5},{5,4},{6,7},{7,6},{8,9},{9,8},{10,11... | collective-permute-start | bytes 24584 | tf_op jit(solution)/shard_map/ppermute | solution.py:455
  71.6 3.7 %collective-permute-start.25 = (f32[16,128]{1,0:T(8,128)S(1)}, f32[16,128]{1,0:T(8,128)S(1)}, u32[]{:S(2)}, u32[]{:S(2)}) collective-permute-start(f32[16,128]{1,0:T(8,128)S(1)} %add.27), channel_id=1, source_target_pairs={{0,2},{1,3},{2,0},{3,1},{4,6},{5,7},{6,4},{7,5},{8,10},{9,11},{10,... | collective-permute-start | bytes 24584 | tf_op jit(solution)/shard_map/ppermute | solution.py:455
